TPU v7x, 32 devices: a whole 2x2x4 slice. The times are simulated.
32 devices in a mesh: members: 2 (over x), tile: 8 (over z, y), sub: 2 (over core).
Axes of the slice: x: 2, y: 2, z: 4, core: 2. Of those that a mesh axis runs over, the one named last changes fastest.
Arguments:
- tracers: float32 [40, 12, 32768], P('members', None, ('tile', 'sub')), parts along dimension 0, may hold values from -6 to 6
- courant: float32 [40, 32768], P('members', ('tile', 'sub')), parts along dimension 0, may hold values from 0.1 to 0.9
- air_surface: float32 [8, 32768], P('members', ('tile', 'sub')), parts along dimension 0, may hold values from -6 to 6
- block_weights: bfloat16 [4096, 128, 128], P(('tile', 'sub')), may hold values from 0 to 0.015625
- block_dest: int32 [4096, 1], replicated, may hold values from 0 to 15; in each aligned block of 256 rows (0 to 255, 256 to 511, ...) at most 32 rows name the same one
- block_row: int32 [4096], replicated, may hold values from 0 to 15
- block_patch: int32 [4096], P(('tile', 'sub')), may hold values from 0 to 15
- ocean_state: float32 [32, 32, 1024], P('members', 'sub', 'tile'), parts along dimension 0, may hold values from -6 to 6
- exchange_rate: float32 [32, 1024], P('sub', 'tile'), may hold values from 0.05 to 0.5
- sea_mask: int32 [32, 1024], P('sub', 'tile'), may hold values 0 or 1
Outputs:
- tracers_out: float32 [40, 12, 32768], P('members', None, ('tile', 'sub')), parts along dimension 0
- ocean_next: float32 [32, 32, 1024], P('members', 'sub', 'tile'), parts along dimension 0
- air_exchange: float32 [32, 32768], P('members', ('tile', 'sub')), parts along dimension 0
There are 2 independent parts, one for each index of `members`. A program takes and returns all parts, laid end to end along the dimension named above; an argument that names none is the same for every part. Nothing has to cross between parts.
Inputs may be any that keep to these rules, and one draw needn't show every extreme that they name: `block_dest`: in the 256 rows of one device no ocean device is named more than 32 times, a bound that some block reaches.
All inputs are finite; a program needn't handle non-finite values. No bound on the sum of `sea_mask` on one device may be relied on, other than what follows from the above.
Results may differ from a plain program's by a relative error of at most 0.0026.
Values may be sent and summed in bfloat16 or wider, within the bound.
No kernel may reach another device: no remote copies, remote signals or barrier semaphores. Data moves between devices by JAX's collectives and lax.ppermute only.
A program may use at most 128 MiB of HBM per device.

v0:
```python
import jax
import jax.numpy as jnp
from jax import lax
from jax.sharding import PartitionSpec as P

ASTEPS = 3


NU = 0.2
COUPLE = 0.5


def from_behind(array, axis, by):
    length = lax.axis_size(axis)
    return lax.ppermute(array, axis, [(i, (i + by) % length) for i in range(length)])


def with_halo(cells, sides, width, closed):
    for axis, dim in sides:
        count = lax.axis_size(axis)
        ends = count if closed else count - 1
        head = lax.slice_in_dim(cells, 0, width, axis=dim)
        tail = lax.slice_in_dim(cells, cells.shape[dim] - width, cells.shape[dim], axis=dim)
        cells = jnp.concatenate(
            [
                lax.ppermute(tail, axis, [(i, (i + 1) % count) for i in range(ends)]),
                cells,
                lax.ppermute(head, axis, [((i + 1) % count, i) for i in range(ends)]),
            ],
            axis=dim,
        )
    return cells


def swapped(array, axis, apart):
    return lax.ppermute(array, axis, [(i, i ^ 1 << apart) for i in range(lax.axis_size(axis))])


def ppm_step(padded, face_numbers, span_cells):
    edge_vals = (
        7.0 * (padded[..., 1 : span_cells + 3] + padded[..., 2 : span_cells + 4])
        - (padded[..., 0 : span_cells + 2] + padded[..., 3 : span_cells + 5])
    ) / 12.0
    left_edge = edge_vals[..., 0 : span_cells + 1]
    right_edge = edge_vals[..., 1 : span_cells + 2]
    centre = padded[..., 2 : span_cells + 3]
    number = face_numbers[:, None, :]
    curvature = 6.0 * (centre - 0.5 * (left_edge + right_edge))
    fluxes = number * (
        right_edge
        - 0.5 * number * (right_edge - left_edge - (1.0 - 2.0 * number / 3.0) * curvature)
    )
    return padded[..., 3 : span_cells + 3] - (fluxes[..., 1:] - fluxes[..., :-1])


def per_device(
    tracers,
    courant,
    air_surface,
    block_weights,
    block_dest,
    block_row,
    block_patch,
    ocean_state,
    exchange_rate,
    sea_mask,
):
    devices = lax.axis_size(("tile", "sub"))
    my_index = lax.axis_index(("tile", "sub"))
    span_cells = tracers.shape[2]
    block_count = block_weights.shape[0]
    patch_cells = block_weights.shape[1]
    patches_dev = span_cells // patch_cells
    fields = tracers.shape[1] + air_surface.shape[0]
    ocean_rows = ocean_state.shape[1]
    capacity = max(2, 2 * block_count // devices)
    slots = devices * capacity
    left_face = from_behind(courant[:, -1:], ("tile", "sub"), 1)
    face_numbers = jnp.concatenate([left_face, courant], axis=1)
    advected = tracers
    for substep in range(ASTEPS):
        padded = with_halo(advected, ((("tile", "sub"), 2),), 3, True)
        advected = ppm_step(padded, face_numbers, span_cells)
    all_dest = block_dest[:, 0].reshape(devices, block_count)
    all_rows = block_row.reshape(devices, block_count)
    positions = jnp.arange(block_count, dtype=jnp.int32)
    earlier_mask = positions[None, :, None] > positions[None, None, :]
    same_dest = all_dest[:, :, None] == all_dest[:, None, :]
    slot_rank = jnp.sum((earlier_mask & same_dest).astype(jnp.int32), axis=2)
    my_dest = lax.dynamic_index_in_dim(all_dest, my_index, 0, keepdims=False)
    my_rank = lax.dynamic_index_in_dim(slot_rank, my_index, 0, keepdims=False)
    my_slots = my_dest * capacity + my_rank
    send_table = (my_slots[:, None] == jnp.arange(slots, dtype=jnp.int32)[None, :]).astype(
        jnp.float32
    )
    send_half = send_table.astype(jnp.bfloat16)
    patch_table = (
        block_patch[:, None] == jnp.arange(patches_dev, dtype=jnp.int32)[None, :]
    ).astype(jnp.bfloat16)
    surface = jnp.concatenate([advected[0], air_surface], axis=0).astype(jnp.bfloat16)
    surface = surface.reshape(fields, patches_dev, patch_cells)
    block_inputs = jnp.einsum(
        "ba,fap->bfp", patch_table, surface, preferred_element_type=jnp.float32
    ).astype(jnp.bfloat16)
    pieces = jnp.einsum(
        "bfi,bij->bfj", block_inputs, block_weights, preferred_element_type=jnp.float32
    )
    outgoing = jnp.einsum("bs,bfj->sfj", send_table, pieces, precision=lax.Precision.HIGHEST)
    outgoing = outgoing.reshape(devices, capacity, fields, patch_cells)
    incoming = lax.all_to_all(
        outgoing.astype(jnp.bfloat16), ("tile", "sub"), split_axis=0, concat_axis=0, tiled=True
    ).astype(outgoing.dtype)
    incoming = incoming.reshape(slots, fields, patch_cells)
    mine_mask = (all_dest == my_index).astype(jnp.float32)
    rank_hot = (
        slot_rank[:, :, None] == jnp.arange(capacity, dtype=jnp.int32)[None, None, :]
    ).astype(jnp.float32)
    row_hot = (
        all_rows[:, :, None] == jnp.arange(ocean_rows, dtype=jnp.int32)[None, None, :]
    ).astype(jnp.float32)
    recv_table = jnp.einsum("pb,pbk,pbr->rpk", mine_mask, rank_hot, row_hot).reshape(
        ocean_rows, slots
    )
    remapped = jnp.einsum("rs,sfj->frj", recv_table, incoming, precision=lax.Precision.HIGHEST)
    east_west = with_halo(ocean_state, (("tile", 2),), 1, True)
    north_south = with_halo(ocean_state, (("sub", 1),), 1, False)
    fold_sign = jnp.where(jnp.arange(fields) >= fields - 2, -1.0, 1.0).astype(jnp.float32)
    mirrored = ocean_state[:, -1, ::-1]
    for bit_number in range(lax.axis_size("tile").bit_length() - 1):
        mirrored = swapped(mirrored, "tile", bit_number)
    top_row = jnp.where(
        lax.axis_index("sub") == lax.axis_size("sub") - 1,
        fold_sign[:, None] * mirrored,
        north_south[:, -1],
    )
    above_rows = jnp.concatenate([north_south[:, 2:-1], top_row[:, None]], axis=1)
    lateral = (
        east_west[:, :, :-2]
        + east_west[:, :, 2:]
        + north_south[:, :-2]
        + above_rows
        - 4.0 * ocean_state
    )
    wet_cells = sea_mask.astype(jnp.float32)
    ocean_next = ocean_state + wet_cells * (exchange_rate * (remapped - ocean_state) + NU * lateral)
    ocean_half = ocean_next.astype(jnp.bfloat16)
    going_back = jnp.einsum(
        "rs,frj->sfj",
        recv_table.astype(jnp.bfloat16),
        ocean_half,
        preferred_element_type=jnp.float32,
    ).astype(jnp.bfloat16)
    going_back = going_back.reshape(devices, capacity, fields, patch_cells)
    arriving = lax.all_to_all(going_back, ("tile", "sub"), split_axis=0, concat_axis=0, tiled=True)
    arriving = arriving.reshape(slots, fields, patch_cells)
    block_returns = jnp.einsum(
        "bs,sfj->bfj", send_half, arriving, preferred_element_type=jnp.float32
    ).astype(jnp.bfloat16)
    spread = jnp.einsum(
        "bfj,bij->bfi", block_returns, block_weights, preferred_element_type=jnp.float32
    )
    collected = jnp.einsum(
        "ba,bfi->fai", patch_table.astype(jnp.float32), spread, precision=lax.Precision.HIGHEST
    )
    air_exchange = collected.reshape(fields, span_cells)
    tracers_out = advected.at[0].add(COUPLE * air_exchange[: tracers.shape[1]])
    return (tracers_out, ocean_next, air_exchange)


def solution(mesh):
    placed = (
        P("members", None, ("tile", "sub")),
        P("members", ("tile", "sub")),
        P("members", ("tile", "sub")),
        P(("tile", "sub"), None, None),
        P(),
        P(),
        P(("tile", "sub")),
        P("members", "sub", "tile"),
        P("sub", "tile"),
        P("sub", "tile"),
    )
    return jax.shard_map(
        per_device,
        mesh=mesh,
        in_specs=placed,
        out_specs=(
            P("members", None, ("tile", "sub")),
            P("members", "sub", "tile"),
            P("members", ("tile", "sub")),
        ),
        check_vma=False,
    )
```

profile of v0, /device:TPU:0, one launch (start us, length us, event | category | flops | bytes accessed | tf_op | source)
XLA Modules:
  0.0 198.4 jit_solution(6458010220968394297)
XLA Ops:
  0.7 2.9 %copy.53 = f32[20,12,2048]{2,1,0:T(8,128)S(1)} copy(f32[20,12,2048]{2,0,1:T(8,128)} %param.12) | data formatting | bytes 3932160 | tf_op args[0]
  3.5 0.8 fusion.89
  4.3 0.5 collective-permute-start.1
  4.7 5.0 %collective-permute-start.2 = (f32[20,12,3]{2,1,0:T(8,128)}, f32[20,12,3]{2,1,0:T(8,128)}, u32[]{:S(2)}, u32[]{:S(2)}) collective-permute-start(f32[20,12,3]{2,1,0:T(8,128)} %get-tuple-element.28), channel_id=1, source_target_pairs={{1,0},{2,1},{3,2},{4,3},{5,4},{6,5},{7,6},{8,7},{9,8},{10,9},{11,1... | collective-permute-start | bytes 8648 | tf_op jit(solution)/shard_map/ppermute | solution.py:28
  9.7 0.8 slice.168
  10.6 0.5 broadcast.143
  11.1 0.7 reduce.5
  11.8 4.5 %collective-permute-done = f32[20,1]{1,0:T(8,128)S(1)} collective-permute-done((f32[20,1]{1,0:T(8,128)S(1)}, f32[20,1]{1,0:T(8,128)S(1)}, u32[]{:S(2)}, u32[]{:S(2)}) %collective-permute-start) | collective-permute-done | bytes 112 | tf_op jit(solution)/shard_map/ppermute | solution.py:15
  16.3 1.1 pad_maximum_fusion.6
  17.4 3.5 %concatenate.70 = f32[20,12,2054]{2,1,0:T(8,128)} concatenate(f32[20,12,3]{2,1,0:T(8,128)S(1)} %collective-permute-done.1, f32[20,12,2048]{2,1,0:T(8,128)S(1)} %copy.53, f32[20,12,3]{2,1,0:T(8,128)} %collective-permute-done.2), dimensions={2} | concatenate | bytes 3943680 | tf_op jit(solution)/shard_map/concatenate | solution.py:24
  20.9 3.8 %fusion.17 = f32[20,12,2050]{2,1,0:T(8,128)S(1)} fusion(f32[20,12,3]{2,1,0:T(8,128)S(1)} %collective-permute-done.1, f32[20,12,3]{2,1,0:T(8,128)} %collective-permute-done.2, f32[20,12,2048]{2,1,0:T(8,128)S(1)} %copy.53, f32[20,12,2054]{2,1,0:T(8,128)} %concatenate.70), kind=kLoop, calls=%fused_computation.24 | loop fusion | flops 3936000 | bytes 5907840 | tf_op jit(solution)/shard_map/div | solution.py:40
  24.7 1.9 fusion.38
  26.6 1.4 fusion.41
  28.1 0.8 fusion.88
  28.8 4.4 %collective-permute-start.4 = (f32[20,12,3]{2,1,0:T(8,128)}, f32[20,12,3]{2,1,0:T(8,128)}, u32[]{:S(2)}, u32[]{:S(2)}) collective-permute-start(f32[20,12,3]{2,1,0:T(8,128)} %get-tuple-element.26), channel_id=1, source_target_pairs={{1,0},{2,1},{3,2},{4,3},{5,4},{6,5},{7,6},{8,7},{9,8},{10,9},{11,1... | collective-permute-start | bytes 8648 | tf_op jit(solution)/shard_map/ppermute | solution.py:28
  33.3 1.3 convert_reduce_fusion
  34.6 1.9 collective-permute-done.3
  36.5 3.5 %concatenate.73 = f32[20,12,2054]{2,1,0:T(8,128)} concatenate(f32[20,12,3]{2,1,0:T(8,128)S(1)} %collective-permute-done.3, f32[20,12,2048]{2,1,0:T(8,128)S(1)} %fusion.41, f32[20,12,3]{2,1,0:T(8,128)} %collective-permute-done.4), dimensions={2} | concatenate | bytes 3943680 | tf_op jit(solution)/shard_map/concatenate | solution.py:24
  40.0 3.8 %fusion.10 = f32[20,12,2050]{2,1,0:T(8,128)S(1)} fusion(f32[20,12,3]{2,1,0:T(8,128)S(1)} %collective-permute-done.3, f32[20,12,3]{2,1,0:T(8,128)} %collective-permute-done.4, f32[20,12,2048]{2,1,0:T(8,128)S(1)} %fusion.41, f32[20,12,2054]{2,1,0:T(8,128)} %concatenate.73), kind=kLoop, calls=%fused_computation.17 | loop fusion | flops 3936000 | bytes 5907840 | tf_op jit(solution)/shard_map/div | solution.py:40
  43.7 1.9 fusion.32
  45.6 0.9 fusion.40
  46.5 1.5 copy-done
  48.1 0.1 fusion.87
  48.2 0.1 collective-permute-start.5
  48.2 4.8 %collective-permute-start.6 = (f32[20,12,3]{2,1,0:T(8,128)S(1)}, f32[20,12,3]{2,1,0:T(8,128)}, u32[]{:S(2)}, u32[]{:S(2)}) collective-permute-start(f32[20,12,3]{2,1,0:T(8,128)S(1)} %get-tuple-element.24), channel_id=1, source_target_pairs={{1,0},{2,1},{3,2},{4,3},{5,4},{6,5},{7,6},{8,7},{9,8},{10,9},{11,1... | collective-permute-start | bytes 8648 | tf_op jit(solution)/shard_map/ppermute | solution.py:28
  53.0 2.7 %collective-permute-done.5 = f32[20,12,3]{2,1,0:T(8,128)S(1)} collective-permute-done((f32[20,12,3]{2,1,0:T(8,128)S(1)}, f32[20,12,3]{2,1,0:T(8,128)S(1)}, u32[]{:S(2)}, u32[]{:S(2)}) %collective-permute-start.5) | collective-permute-done | bytes 2912 | tf_op jit(solution)/shard_map/ppermute | solution.py:26
  55.7 0.1 collective-permute-done.6
  55.8 4.6 %concatenate.76 = f32[20,12,2054]{2,1,0:T(8,128)} concatenate(f32[20,12,3]{2,1,0:T(8,128)S(1)} %collective-permute-done.5, f32[20,12,2048]{2,1,0:T(8,128)} %copy-done, f32[20,12,3]{2,1,0:T(8,128)} %collective-permute-done.6), dimensions={2} | concatenate | bytes 3943680 | tf_op jit(solution)/shard_map/concatenate | solution.py:24
  60.4 3.8 %fusion.3 = f32[20,12,2050]{2,1,0:T(8,128)S(1)} fusion(f32[20,12,3]{2,1,0:T(8,128)S(1)} %collective-permute-done.5, f32[20,12,3]{2,1,0:T(8,128)} %collective-permute-done.6, f32[20,12,2048]{2,1,0:T(8,128)S(1)} %copy-done.1, f32[20,12,2054]{2,1,0:T(8,128)} %concatenate.76), kind=kLoop, calls=%fused_computation.10 | loop fusion | flops 3936000 | bytes 5907840 | tf_op jit(solution)/shard_map/div | solution.py:40
  64.2 1.9 fusion.26
  66.1 0.0 slice-start.1
  66.1 0.9 fusion.39
  67.1 0.5 convolution_convert_fusion.2
  67.5 1.5 slice-done.1
  69.1 2.4 %fusion.56 = f32[256,16,128]{2,1,0:T(8,128)S(1)} fusion(bf16[256,128,128]{2,1,0:T(8,128)(2,1)S(1)} %bitcast.64, bf16[256,16,128]{2,0,1:T(8,128)(2,1)S(1)} %convolution_convert_fusion.2), kind=kOutput, calls=%fused_computation.74 | convolution fusion | flops 134217728 | bytes 11534336 | tf_op jit(solution)/shard_map/bfi,bij->bfj/dot_general | solution.py:105
  71.4 2.6 %fusion.46 = bf16[512,16,128]{2,0,1:T(8,128)(2,1)S(1)} fusion(f32[256,16,128]{2,1,0:T(8,128)S(1)} %fusion.56, s32[256]{0:T(256)S(1)} %bitcast.79), kind=kOutput, calls=%fused_computation.62 | convolution fusion | flops 3222405120 | bytes 4195328 | tf_op jit(solution)/shard_map/bs,bfj->sfj/dot_general | solution.py:108
  74.1 1.9 copy.58
  75.9 6.2 %all-to-all-start = ((bf16[16,32,16,128]{3,1,2,0:T(8,128)(2,1)}), bf16[16,32,16,128]{3,1,2,0:T(8,128)(2,1)S(1)}, u32[]{:S(2)}, u32[]{:S(2)}) async-start(bf16[16,32,16,128]{3,1,2,0:T(8,128)(2,1)} %copy.58), calls=%async_computation | async-start | bytes 4194304 | tf_op jit(solution)/shard_map/all_to_all | solution.py:110
  82.2 2.3 %collective-permute-start.9 = (f32[16,1,128]{2,0,1:T(8,128)S(1)}, f32[16,1,128]{2,0,1:T(8,128)S(1)}, u32[]{:S(2)}, u32[]{:S(2)}) collective-permute-start(f32[16,1,128]{2,0,1:T(8,128)S(1)} %bitcast.77), channel_id=1, source_target_pairs={{0,1},{2,3},{4,5},{6,7},{8,9},{10,11},{12,13},{14,15},{16,17},{18,... | collective-permute-start | bytes 24584 | tf_op jit(solution)/shard_map/ppermute | solution.py:26
  84.5 0.1 rev.3
  84.6 1.7 collective-permute-start.10
  86.3 1.3 collective-permute-start.13
  87.6 0.1 fusion.91
  87.7 0.4 collective-permute-start.7
  88.1 4.4 %collective-permute-start.8 = (f32[16,16,1]{2,1,0:T(8,128)S(1)}, f32[16,16,1]{2,1,0:T(8,128)S(1)}, u32[]{:S(2)}, u32[]{:S(2)}) collective-permute-start(f32[16,16,1]{2,1,0:T(8,128)S(1)} %get-tuple-element.36), channel_id=1, source_target_pairs={{2,0},{4,2},{6,4},{8,6},{10,8},{12,10},{14,12},{0,14},{3,1},{5,3},... | collective-permute-start | bytes 3080 | tf_op jit(solution)/shard_map/ppermute | solution.py:28
  92.5 3.2 %collective-permute-done.10 = f32[16,128]{1,0:T(8,128)S(1)} collective-permute-done((f32[16,128]{1,0:T(8,128)S(1)}, f32[16,128]{1,0:T(8,128)S(1)}, u32[]{:S(2)}, u32[]{:S(2)}) %collective-permute-start.10) | collective-permute-done | bytes 8224 | tf_op jit(solution)/shard_map/ppermute | solution.py:36
  95.6 0.2 collective-permute-start.11
  95.9 0.2 bitcast_convert_fusion
  96.1 24.0 %collective-permute-done.11 = f32[16,128]{1,0:T(8,128)S(1)} collective-permute-done((f32[16,128]{1,0:T(8,128)S(1)}, f32[16,128]{1,0:T(8,128)S(1)}, u32[]{:S(2)}, u32[]{:S(2)}) %collective-permute-start.11) | collective-permute-done | bytes 8224 | tf_op jit(solution)/shard_map/ppermute | solution.py:36
  120.1 4.4 %collective-permute-start.12 = (f32[16,128]{1,0:T(8,128)S(1)}, f32[16,128]{1,0:T(8,128)S(1)}, u32[]{:S(2)}, u32[]{:S(2)}) collective-permute-start(f32[16,128]{1,0:T(8,128)S(1)} %collective-permute-done.11), channel_id=1, source_target_pairs={{0,8},{2,10},{4,12},{6,14},{8,0},{10,2},{12,4},{14,6},{1,9},{3,11}... | collective-permute-start | bytes 24584 | tf_op jit(solution)/shard_map/ppermute | solution.py:36
  124.6 0.1 reshape.150
  124.7 9.7 %collective-permute-done.12 = f32[16,128]{1,0:T(8,128)S(1)} collective-permute-done((f32[16,128]{1,0:T(8,128)S(1)}, f32[16,128]{1,0:T(8,128)S(1)}, u32[]{:S(2)}, u32[]{:S(2)}) %collective-permute-start.12) | collective-permute-done | bytes 8224 | tf_op jit(solution)/shard_map/ppermute | solution.py:36
  134.4 0.1 bitcast_select_fusion
  134.5 1.0 fusion.53
  135.5 0.7 convolution_convert_fusion
  136.3 0.5 copy.62
  136.8 0.0 slice-start.3
  136.8 51.1 %all_to_all.10 = bf16[16,32,16,128]{3,1,2,0:T(8,128)(2,1)S(1)} all-to-all(bf16[16,32,16,128]{3,1,2,0:T(8,128)(2,1)S(1)} %copy.62), channel_id=1, replica_groups=mesh['members'=2,'tile'=8,'sub'=2] {'tile','sub'}, dimensions={0} | all-to-all | bytes 4194304 | tf_op jit(solution)/shard_map/all_to_all | solution.py:154
  187.9 0.5 copy.63
  188.5 0.7 convolution_convert_fusion.1
  189.3 4.5 %fusion.54 = f32[256,16,128]{2,1,0:T(8,128)S(1)} fusion(bf16[256,128,128]{2,1,0:T(8,128)(2,1)S(1)} %bitcast.66, bf16[256,16,128]{2,0,1:T(8,128)(2,1)S(1)} %convolution_convert_fusion.1), kind=kOutput, calls=%fused_computation.72 | convolution fusion | flops 134217728 | bytes 11534336 | tf_op jit(solution)/shard_map/bfj,bij->bfi/dot_general | solution.py:159
  193.7 1.3 fusion.42
  195.1 2.6 %copy.66 = f32[20,12,2048]{2,0,1:T(8,128)} copy(f32[20,12,2048]{2,1,0:T(8,128)S(1)} %add_dynamic-update-slice_fusion) | data formatting | bytes 3932160
  197.7 0.7 copy.88
  (60 shorter events, 0.3 us)
Async XLA Ops:
  0.6 9.9 %copy-start.7 = (f32[4,2048]{1,0:T(4,128)S(1)}, f32[4,2048]{1,0:T(4,128)}, u32[]{:S(2)}) copy-start(f32[4,2048]{1,0:T(4,128)} %param.14) | copy-start | bytes 98308
  0.6 10.4 %copy-start.8 = (s32[4096,1]{0,1:T(1,128)S(1)}, s32[4096,1]{0,1:T(1,128)}, u32[]{:S(2)}) copy-start(s32[4096,1]{0,1:T(1,128)} %param.16) | copy-start | bytes 49156
  4.3 13.1 %collective-permute-start.1 = (f32[20,12,3]{2,1,0:T(8,128)}, f32[20,12,3]{2,1,0:T(8,128)S(1)}, u32[]{:S(2)}, u32[]{:S(2)}) collective-permute-start(f32[20,12,3]{2,1,0:T(8,128)} %get-tuple-element.29), channel_id=1, source_target_pairs={{0,1},{1,2},{2,3},{3,4},{4,5},{5,6},{6,7},{7,8},{8,9},{9,10},{10,1... | collective-permute-start | bytes 8648 | tf_op jit(solution)/shard_map/ppermute | solution.py:26
  4.7 12.7 %collective-permute-start.2 = (f32[20,12,3]{2,1,0:T(8,128)}, f32[20,12,3]{2,1,0:T(8,128)}, u32[]{:S(2)}, u32[]{:S(2)}) collective-permute-start(f32[20,12,3]{2,1,0:T(8,128)} %get-tuple-element.28), channel_id=1, source_target_pairs={{1,0},{2,1},{3,2},{4,3},{5,4},{6,5},{7,6},{8,7},{9,8},{10,9},{11,1... | collective-permute-start | bytes 8648 | tf_op jit(solution)/shard_map/ppermute | solution.py:28
  10.5 5.8 %collective-permute-start = (f32[20,1]{1,0:T(8,128)S(1)}, f32[20,1]{1,0:T(8,128)S(1)}, u32[]{:S(2)}, u32[]{:S(2)}) collective-permute-start(f32[20,1]{1,0:T(8,128)S(1)} %slice.168), channel_id=1, source_target_pairs={{0,1},{1,2},{2,3},{3,4},{4,5},{5,6},{6,7},{7,8},{8,9},{9,10},{10,1... | collective-permute-start | bytes 248 | tf_op jit(solution)/shard_map/ppermute | solution.py:15
  24.7 1.9 copy-start.4
  28.8 7.7 %collective-permute-start.3 = (f32[20,12,3]{2,1,0:T(8,128)}, f32[20,12,3]{2,1,0:T(8,128)S(1)}, u32[]{:S(2)}, u32[]{:S(2)}) collective-permute-start(f32[20,12,3]{2,1,0:T(8,128)} %get-tuple-element.27), channel_id=1, source_target_pairs={{0,1},{1,2},{2,3},{3,4},{4,5},{5,6},{6,7},{7,8},{8,9},{9,10},{10,1... | collective-permute-start | bytes 8648 | tf_op jit(solution)/shard_map/ppermute | solution.py:26
  28.8 7.7 %collective-permute-start.4 = (f32[20,12,3]{2,1,0:T(8,128)}, f32[20,12,3]{2,1,0:T(8,128)}, u32[]{:S(2)}, u32[]{:S(2)}) collective-permute-start(f32[20,12,3]{2,1,0:T(8,128)} %get-tuple-element.26), channel_id=1, source_target_pairs={{1,0},{2,1},{3,2},{4,3},{5,4},{6,5},{7,6},{8,7},{9,8},{10,9},{11,1... | collective-permute-start | bytes 8648 | tf_op jit(solution)/shard_map/ppermute | solution.py:28
  46.5 1.5 copy-start
  48.2 7.6 %collective-permute-start.5 = (f32[20,12,3]{2,1,0:T(8,128)S(1)}, f32[20,12,3]{2,1,0:T(8,128)S(1)}, u32[]{:S(2)}, u32[]{:S(2)}) collective-permute-start(f32[20,12,3]{2,1,0:T(8,128)S(1)} %get-tuple-element.25), channel_id=1, source_target_pairs={{0,1},{1,2},{2,3},{3,4},{4,5},{5,6},{6,7},{7,8},{8,9},{9,10},{10,1... | collective-permute-start | bytes 8648 | tf_op jit(solution)/shard_map/ppermute | solution.py:26
  48.2 7.6 %collective-permute-start.6 = (f32[20,12,3]{2,1,0:T(8,128)S(1)}, f32[20,12,3]{2,1,0:T(8,128)}, u32[]{:S(2)}, u32[]{:S(2)}) collective-permute-start(f32[20,12,3]{2,1,0:T(8,128)S(1)} %get-tuple-element.24), channel_id=1, source_target_pairs={{1,0},{2,1},{3,2},{4,3},{5,4},{6,5},{7,6},{8,7},{9,8},{10,9},{11,1... | collective-permute-start | bytes 8648 | tf_op jit(solution)/shard_map/ppermute | solution.py:28
  53.0 7.4 %copy-start.1 = (f32[20,12,2048]{2,1,0:T(8,128)S(1)}, f32[20,12,2048]{2,1,0:T(8,128)}, u32[]{:S(2)}) copy-start(f32[20,12,2048]{2,1,0:T(8,128)} %copy-done) | copy-start | bytes 5898244
  64.2 3.4 %slice-start = ((s8[8388608]{0:T(1024)(128)(4,1)}), s8[4194304]{0:T(1024)(128)(4,1)S(1)}, s32[]{:S(2)}) async-start(s8[8388608]{0:T(1024)(128)(4,1)} %bitcast.63), calls=%async_computation.2 | async-start | bytes 8388608
  66.1 1.0 copy-start.12
  66.1 3.0 %slice-start.1 = ((s8[8388608]{0:T(1024)(128)(4,1)}), s8[4194304]{0:T(1024)(128)(4,1)S(1)}, s32[]{:S(2)}) async-start(s8[8388608]{0:T(1024)(128)(4,1)} %bitcast.63), calls=%async_computation.3 | async-start | bytes 8388608
  67.0 4.4 %copy-start.2 = (f32[20,12,2048]{2,1,0:T(8,128)}, f32[20,12,2048]{2,1,0:T(8,128)S(1)}, u32[]{:S(2)}) copy-start(f32[20,12,2048]{2,1,0:T(8,128)S(1)} %fusion.39) | copy-start | bytes 5898244
  75.9 6.3 %copy-start.5 = (f32[16,16,128]{2,1,0:T(8,128)S(1)}, f32[16,16,128]{2,1,0:T(8,128)}, u32[]{:S(2)}) copy-start(f32[16,16,128]{2,1,0:T(8,128)} %param.19) | copy-start | bytes 393220
  75.9 16.5 %copy-start.9 = (s32[4096]{0:T(1024)S(1)}, s32[4096]{0:T(1024)}, u32[]{:S(2)}) copy-start(s32[4096]{0:T(1024)} %param.17) | copy-start | bytes 49156
  75.9 48.6 %copy-start.11 = (s32[16,128]{1,0:T(8,128)S(1)}, s32[16,128]{1,0:T(8,128)}, u32[]{:S(2)}) copy-start(s32[16,128]{1,0:T(8,128)} %param.21) | copy-start | bytes 24580
  75.9 58.6 %copy-start.10 = (f32[16,128]{1,0:T(8,128)S(1)}, f32[16,128]{1,0:T(8,128)}, u32[]{:S(2)}) copy-start(f32[16,128]{1,0:T(8,128)} %param.20) | copy-start | bytes 24580
  75.9 58.6 %all-to-all-start = ((bf16[16,32,16,128]{3,1,2,0:T(8,128)(2,1)}), bf16[16,32,16,128]{3,1,2,0:T(8,128)(2,1)S(1)}, u32[]{:S(2)}, u32[]{:S(2)}) async-start(bf16[16,32,16,128]{3,1,2,0:T(8,128)(2,1)} %copy.58), calls=%async_computation | async-start | bytes 4194304 | tf_op jit(solution)/shard_map/all_to_all | solution.py:110
  82.2 52.3 %collective-permute-start.9 = (f32[16,1,128]{2,0,1:T(8,128)S(1)}, f32[16,1,128]{2,0,1:T(8,128)S(1)}, u32[]{:S(2)}, u32[]{:S(2)}) collective-permute-start(f32[16,1,128]{2,0,1:T(8,128)S(1)} %bitcast.77), channel_id=1, source_target_pairs={{0,1},{2,3},{4,5},{6,7},{8,9},{10,11},{12,13},{14,15},{16,17},{18,... | collective-permute-start | bytes 24584 | tf_op jit(solution)/shard_map/ppermute | solution.py:26
  84.6 11.0 %collective-permute-start.10 = (f32[16,128]{1,0:T(8,128)S(1)}, f32[16,128]{1,0:T(8,128)S(1)}, u32[]{:S(2)}, u32[]{:S(2)}) collective-permute-start(f32[16,128]{1,0:T(8,128)S(1)} %bitcast.82), channel_id=1, source_target_pairs={{0,2},{2,0},{4,6},{6,4},{8,10},{10,8},{12,14},{14,12},{1,3},{3,1},... | collective-permute-start | bytes 24584 | tf_op jit(solution)/shard_map/ppermute | solution.py:36
  86.3 38.4 %collective-permute-start.13 = (f32[16,1,128]{2,0,1:T(8,128)S(1)}, f32[16,1,128]{2,0,1:T(8,128)S(1)}, u32[]{:S(2)}, u32[]{:S(2)}) collective-permute-start(f32[16,1,128]{2,0,1:T(8,128)S(1)} %bitcast.83), channel_id=1, source_target_pairs={{1,0},{3,2},{5,4},{7,6},{9,8},{11,10},{13,12},{15,14},{17,16},{19,... | collective-permute-start | bytes 24584 | tf_op jit(solution)/shard_map/ppermute | solution.py:28
  87.7 46.8 %collective-permute-start.7 = (f32[16,16,1]{2,1,0:T(8,128)S(1)}, f32[16,16,1]{2,1,0:T(8,128)S(1)}, u32[]{:S(2)}, u32[]{:S(2)}) collective-permute-start(f32[16,16,1]{2,1,0:T(8,128)S(1)} %get-tuple-element.35), channel_id=1, source_target_pairs={{0,2},{2,4},{4,6},{6,8},{8,10},{10,12},{12,14},{14,0},{1,3},{3,5},... | collective-permute-start | bytes 3080 | tf_op jit(solution)/shard_map/ppermute | solution.py:26
  88.1 46.4 %collective-permute-start.8 = (f32[16,16,1]{2,1,0:T(8,128)S(1)}, f32[16,16,1]{2,1,0:T(8,128)S(1)}, u32[]{:S(2)}, u32[]{:S(2)}) collective-permute-start(f32[16,16,1]{2,1,0:T(8,128)S(1)} %get-tuple-element.36), channel_id=1, source_target_pairs={{2,0},{4,2},{6,4},{8,6},{10,8},{12,10},{14,12},{0,14},{3,1},{5,3},... | collective-permute-start | bytes 3080 | tf_op jit(solution)/shard_map/ppermute | solution.py:28
  95.6 24.5 %collective-permute-start.11 = (f32[16,128]{1,0:T(8,128)S(1)}, f32[16,128]{1,0:T(8,128)S(1)}, u32[]{:S(2)}, u32[]{:S(2)}) collective-permute-start(f32[16,128]{1,0:T(8,128)S(1)} %collective-permute-done.10), channel_id=1, source_target_pairs={{0,4},{2,6},{4,0},{6,2},{8,12},{10,14},{12,8},{14,10},{1,5},{3,7},... | collective-permute-start | bytes 24584 | tf_op jit(solution)/shard_map/ppermute | solution.py:36
  120.1 14.3 %collective-permute-start.12 = (f32[16,128]{1,0:T(8,128)S(1)}, f32[16,128]{1,0:T(8,128)S(1)}, u32[]{:S(2)}, u32[]{:S(2)}) collective-permute-start(f32[16,128]{1,0:T(8,128)S(1)} %collective-permute-done.11), channel_id=1, source_target_pairs={{0,8},{2,10},{4,12},{6,14},{8,0},{10,2},{12,4},{14,6},{1,9},{3,11}... | collective-permute-start | bytes 24584 | tf_op jit(solution)/shard_map/ppermute | solution.py:36
  135.5 1.3 copy-start.6
  136.3 53.0 %slice-start.2 = ((s8[8388608]{0:T(1024)(128)(4,1)}), s8[4194304]{0:T(1024)(128)(4,1)S(1)}, s32[]{:S(2)}) async-start(s8[8388608]{0:T(1024)(128)(4,1)} %bitcast.65), calls=%async_computation.4 | async-start | bytes 8388608
  136.8 52.4 %slice-start.3 = ((s8[8388608]{0:T(1024)(128)(4,1)}), s8[4194304]{0:T(1024)(128)(4,1)S(1)}, s32[]{:S(2)}) async-start(s8[8388608]{0:T(1024)(128)(4,1)} %bitcast.65), calls=%async_computation.5 | async-start | bytes 8388608
  189.3 5.9 %copy-start.3 = (f32[20,12,2048]{2,1,0:T(8,128)S(1)}, f32[20,12,2048]{2,1,0:T(8,128)}, u32[]{:S(2)}) copy-start(f32[20,12,2048]{2,1,0:T(8,128)} %copy-done.2) | copy-start | bytes 5898244
where the time goes:
time: 199 us; the launch traced here: 198 us
  blocking collectives  51.1 us (26%)
  waiting for transfers between devices  46.2 us (23%)
  starting transfers between devices  35.6 us (18%)
  local copies, waits for them, and re-layouts  27 us (14%)
  other arithmetic  23.4 us (12%)
  matrix products  13.9 us (7%)
    all_to_all x1, blocking collectives, per_device(): lax.all_to_all(going_back, ('tile', 'sub'), split_axis=0, concat_axis=0,...  51.1 us
    ppermute x3, waiting for transfers between devices, swapped(): lax.ppermute(array, axis, [(i, i ^ 1 << apart) for i in range(lax.axis_si...  36.9 us
    ppermute x5, starting transfers between devices, with_halo(): lax.ppermute(head, axis, [((i + 1) % count, i) for i in range(ends)])  19.8 us
    concatenate x3, local copies, waits for them, and re-layouts, with_halo(): jnp.concatenate([lax.ppermute(tail, axis, [(i, (i + 1) % count) for i in...  11.5 us
    div x3, other arithmetic, ppm_step(): (7.0 * (padded[..., 1:span_cells + 3] + padded[..., 2:span_cells + 4]) -...  11.3 us
    unnamed x40, local copies, waits for them, and re-layouts  9.74 us
    ppermute x3, starting transfers between devices, swapped(): lax.ppermute(array, axis, [(i, i ^ 1 << apart) for i in range(lax.axis_si...  6.32 us
    all_to_all x1, starting transfers between devices, per_device(): lax.all_to_all(outgoing.astype(jnp.bfloat16), ('tile', 'sub'), split_axis...  6.24 us
  transfers between devices with their start and end apart: 15, of which 7 were waited for; matrix products, arithmetic and copies ran while one was open for 3% of the time, Pallas kernels for 0%

commit v1 on v0

v1 whole, which is shorter than its diff:
```python
import functools

import jax
import jax.numpy as jnp
from jax import lax
from jax.experimental import pallas as pl
from jax.experimental.pallas import tpu as pltpu
from jax.sharding import PartitionSpec as P

ASTEPS = 3
NU = 0.2
COUPLE = 0.5
LANES = 128
EDGE = 16
GROUPS = LANES // EDGE
UNROLL = 16
BIG = 48 * 1024 * 1024

VMEM = pl.BlockSpec(memory_space=pltpu.VMEM)
SMEM = pl.BlockSpec(memory_space=pltpu.SMEM)
ANY = pl.BlockSpec(memory_space=pl.ANY)
f32 = jnp.float32
bf16 = jnp.bfloat16


def params(limit=BIG):
    return pltpu.CompilerParams(vmem_limit_bytes=limit)


def lane_roll(x, shift):
    length = x.shape[-1]
    shift = shift % length
    return x if shift == 0 else pltpu.roll(x, shift, x.ndim - 1)


def coefficients(c):
    d = 1.0 - c
    return c * d * d * (1.0 / 12.0), c * c * d * (1.0 / 12.0), c * c * (3.0 - 2.0 * c)


def advect(q, right, left, own):
    for _ in range(ASTEPS):
        pair = q + lane_roll(q, -1)
        edge = 8.0 * pair - (lane_roll(pair, 1) + lane_roll(pair, -1))
        flux = right * edge - left * lane_roll(edge, 1) + own * q
        q = q - (flux - lane_roll(flux, 1))
    return q


def pack_kernel(tracers, levels, parity_ref, left_t, right_t, left_c, right_c, a_ref, b_ref):
    parity = parity_ref[0]
    lane = lax.broadcasted_iota(jnp.int32, (levels, LANES), 1)
    pad = pl.cdiv(levels, 8) * 8
    for out, from_left in ((a_ref, parity == 1), (b_ref, parity == 0)):
        for part in range(pl.cdiv(tracers + 1, GROUPS)):
            total = jnp.zeros((levels, LANES), f32)
            for group in range(GROUPS):
                item = part * GROUPS + group
                if item > tracers:
                    continue
                low = left_t[item] if item < tracers else left_c[...]
                high = right_t[item] if item < tracers else right_c[...]
                moved = jnp.where(
                    from_left,
                    lane_roll(low, EDGE * group),
                    lane_roll(high, EDGE * (group + 1)),
                )
                total = jnp.where(lane // EDGE == group, moved, total)
            out[part * pad : part * pad + levels, :] = total
        top = pl.cdiv(tracers + 1, GROUPS) * pad
        for item in range(tracers):
            out[top + item : top + item + 1, :] = jnp.where(
                from_left, left_t[item, 0:1, :], right_t[item, 0:1, :]
            )
        out[top + tracers : top + tracers + 1, :] = jnp.where(
            from_left, left_c[0:1, :], right_c[0:1, :]
        )


def pack(tracers_t, courant, parity):
    tracers, levels, span = tracers_t.shape
    last = span // LANES - 1
    pad = pl.cdiv(levels, 8) * 8
    rows = pl.cdiv(tracers + 1, GROUPS) * pad + pl.cdiv(tracers + 1, 8) * 8
    message = jax.ShapeDtypeStruct((rows, LANES), f32)
    return pl.pallas_call(
        functools.partial(pack_kernel, tracers, levels),
        grid=(1,),
        out_shape=(message, message),
        in_specs=[
            SMEM,
            pl.BlockSpec((tracers, levels, LANES), lambda i: (0, 0, 0)),
            pl.BlockSpec((tracers, levels, LANES), lambda i: (0, 0, last)),
            pl.BlockSpec((levels, LANES), lambda i: (0, 0)),
            pl.BlockSpec((levels, LANES), lambda i: (0, last)),
        ],
        out_specs=(
            pl.BlockSpec((rows, LANES), lambda i: (0, 0)),
            pl.BlockSpec((rows, LANES), lambda i: (0, 0)),
        ),
        compiler_params=params(16 * 1024 * 1024),
        name="pack_edges",
    )(parity, tracers_t, tracers_t, courant, courant)


def forward_kernel(
    dims,
    parity_ref,
    slot_ref,
    patch_ref,
    level0,
    courant0,
    air,
    msg_a,
    msg_b,
    weights_hbm,
    send_ref,
    keep_ref,
    weights,
    surface,
    total,
    sems,
):
    tracers, span, top, pieces_n, per_piece = dims
    copies = [
        pltpu.make_async_copy(
            weights_hbm.at[pl.ds(i * per_piece, per_piece)],
            weights.at[pl.ds(i * per_piece, per_piece)],
            sems.at[i],
        )
        for i in range(pieces_n)
    ]
    for copy in copies:
        copy.start()
    even = parity_ref[0] == 0
    a, b = msg_a[top : top + tracers + 1, :], msg_b[top : top + tracers + 1, :]
    left, right = jnp.where(even, b, a), jnp.where(even, a, b)
    q = jnp.concatenate([left[:tracers], level0[...], right[:tracers]], axis=1)
    c = jnp.concatenate([left[tracers:], courant0[0:1, :], right[tracers:]], axis=1)
    advected = advect(q, *coefficients(c))[:, LANES : LANES + span]
    fields = jnp.concatenate([advected, air[...]], axis=0).astype(bf16)
    for p in range(span // LANES):
        surface[p] = fields[:, p * LANES : (p + 1) * LANES]
    total[...] = jnp.zeros_like(total)

    for i in range(pieces_n):
        copies[i].wait()

        def step(g, carry, i=i):
            base = i * per_piece + g * UNROLL
            products = []
            for u in range(UNROLL):
                products.append(
                    jnp.dot(
                        surface[patch_ref[base + u]],
                        weights[base + u],
                        preferred_element_type=f32,
                    )
                )
            for u in range(UNROLL):
                total[slot_ref[base + u]] += products[u]
            return carry

        lax.fori_loop(0, per_piece // UNROLL, step, 0)
    half = total.shape[0] // 2
    keep_ref[...] = total[:half]
    send_ref[...] = total[half:].astype(bf16)


def forward(parity, slot, patch, level0, courant, air, msg_a, msg_b, weights, rows):
    tracers, span = level0.shape
    levels = courant.shape[0]
    blocks = weights.shape[0]
    fields = tracers + air.shape[0]
    pieces_n = 8
    pad = pl.cdiv(levels, 8) * 8
    top = pl.cdiv(tracers + 1, GROUPS) * pad
    dims = (tracers, span, top, pieces_n, blocks // pieces_n)
    return pl.pallas_call(
        functools.partial(forward_kernel, dims),
        out_shape=(
            jax.ShapeDtypeStruct((rows // 2, fields, LANES), bf16),
            jax.ShapeDtypeStruct((rows // 2, fields, LANES), f32),
        ),
        in_specs=[SMEM, SMEM, SMEM, VMEM, VMEM, VMEM, VMEM, VMEM, ANY],
        out_specs=(VMEM, VMEM),
        scratch_shapes=[
            pltpu.VMEM(weights.shape, bf16),
            pltpu.VMEM((span // LANES, fields, LANES), bf16),
            pltpu.VMEM((rows, fields, LANES), f32),
            pltpu.SemaphoreType.DMA((pieces_n,)),
        ],
        compiler_params=params(),
        name="blocks_to_rows",
    )(parity, slot, patch, level0, courant, air, msg_a, msg_b, weights)


def merge_kernel(chunk, keep, got, own_ref, *outs):
    own_ref[...] = keep[:chunk] + got[:chunk].astype(f32)
    for d, out in enumerate(outs):
        part = slice((d + 1) * chunk, (d + 2) * chunk)
        out[...] = (keep[part] + got[part].astype(f32)).astype(bf16)


def merge(keep, got, chunk):
    rows, fields, lanes = keep.shape
    count = rows // chunk
    return pl.pallas_call(
        functools.partial(merge_kernel, chunk),
        out_shape=(jax.ShapeDtypeStruct((chunk, fields, lanes), f32),)
        + (jax.ShapeDtypeStruct((chunk, fields, lanes), bf16),) * (count - 1),
        in_specs=[VMEM, VMEM],
        out_specs=(VMEM,) * count,
        compiler_params=params(),
        name="merge_cores",
    )(keep, got)


def ocean_kernel(
    count, state, south, north, east_west, rate, wet, own, *rest
):
    got, (next_ref, half_ref) = rest[:count], rest[count:]
    rows, fields, lanes = state.shape
    lane = lax.broadcasted_iota(jnp.int32, (fields, lanes), 1)
    from_west, from_east = east_west[0], east_west[1]
    for r in range(rows):
        here = state[r]
        west = jnp.where(lane == 0, lane_roll(from_west, -r), lane_roll(here, 1))
        east = jnp.where(
            lane == lanes - 1, lane_roll(from_east, lanes - 1 - rows - r), lane_roll(here, -1)
        )
        below = state[r - 1] if r else south[...]
        above = state[r + 1] if r < rows - 1 else north[...]
        lateral = west + east + below + above - 4.0 * here
        remapped = own[r]
        for chunk in got:
            remapped = remapped + chunk[r].astype(f32)
        new = here + wet[r : r + 1, :].astype(f32) * (
            rate[r : r + 1, :] * (remapped - here) + NU * lateral
        )
        next_ref[r] = new
        half_ref[r] = new.astype(bf16)


def ocean(state, south, north, east_west, rate, wet, own, got):
    return pl.pallas_call(
        functools.partial(ocean_kernel, len(got)),
        out_shape=(
            jax.ShapeDtypeStruct(state.shape, f32),
            jax.ShapeDtypeStruct(state.shape, bf16),
        ),
        in_specs=[VMEM] * (7 + len(got)),
        out_specs=(VMEM, VMEM),
        compiler_params=params(),
        name="ocean_update",
    )(state, south, north, east_west, rate, wet, own, *got)


def edges_kernel(state, out_ref):
    rows, fields, lanes = state.shape
    lane = lax.broadcasted_iota(jnp.int32, (fields, lanes), 1)
    total = jnp.zeros((fields, lanes), f32)
    for r in range(rows):
        total = jnp.where(lane == r, lane_roll(state[r], r + 1), total)
        total = jnp.where(lane == rows + r, lane_roll(state[r], rows + r), total)
    out_ref[...] = total


def ocean_edges(state):
    rows, fields, lanes = state.shape
    return pl.pallas_call(
        edges_kernel,
        out_shape=jax.ShapeDtypeStruct((fields, lanes), f32),
        in_specs=[VMEM],
        out_specs=VMEM,
        compiler_params=params(16 * 1024 * 1024),
        name="ocean_edges",
    )(state)


def advect_kernel(tracers, levels, parity_ref, q_ref, c_ref, msg_a, msg_b, out_ref, right, left, own):
    item = pl.program_id(0)
    even = parity_ref[0] == 0
    span = q_ref.shape[2]
    pad = pl.cdiv(levels, 8) * 8

    def sides(part, group):
        start = pl.multiple_of(part * pad, 8)
        a, b = msg_a[pl.ds(start, levels), :], msg_b[pl.ds(start, levels), :]
        low, high = jnp.where(even, b, a), jnp.where(even, a, b)
        shift = EDGE * group
        return (
            pltpu.roll(low, (2 * LANES - EDGE - shift) % LANES, 1),
            pltpu.roll(high, (LANES - shift) % LANES, 1),
        )

    @pl.when(item == 0)
    def _():
        low, high = sides(tracers // GROUPS, tracers % GROUPS)
        c = jnp.concatenate([low, c_ref[...], high], axis=1)
        right[...], left[...], own[...] = coefficients(c)

    low, high = sides(item // GROUPS, item % GROUPS)
    q = jnp.concatenate([low, q_ref[0], high], axis=1)
    out_ref[0] = advect(q, right[...], left[...], own[...])[:, LANES : LANES + span]


def advect_all(parity, tracers_t, courant, msg_a, msg_b):
    tracers, levels, span = tracers_t.shape
    wide = span + 2 * LANES
    whole = lambda shape: pl.BlockSpec(shape, lambda i: (0,) * len(shape))
    return pl.pallas_call(
        functools.partial(advect_kernel, tracers, levels),
        grid=(tracers,),
        out_shape=jax.ShapeDtypeStruct(tracers_t.shape, f32),
        in_specs=[
            SMEM,
            pl.BlockSpec((1, levels, span), lambda i: (i, 0, 0)),
            whole(courant.shape),
            whole(msg_a.shape),
            whole(msg_b.shape),
        ],
        out_specs=pl.BlockSpec((1, levels, span), lambda i: (i, 0, 0)),
        scratch_shapes=[pltpu.VMEM((levels, wide), f32)] * 3,
        compiler_params=params(16 * 1024 * 1024),
        cost_estimate=pl.CostEstimate(
            flops=60 * tracers * levels * span,
            bytes_accessed=8 * tracers * levels * span,
            transcendentals=0,
        ),
        name="advect_levels",
    )(parity, tracers_t, courant, msg_a, msg_b)


def backward_kernel(
    dims,
    slot_ref,
    patch_ref,
    mine,
    other,
    weights_hbm,
    advected_hbm,
    air_ref,
    out_hbm,
    weights,
    rows,
    total,
    bottom,
    sems,
    bottom_sem,
):
    tracers, span, pieces_n, per_piece = dims
    copies = [
        pltpu.make_async_copy(
            weights_hbm.at[pl.ds(i * per_piece, per_piece)],
            weights.at[pl.ds(i * per_piece, per_piece)],
            sems.at[i],
        )
        for i in range(pieces_n)
    ]
    for copy in copies:
        copy.start()
    fetch = pltpu.make_async_copy(advected_hbm.at[:, pl.ds(0, 8), :], bottom, bottom_sem)
    fetch.start()
    half = mine.shape[0]
    rows[:half] = mine[...]
    rows[half:] = other[...]
    total[...] = jnp.zeros_like(total)

    for i in range(pieces_n):
        copies[i].wait()

        def step(g, carry, i=i):
            base = i * per_piece + g * UNROLL
            products = []
            for u in range(UNROLL):
                products.append(
                    lax.dot_general(
                        rows[slot_ref[base + u]],
                        weights[base + u],
                        (((1,), (1,)), ((), ())),
                        preferred_element_type=f32,
                    )
                )
            for u in range(UNROLL):
                total[patch_ref[base + u]] += products[u]
            return carry

        lax.fori_loop(0, per_piece // UNROLL, step, 0)
    fetch.wait()
    for p in range(span // LANES):
        part = slice(p * LANES, (p + 1) * LANES)
        exchange = total[p]
        air_ref[:, part] = exchange
        bottom[:, 0, part] += COUPLE * exchange[:tracers]
    store = pltpu.make_async_copy(bottom, out_hbm.at[:, pl.ds(0, 8), :], bottom_sem)
    store.start()
    store.wait()


def backward(slot, patch, mine, other, weights, advected):
    tracers, levels, span = advected.shape
    blocks = weights.shape[0]
    half, fields, lanes = mine.shape
    pieces_n = 8
    dims = (tracers, span, pieces_n, blocks // pieces_n)
    return pl.pallas_call(
        functools.partial(backward_kernel, dims),
        out_shape=(
            jax.ShapeDtypeStruct((fields, span), f32),
            jax.ShapeDtypeStruct(advected.shape, f32),
        ),
        in_specs=[SMEM, SMEM, VMEM, VMEM, ANY, ANY],
        out_specs=(VMEM, ANY),
        input_output_aliases={5: 1},
        scratch_shapes=[
            pltpu.VMEM(weights.shape, bf16),
            pltpu.VMEM((2 * half, fields, lanes), bf16),
            pltpu.VMEM((span // lanes, fields, lanes), f32),
            pltpu.VMEM((tracers, 8, span), f32),
            pltpu.SemaphoreType.DMA((pieces_n,)),
            pltpu.SemaphoreType.DMA,
        ],
        compiler_params=params(),
        name="rows_to_columns",
    )(slot, patch, mine, other, weights, advected)


def per_device(
    tracers,
    courant,
    air_surface,
    block_weights,
    block_dest,
    block_row,
    block_patch,
    ocean_state,
    exchange_rate,
    sea_mask,
):
    tiles, subs = lax.axis_size("tile"), lax.axis_size("sub")
    devices = tiles * subs
    my_tile, my_sub = lax.axis_index("tile"), lax.axis_index("sub")
    my_index = my_tile * subs + my_sub
    blocks = block_weights.shape[0]
    fields, ocean_rows, lanes = ocean_state.shape
    flat = ("tile", "sub")
    parity = (my_index % 2).astype(jnp.int32).reshape(1)

    tracers_t = jnp.transpose(tracers, (1, 0, 2))
    pack_a, pack_b = pack(tracers_t, courant, parity)
    msg_a = lax.ppermute(pack_a, flat, [(i, i ^ 1) for i in range(devices)])
    msg_b = lax.ppermute(
        pack_b, flat, [(i, (i + 1 if i % 2 else i - 1) % devices) for i in range(devices)]
    )

    start = my_index * blocks
    dest = lax.dynamic_slice(block_dest.reshape(-1), (start,), (blocks,))
    row = lax.dynamic_slice(block_row, (start,), (blocks,))
    chunk_of = ((dest // subs) ^ my_tile) + tiles * ((dest % subs + subs - my_sub) % subs)
    slot = chunk_of * ocean_rows + row

    keep_send = forward(
        parity, slot, block_patch, tracers[0], courant, air_surface, msg_a, msg_b,
        block_weights, devices * ocean_rows,
    )
    send, keep = keep_send
    swap = [(0, 1), (1, 0)]
    own, *partial = merge(keep, lax.ppermute(send, "sub", swap), ocean_rows)
    across = lambda x, d: lax.ppermute(x, "tile", [(i, i ^ d) for i in range(tiles)])
    got = [across(x, d) for d, x in reversed(list(enumerate(partial, 1)))]

    advected = advect_all(parity, tracers_t, courant, msg_a, msg_b)

    state = jnp.transpose(ocean_state, (1, 0, 2))
    edges = ocean_edges(state)
    east_west = jnp.stack(
        [
            lax.ppermute(edges, "tile", [(i, (i + 1) % tiles) for i in range(tiles)]),
            lax.ppermute(edges, "tile", [((i + 1) % tiles, i) for i in range(tiles)]),
        ]
    )
    sign = jnp.where(jnp.arange(fields) >= fields - 2, -1.0, 1.0).astype(f32)[:, None]
    fold = lax.ppermute(
        sign * state[-1][:, ::-1], "tile", [(i, tiles - 1 - i) for i in range(tiles)]
    )
    is_top = my_sub == subs - 1
    beside = lax.ppermute(jnp.where(is_top, state[0], state[-1]), "sub", swap)
    south = jnp.where(my_sub == 0, 0.0, beside)
    north = jnp.where(is_top, fold, beside)

    next_t, half = ocean(
        state, south, north, east_west, exchange_rate, sea_mask, own, got
    )
    order = list(range(tiles - 1, 0, -1))
    arrived = {d: across(half, d) for d in order}
    mine = jnp.concatenate([half] + [arrived[d] for d in range(1, tiles)], axis=0)
    other = lax.ppermute(mine, "sub", swap)
    air_exchange, out_t = backward(slot, block_patch, mine, other, block_weights, advected)
    return (
        jnp.transpose(out_t, (1, 0, 2)),
        jnp.transpose(next_t, (1, 0, 2)),
        air_exchange,
    )


def solution(mesh):
    placed = (
        P("members", None, ("tile", "sub")),
        P("members", ("tile", "sub")),
        P("members", ("tile", "sub")),
        P(("tile", "sub"), None, None),
        P(),
        P(),
        P(("tile", "sub")),
        P("members", "sub", "tile"),
        P("sub", "tile"),
        P("sub", "tile"),
    )
    return jax.shard_map(
        per_device,
        mesh=mesh,
        in_specs=placed,
        out_specs=(
            P("members", None, ("tile", "sub")),
            P("members", "sub", "tile"),
            P("members", ("tile", "sub")),
        ),
        check_vma=False,
    )
```

time: 199 us -> 93 us (0.47)
  blocking collectives: 51.1 us -> 0 us
  Pallas kernels: 0 us -> 34.4 us
  waiting for transfers between devices: 46.2 us -> 17.7 us
  other arithmetic: 23.4 us -> 0.86 us
  local copies, waits for them, and re-layouts: 27 us -> 5.83 us
  matrix products: 13.9 us -> 0 us
  starting transfers between devices: 35.6 us -> 33.2 us
    all_to_all x1 -> x0, blocking collectives: 51.1 us -> none  [per_device(): lax.all_to_all(going_back, ('tile', 'sub'), split_axis=0, concat_axis=0,...]
    pallas_call x0 -> x7, Pallas kernels: none -> 34.4 us  [the longest x1 17.1 us: advect_all(): pl.pallas_call(functools.partial(advect_kernel, tracers, levels), grid=(t...]
    ppermute x14 -> x22, waiting for transfers between devices: 46.2 us -> 17.7 us  [the longest x14 17.1 us: per_device(): lax.ppermute(x, 'tile', [(i, i ^ d) for i in range(tiles)])]
    dot_general x9 -> x0, matrix products: 13.9 us -> none  [the longest x1 4.46 us: per_device(): jnp.einsum('bfj,bij->bfi', block_returns, block_weights, preferred_elemen...]
    concatenate x4 -> x1, local copies, waits for them, and re-layouts: 11.6 us -> 0.01 us  [per_device(): jnp.concatenate([half] + [arrived[d] for d in range(1, tiles)], axis=0)]
    div x3 -> x0, other arithmetic: 11.3 us -> none  [ppm_step(): (7.0 * (padded[..., 1:span_cells + 3] + padded[..., 2:span_cells + 4]) -...]
    all_to_all x1 -> x0, starting transfers between devices: 6.24 us -> none  [per_device(): lax.all_to_all(outgoing.astype(jnp.bfloat16), ('tile', 'sub'), split_axis...]
    mul x4 -> x1, other arithmetic: 5.66 us -> 0.07 us  [per_device(): sign * state[-1][:, ::-1]]
  transfers between devices with their start and end apart: 15 -> 22, of which waited for: 7 -> 8; matrix products, arithmetic and copies ran while one was open for 3% -> 2% of each run, Pallas kernels for 0% -> 26%
where the time goes in v1:
time: 93 us; the launch traced here: 92.8 us
  Pallas kernels  34.4 us (37%)
  starting transfers between devices  33.2 us (36%)
  waiting for transfers between devices  17.7 us (19%)
  local copies, waits for them, and re-layouts  5.83 us (6%)
    ppermute x14, starting transfers between devices, per_device(): lax.ppermute(x, 'tile', [(i, i ^ d) for i in range(tiles)])  19.9 us
    ppermute x14, waiting for transfers between devices, per_device(): lax.ppermute(x, 'tile', [(i, i ^ d) for i in range(tiles)])  17.1 us
    pallas_call x1, Pallas kernels, advect_all(): pl.pallas_call(functools.partial(advect_kernel, tracers, levels), grid=(t...  17.1 us
    pallas_call x1, Pallas kernels, backward(): pl.pallas_call(functools.partial(backward_kernel, dims), out_shape=(jax.S...  9.79 us
    pallas_call x1, Pallas kernels, forward(): pl.pallas_call(functools.partial(forward_kernel, dims), out_shape=(jax.Sh...  6.83 us
    unnamed x34, local copies, waits for them, and re-layouts  5.68 us
    ppermute x1, starting transfers between devices, per_device(): lax.ppermute(pack_b, flat, [(i, (i + 1 if i % 2 else i - 1) % devices) fo...  5.67 us
    ppermute x1, starting transfers between devices, per_device(): lax.ppermute(sign * state[-1][:, ::-1], 'tile', [(i, tiles - 1 - i) for i...  4.84 us
  transfers between devices with their start and end apart: 22, of which 8 were waited for; matrix products, arithmetic and copies ran while one was open for 2% of the time, Pallas kernels for 26%

profile of v1, /device:TPU:0, one launch (start us, length us, event | category | flops | bytes accessed | tf_op | source)
XLA Modules:
  0.0 92.8 jit_solution(3279716822639133383)
XLA Ops:
  0.6 0.0 copy-start
  0.7 1.7 %copy-done.1 = f32[20,12,2048]{2,0,1:T(8,128)S(1)} copy-done((f32[20,12,2048]{2,0,1:T(8,128)S(1)}, f32[20,12,2048]{2,0,1:T(8,128)}, u32[]{:S(2)}) %copy-start.1) | copy-done | bytes 1966104
  2.3 0.9 copy-done.3
  3.3 0.2 pack_edges.1
  3.5 0.5 collective-permute-start.4
  4.0 5.7 %collective-permute-start.5 = (f32[64,128]{1,0:T(8,128)S(1)}, f32[64,128]{1,0:T(8,128)S(1)}, u32[]{:S(2)}, u32[]{:S(2)}) collective-permute-start(f32[64,128]{1,0:T(8,128)S(1)} %get-tuple-element.20), channel_id=1, source_target_pairs={{0,15},{1,2},{2,1},{3,4},{4,3},{5,6},{6,5},{7,8},{8,7},{9,10},{10,... | collective-permute-start | bytes 98312 | tf_op jit(solution)/shard_map/ppermute | solution.py:453
  9.8 0.1 collective-permute-start
  9.9 0.8 dynamic-slice_add_fusion.slot_ref
  10.7 0.1 slice.12
  10.7 0.0 collective-permute-done.4.msg_a
  10.8 0.5 collective-permute-done.5.msg_b
  11.3 0.0 copy-start.8
  11.3 0.0 copy-start.9
  11.3 6.8 %blocks_to_rows.1 = (bf16[128,16,128]{2,1,0:T(8,128)(2,1)}, f32[128,16,128]{2,1,0:T(8,128)S(1)}) custom-call(s32[1]{0:T(128)} %bitcast.6.parity_ref, s32[256]{0:T(256)S(1)} %dynamic-slice_add_fusion.slot_ref, s32[256]{0:T(256)S(1)} %copy-done.10, f32[12,2048]{1,0:T(8,128)S(1)} %bitcast.28, f32[20,2048]{1,0:T(8,128)S(1)} %copy-done.4, ...), custom_call_target="tpu_custom_call" | custom-call | tf_op jit(solution)/shard_map/blocks_to_rows/pallas_call | solution.py:179
  18.2 0.0 copy-start.5
  18.2 1.0 %copy-done.5 = f32[128,16,128]{2,1,0:T(8,128)} copy-done((f32[128,16,128]{2,1,0:T(8,128)}, f32[128,16,128]{2,1,0:T(8,128)S(1)}, u32[]{:S(2)}) %copy-start.5) | copy-done | bytes 1048600
  19.1 0.0 collective-permute-start.6
  19.2 0.1 rev.3
  19.2 0.1 broadcast_multiply_fusion
  19.3 4.8 %collective-permute-start.1 = (f32[16,128]{1,0:T(8,128)S(1)}, f32[16,128]{1,0:T(8,128)S(1)}, u32[]{:S(2)}, u32[]{:S(2)}) collective-permute-start(f32[16,128]{1,0:T(8,128)S(1)} %broadcast_multiply_fusion), channel_id=1, source_target_pairs={{0,14},{2,12},{4,10},{6,8},{8,6},{10,4},{12,2},{14,0},{1,15},{3,13... | collective-permute-start | bytes 24584 | tf_op jit(solution)/shard_map/ppermute | solution.py:484
  24.1 0.1 ocean_edges.1
  24.3 0.1 collective-permute-start.3
  24.3 2.0 %collective-permute-start.2 = (f32[16,128]{1,0:T(8,128)S(1)}, f32[16,128]{1,0:T(8,128)S(1)}, u32[]{:S(2)}, u32[]{:S(2)}) collective-permute-start(f32[16,128]{1,0:T(8,128)S(1)} %ocean_edges.1), channel_id=1, source_target_pairs={{0,2},{2,4},{4,6},{6,8},{8,10},{10,12},{12,14},{14,0},{1,3},{3,5},... | collective-permute-start | bytes 24584 | tf_op jit(solution)/shard_map/ppermute | solution.py:479
  26.4 0.0 collective-permute-done.6.got
  26.4 1.2 %copy-done.6 = f32[128,16,128]{2,1,0:T(8,128)S(1)} copy-done((f32[128,16,128]{2,1,0:T(8,128)S(1)}, f32[128,16,128]{2,1,0:T(8,128)}, u32[]{:S(2)}) %copy-start.6) | copy-done | bytes 1048600
  27.6 0.1 merge_cores.1
  27.7 2.8 %collective-permute-start.7 = (bf16[16,16,128]{2,1,0:T(8,128)(2,1)S(1)}, bf16[16,16,128]{2,1,0:T(8,128)(2,1)S(1)}, u32[]{:S(2)}, u32[]{:S(2)}) collective-permute-start(bf16[16,16,128]{2,1,0:T(8,128)(2,1)S(1)} %get-tuple-element.24), channel_id=1, source_target_pairs={{0,14},{2,12},{4,10},{6,8},{8,6},{10,4},{12,2},{14,0},{1,15},{3,13... | collective-permute-start | bytes 196616 | tf_op jit(solution)/shard_map/ppermute | solution.py:470
  30.5 0.0 collective-permute-done
  30.5 0.5 collective-permute-start.8
  31.0 0.0 collective-permute-done.1
  31.0 0.0 collective-permute-start.9
  31.0 0.0 collective-permute-done.3
  31.0 4.4 %collective-permute-start.10 = (bf16[16,16,128]{2,1,0:T(8,128)(2,1)S(1)}, bf16[16,16,128]{2,1,0:T(8,128)(2,1)S(1)}, u32[]{:S(2)}, u32[]{:S(2)}) collective-permute-start(bf16[16,16,128]{2,1,0:T(8,128)(2,1)S(1)} %get-tuple-element.27), channel_id=1, source_target_pairs={{0,8},{2,10},{4,12},{6,14},{8,0},{10,2},{12,4},{14,6},{1,9},{3,11}... | collective-permute-start | bytes 196616 | tf_op jit(solution)/shard_map/ppermute | solution.py:470
  35.4 0.0 collective-permute-done.2
  35.4 0.5 collective-permute-start.11
  35.9 0.0 collective-permute-done.7.rest_0_
  35.9 1.0 %collective-permute-start.12 = (bf16[16,16,128]{2,1,0:T(8,128)(2,1)S(1)}, bf16[16,16,128]{2,1,0:T(8,128)(2,1)S(1)}, u32[]{:S(2)}, u32[]{:S(2)}) collective-permute-start(bf16[16,16,128]{2,1,0:T(8,128)(2,1)S(1)} %get-tuple-element.29), channel_id=1, source_target_pairs={{0,4},{2,6},{4,0},{6,2},{8,12},{10,14},{12,8},{14,10},{1,5},{3,7},... | collective-permute-start | bytes 196616 | tf_op jit(solution)/shard_map/ppermute | solution.py:470
  36.9 0.6 collective-permute-done.8.rest_1_
  37.5 1.4 %collective-permute-start.13 = (bf16[16,16,128]{2,1,0:T(8,128)(2,1)S(1)}, bf16[16,16,128]{2,1,0:T(8,128)(2,1)S(1)}, u32[]{:S(2)}, u32[]{:S(2)}) collective-permute-start(bf16[16,16,128]{2,1,0:T(8,128)(2,1)S(1)} %get-tuple-element.30), channel_id=1, source_target_pairs={{0,2},{2,0},{4,6},{6,4},{8,10},{10,8},{12,14},{14,12},{1,3},{3,1},... | collective-permute-start | bytes 196616 | tf_op jit(solution)/shard_map/ppermute | solution.py:470
  38.9 0.0 collective-permute-done.9.rest_2_
  38.9 2.3 %collective-permute-done.10.rest_3_ = bf16[16,16,128]{2,1,0:T(8,128)(2,1)S(1)} collective-permute-done((bf16[16,16,128]{2,1,0:T(8,128)(2,1)S(1)}, bf16[16,16,128]{2,1,0:T(8,128)(2,1)S(1)}, u32[]{:S(2)}, u32[]{:S(2)}) %collective-permute-start.10) | collective-permute-done | bytes 65568 | tf_op jit(solution)/shard_map/ppermute | solution.py:470
  41.2 0.2 collective-permute-done.11.rest_4_
  41.4 0.6 collective-permute-done.12.rest_5_
  42.0 0.0 collective-permute-done.13.rest_6_
  42.0 0.2 ocean_update.1
  42.2 2.9 %collective-permute-start.20 = (bf16[16,16,128]{2,1,0:T(8,128)(2,1)S(1)}, bf16[16,16,128]{2,1,0:T(8,128)(2,1)S(1)}, u32[]{:S(2)}, u32[]{:S(2)}) collective-permute-start(bf16[16,16,128]{2,1,0:T(8,128)(2,1)S(1)} %get-tuple-element.31), channel_id=1, source_target_pairs={{0,14},{2,12},{4,10},{6,8},{8,6},{10,4},{12,2},{14,0},{1,15},{3,13... | collective-permute-start | bytes 196616 | tf_op jit(solution)/shard_map/ppermute | solution.py:470
  45.2 1.6 %collective-permute-start.19 = (bf16[16,16,128]{2,1,0:T(8,128)(2,1)S(1)}, bf16[16,16,128]{2,1,0:T(8,128)(2,1)S(1)}, u32[]{:S(2)}, u32[]{:S(2)}) collective-permute-start(bf16[16,16,128]{2,1,0:T(8,128)(2,1)S(1)} %get-tuple-element.31), channel_id=1, source_target_pairs={{0,12},{2,14},{4,8},{6,10},{8,4},{10,6},{12,0},{14,2},{1,13},{3,15... | collective-permute-start | bytes 196616 | tf_op jit(solution)/shard_map/ppermute | solution.py:470
  46.8 0.0 collective-permute-start.18
  46.8 3.2 %collective-permute-start.17 = (bf16[16,16,128]{2,1,0:T(8,128)(2,1)S(1)}, bf16[16,16,128]{2,1,0:T(8,128)(2,1)S(1)}, u32[]{:S(2)}, u32[]{:S(2)}) collective-permute-start(bf16[16,16,128]{2,1,0:T(8,128)(2,1)S(1)} %get-tuple-element.31), channel_id=1, source_target_pairs={{0,8},{2,10},{4,12},{6,14},{8,0},{10,2},{12,4},{14,6},{1,9},{3,11}... | collective-permute-start | bytes 196616 | tf_op jit(solution)/shard_map/ppermute | solution.py:470
  49.9 1.2 %collective-permute-start.14 = (bf16[16,16,128]{2,1,0:T(8,128)(2,1)S(1)}, bf16[16,16,128]{2,1,0:T(8,128)(2,1)S(1)}, u32[]{:S(2)}, u32[]{:S(2)}) collective-permute-start(bf16[16,16,128]{2,1,0:T(8,128)(2,1)S(1)} %get-tuple-element.31), channel_id=1, source_target_pairs={{0,2},{2,0},{4,6},{6,4},{8,10},{10,8},{12,14},{14,12},{1,3},{3,1},... | collective-permute-start | bytes 196616 | tf_op jit(solution)/shard_map/ppermute | solution.py:470
  51.2 3.7 %collective-permute-done.14 = bf16[16,16,128]{2,1,0:T(8,128)(2,1)S(1)} collective-permute-done((bf16[16,16,128]{2,1,0:T(8,128)(2,1)S(1)}, bf16[16,16,128]{2,1,0:T(8,128)(2,1)S(1)}, u32[]{:S(2)}, u32[]{:S(2)}) %collective-permute-start.14) | collective-permute-done | bytes 65568 | tf_op jit(solution)/shard_map/ppermute | solution.py:470
  54.9 0.0 collective-permute-start.15
  54.9 4.9 %collective-permute-done.15 = bf16[16,16,128]{2,1,0:T(8,128)(2,1)S(1)} collective-permute-done((bf16[16,16,128]{2,1,0:T(8,128)(2,1)S(1)}, bf16[16,16,128]{2,1,0:T(8,128)(2,1)S(1)}, u32[]{:S(2)}, u32[]{:S(2)}) %collective-permute-start.15) | collective-permute-done | bytes 65568 | tf_op jit(solution)/shard_map/ppermute | solution.py:470
  59.8 0.4 collective-permute-start.16
  60.2 4.8 %collective-permute-done.16 = bf16[16,16,128]{2,1,0:T(8,128)(2,1)S(1)} collective-permute-done((bf16[16,16,128]{2,1,0:T(8,128)(2,1)S(1)}, bf16[16,16,128]{2,1,0:T(8,128)(2,1)S(1)}, u32[]{:S(2)}, u32[]{:S(2)}) %collective-permute-start.16) | collective-permute-done | bytes 65568 | tf_op jit(solution)/shard_map/ppermute | solution.py:470
  65.0 0.0 collective-permute-done.17
  65.0 0.0 collective-permute-done.18
  65.0 0.0 collective-permute-done.19
  65.1 0.0 collective-permute-done.20
  65.1 0.1 collective-permute-start.21
  65.2 17.1 %advect_levels.1.advected_hbm = f32[12,20,2048]{2,1,0:T(8,128)} custom-call(s32[1]{0:T(128)} %bitcast.6.parity_ref, f32[12,20,2048]{2,1,0:T(8,128)S(1)} %bitcast.23, f32[20,2048]{1,0:T(8,128)S(1)} %copy-done.4, f32[64,128]{1,0:T(8,128)S(1)} %collective-permute-done.4.msg_a, f32[64,128]{1,0:T(8,128)S(1)} %collective-permute-done.5.msg_b), custom_call_target="tpu_custom_call" | custom-call | flops 29491200 | bytes 3932160 | tf_op jit(solution)/shard_map/advect_levels/pallas_call | solution.py:312
  82.3 0.7 copy.16
  83.0 0.0 collective-permute-done.21.other
  83.0 9.8 %rows_to_columns.1 = (f32[16,2048]{1,0:T(8,128)}, f32[12,20,2048]{2,1,0:T(8,128)}) custom-call(s32[256]{0:T(256)S(1)} %dynamic-slice_add_fusion.slot_ref, s32[256]{0:T(256)S(1)} %copy-done.10, bf16[128,16,128]{2,1,0:T(8,128)(2,1)S(1)} %constant_dynamic-update-slice_fusion.mine, ...), custom_call_target="tpu_custom_call", output_to_operand_aliasing={{1}: (5, {})} | custom-call | tf_op jit(solution)/shard_map/rows_to_columns/pallas_call | solution.py:407
  (32 shorter events, 0.2 us)
Async XLA Ops:
  0.6 9.2 %copy-start = (s32[4096,1]{0,1:T(1,128)S(1)}, s32[4096,1]{0,1:T(1,128)}, u32[]{:S(2)}) copy-start(s32[4096,1]{0,1:T(1,128)} %param.14) | copy-start | bytes 49156
  0.7 1.7 %copy-start.1 = (f32[20,12,2048]{2,0,1:T(8,128)S(1)}, f32[20,12,2048]{2,0,1:T(8,128)}, u32[]{:S(2)}) copy-start(f32[20,12,2048]{2,0,1:T(8,128)} %param.10) | copy-start | bytes 5898244
  2.3 0.9 copy-start.3
  3.3 6.5 %copy-start.11 = (f32[16,16,128]{2,1,0:T(8,128)S(1)}, f32[16,16,128]{2,1,0:T(8,128)}, u32[]{:S(2)}) copy-start(f32[16,16,128]{2,1,0:T(8,128)} %param.17) | copy-start | bytes 393220
  3.3 7.4 %copy-start.2 = (f32[20,12,2048]{2,0,1:T(8,128)S(1)}, f32[20,12,2048]{2,0,1:T(8,128)}, u32[]{:S(2)}) copy-start(f32[20,12,2048]{2,0,1:T(8,128)} %param.10) | copy-start | bytes 5898244
  3.3 8.0 %copy-start.4 = (f32[20,2048]{1,0:T(8,128)S(1)}, f32[20,2048]{1,0:T(8,128)}, u32[]{:S(2)}) copy-start(f32[20,2048]{1,0:T(8,128)} %c_ref.1) | copy-start | bytes 491524
  3.3 8.0 %copy-start.7 = (f32[4,2048]{1,0:T(4,128)S(1)}, f32[4,2048]{1,0:T(4,128)}, u32[]{:S(2)}) copy-start(f32[4,2048]{1,0:T(4,128)} %air.1) | copy-start | bytes 98308
  3.3 8.0 %copy-start.10 = (s32[256]{0:T(256)S(1)}, s32[256]{0:T(256)}, u32[]{:S(2)}) copy-start(s32[256]{0:T(256)} %patch_ref.3) | copy-start | bytes 3076
  3.5 7.2 %collective-permute-start.4 = (f32[64,128]{1,0:T(8,128)S(1)}, f32[64,128]{1,0:T(8,128)S(1)}, u32[]{:S(2)}, u32[]{:S(2)}) collective-permute-start(f32[64,128]{1,0:T(8,128)S(1)} %get-tuple-element.19), channel_id=1, source_target_pairs={{0,1},{1,0},{2,3},{3,2},{4,5},{5,4},{6,7},{7,6},{8,9},{9,8},{10,11... | collective-permute-start | bytes 98312 | tf_op jit(solution)/shard_map/ppermute | solution.py:452
  4.0 7.3 %collective-permute-start.5 = (f32[64,128]{1,0:T(8,128)S(1)}, f32[64,128]{1,0:T(8,128)S(1)}, u32[]{:S(2)}, u32[]{:S(2)}) collective-permute-start(f32[64,128]{1,0:T(8,128)S(1)} %get-tuple-element.20), channel_id=1, source_target_pairs={{0,15},{1,2},{2,1},{3,4},{4,3},{5,6},{6,5},{7,8},{8,7},{9,10},{10,... | collective-permute-start | bytes 98312 | tf_op jit(solution)/shard_map/ppermute | solution.py:453
  9.8 20.7 %collective-permute-start = (f32[16,128]{1,0:T(8,128)S(1)}, f32[16,128]{1,0:T(8,128)S(1)}, u32[]{:S(2)}, u32[]{:S(2)}) collective-permute-start(f32[16,128]{1,0:T(8,128)S(1)} %fusion), channel_id=1, source_target_pairs={{0,1},{1,0},{2,3},{3,2},{4,5},{5,4},{6,7},{7,6},{8,9},{9,8},{10,11... | collective-permute-start | bytes 24584 | tf_op jit(solution)/shard_map/ppermute | solution.py:488
  11.3 30.7 %copy-start.8 = (f32[16,128]{1,0:T(8,128)S(1)}, f32[16,128]{1,0:T(8,128)}, u32[]{:S(2)}) copy-start(f32[16,128]{1,0:T(8,128)} %rate.1) | copy-start | bytes 24580
  11.3 30.7 %copy-start.9 = (s32[16,128]{1,0:T(8,128)S(1)}, s32[16,128]{1,0:T(8,128)}, u32[]{:S(2)}) copy-start(s32[16,128]{1,0:T(8,128)} %wet.1) | copy-start | bytes 24580
  18.2 1.0 %copy-start.5 = (f32[128,16,128]{2,1,0:T(8,128)}, f32[128,16,128]{2,1,0:T(8,128)S(1)}, u32[]{:S(2)}) copy-start(f32[128,16,128]{2,1,0:T(8,128)S(1)} %get-tuple-element.21.keep) | copy-start | bytes 3145732
  19.1 7.2 %collective-permute-start.6 = (bf16[128,16,128]{2,1,0:T(8,128)(2,1)}, bf16[128,16,128]{2,1,0:T(8,128)(2,1)S(1)}, u32[]{:S(2)}, u32[]{:S(2)}) collective-permute-start(bf16[128,16,128]{2,1,0:T(8,128)(2,1)} %get-tuple-element.22), channel_id=1, source_target_pairs={{0,1},{1,0},{2,3},{3,2},{4,5},{5,4},{6,7},{7,6},{8,9},{9,8},{10,11... | collective-permute-start | bytes 1572872 | tf_op jit(solution)/shard_map/ppermute | solution.py:469
  19.3 11.7 %collective-permute-start.1 = (f32[16,128]{1,0:T(8,128)S(1)}, f32[16,128]{1,0:T(8,128)S(1)}, u32[]{:S(2)}, u32[]{:S(2)}) collective-permute-start(f32[16,128]{1,0:T(8,128)S(1)} %broadcast_multiply_fusion), channel_id=1, source_target_pairs={{0,14},{2,12},{4,10},{6,8},{8,6},{10,4},{12,2},{14,0},{1,15},{3,13... | collective-permute-start | bytes 24584 | tf_op jit(solution)/shard_map/ppermute | solution.py:484
  24.3 6.8 %collective-permute-start.3 = (f32[16,128]{1,0:T(8,128)S(1)}, f32[16,128]{1,0:T(8,128)S(1)}, u32[]{:S(2)}, u32[]{:S(2)}) collective-permute-start(f32[16,128]{1,0:T(8,128)S(1)} %ocean_edges.1), channel_id=1, source_target_pairs={{2,0},{4,2},{6,4},{8,6},{10,8},{12,10},{14,12},{0,14},{3,1},{5,3},... | collective-permute-start | bytes 24584 | tf_op jit(solution)/shard_map/ppermute | solution.py:480
  24.3 11.1 %collective-permute-start.2 = (f32[16,128]{1,0:T(8,128)S(1)}, f32[16,128]{1,0:T(8,128)S(1)}, u32[]{:S(2)}, u32[]{:S(2)}) collective-permute-start(f32[16,128]{1,0:T(8,128)S(1)} %ocean_edges.1), channel_id=1, source_target_pairs={{0,2},{2,4},{4,6},{6,8},{8,10},{10,12},{12,14},{14,0},{1,3},{3,5},... | collective-permute-start | bytes 24584 | tf_op jit(solution)/shard_map/ppermute | solution.py:479
  26.4 1.2 %copy-start.6 = (f32[128,16,128]{2,1,0:T(8,128)S(1)}, f32[128,16,128]{2,1,0:T(8,128)}, u32[]{:S(2)}) copy-start(f32[128,16,128]{2,1,0:T(8,128)} %copy-done.5) | copy-start | bytes 3145732
  27.7 8.2 %collective-permute-start.7 = (bf16[16,16,128]{2,1,0:T(8,128)(2,1)S(1)}, bf16[16,16,128]{2,1,0:T(8,128)(2,1)S(1)}, u32[]{:S(2)}, u32[]{:S(2)}) collective-permute-start(bf16[16,16,128]{2,1,0:T(8,128)(2,1)S(1)} %get-tuple-element.24), channel_id=1, source_target_pairs={{0,14},{2,12},{4,10},{6,8},{8,6},{10,4},{12,2},{14,0},{1,15},{3,13... | collective-permute-start | bytes 196616 | tf_op jit(solution)/shard_map/ppermute | solution.py:470
  30.5 7.0 %collective-permute-start.8 = (bf16[16,16,128]{2,1,0:T(8,128)(2,1)S(1)}, bf16[16,16,128]{2,1,0:T(8,128)(2,1)S(1)}, u32[]{:S(2)}, u32[]{:S(2)}) collective-permute-start(bf16[16,16,128]{2,1,0:T(8,128)(2,1)S(1)} %get-tuple-element.25), channel_id=1, source_target_pairs={{0,12},{2,14},{4,8},{6,10},{8,4},{10,6},{12,0},{14,2},{1,13},{3,15... | collective-permute-start | bytes 196616 | tf_op jit(solution)/shard_map/ppermute | solution.py:470
  31.0 7.9 %collective-permute-start.9 = (bf16[16,16,128]{2,1,0:T(8,128)(2,1)S(1)}, bf16[16,16,128]{2,1,0:T(8,128)(2,1)S(1)}, u32[]{:S(2)}, u32[]{:S(2)}) collective-permute-start(bf16[16,16,128]{2,1,0:T(8,128)(2,1)S(1)} %get-tuple-element.26), channel_id=1, source_target_pairs={{0,10},{2,8},{4,14},{6,12},{8,2},{10,0},{12,6},{14,4},{1,11},{3,9}... | collective-permute-start | bytes 196616 | tf_op jit(solution)/shard_map/ppermute | solution.py:470
  31.0 10.2 %collective-permute-start.10 = (bf16[16,16,128]{2,1,0:T(8,128)(2,1)S(1)}, bf16[16,16,128]{2,1,0:T(8,128)(2,1)S(1)}, u32[]{:S(2)}, u32[]{:S(2)}) collective-permute-start(bf16[16,16,128]{2,1,0:T(8,128)(2,1)S(1)} %get-tuple-element.27), channel_id=1, source_target_pairs={{0,8},{2,10},{4,12},{6,14},{8,0},{10,2},{12,4},{14,6},{1,9},{3,11}... | collective-permute-start | bytes 196616 | tf_op jit(solution)/shard_map/ppermute | solution.py:470
  35.4 6.0 %collective-permute-start.11 = (bf16[16,16,128]{2,1,0:T(8,128)(2,1)S(1)}, bf16[16,16,128]{2,1,0:T(8,128)(2,1)S(1)}, u32[]{:S(2)}, u32[]{:S(2)}) collective-permute-start(bf16[16,16,128]{2,1,0:T(8,128)(2,1)S(1)} %get-tuple-element.28), channel_id=1, source_target_pairs={{0,6},{2,4},{4,2},{6,0},{8,14},{10,12},{12,10},{14,8},{1,7},{3,5},... | collective-permute-start | bytes 196616 | tf_op jit(solution)/shard_map/ppermute | solution.py:470
  35.9 6.1 %collective-permute-start.12 = (bf16[16,16,128]{2,1,0:T(8,128)(2,1)S(1)}, bf16[16,16,128]{2,1,0:T(8,128)(2,1)S(1)}, u32[]{:S(2)}, u32[]{:S(2)}) collective-permute-start(bf16[16,16,128]{2,1,0:T(8,128)(2,1)S(1)} %get-tuple-element.29), channel_id=1, source_target_pairs={{0,4},{2,6},{4,0},{6,2},{8,12},{10,14},{12,8},{14,10},{1,5},{3,7},... | collective-permute-start | bytes 196616 | tf_op jit(solution)/shard_map/ppermute | solution.py:470
  37.5 4.5 %collective-permute-start.13 = (bf16[16,16,128]{2,1,0:T(8,128)(2,1)S(1)}, bf16[16,16,128]{2,1,0:T(8,128)(2,1)S(1)}, u32[]{:S(2)}, u32[]{:S(2)}) collective-permute-start(bf16[16,16,128]{2,1,0:T(8,128)(2,1)S(1)} %get-tuple-element.30), channel_id=1, source_target_pairs={{0,2},{2,0},{4,6},{6,4},{8,10},{10,8},{12,14},{14,12},{1,3},{3,1},... | collective-permute-start | bytes 196616 | tf_op jit(solution)/shard_map/ppermute | solution.py:470
  42.2 22.8 %collective-permute-start.20 = (bf16[16,16,128]{2,1,0:T(8,128)(2,1)S(1)}, bf16[16,16,128]{2,1,0:T(8,128)(2,1)S(1)}, u32[]{:S(2)}, u32[]{:S(2)}) collective-permute-start(bf16[16,16,128]{2,1,0:T(8,128)(2,1)S(1)} %get-tuple-element.31), channel_id=1, source_target_pairs={{0,14},{2,12},{4,10},{6,8},{8,6},{10,4},{12,2},{14,0},{1,15},{3,13... | collective-permute-start | bytes 196616 | tf_op jit(solution)/shard_map/ppermute | solution.py:470
  45.2 19.9 %collective-permute-start.19 = (bf16[16,16,128]{2,1,0:T(8,128)(2,1)S(1)}, bf16[16,16,128]{2,1,0:T(8,128)(2,1)S(1)}, u32[]{:S(2)}, u32[]{:S(2)}) collective-permute-start(bf16[16,16,128]{2,1,0:T(8,128)(2,1)S(1)} %get-tuple-element.31), channel_id=1, source_target_pairs={{0,12},{2,14},{4,8},{6,10},{8,4},{10,6},{12,0},{14,2},{1,13},{3,15... | collective-permute-start | bytes 196616 | tf_op jit(solution)/shard_map/ppermute | solution.py:470
  46.8 18.2 %collective-permute-start.18 = (bf16[16,16,128]{2,1,0:T(8,128)(2,1)S(1)}, bf16[16,16,128]{2,1,0:T(8,128)(2,1)S(1)}, u32[]{:S(2)}, u32[]{:S(2)}) collective-permute-start(bf16[16,16,128]{2,1,0:T(8,128)(2,1)S(1)} %get-tuple-element.31), channel_id=1, source_target_pairs={{0,10},{2,8},{4,14},{6,12},{8,2},{10,0},{12,6},{14,4},{1,11},{3,9}... | collective-permute-start | bytes 196616 | tf_op jit(solution)/shard_map/ppermute | solution.py:470
  46.8 18.2 %collective-permute-start.17 = (bf16[16,16,128]{2,1,0:T(8,128)(2,1)S(1)}, bf16[16,16,128]{2,1,0:T(8,128)(2,1)S(1)}, u32[]{:S(2)}, u32[]{:S(2)}) collective-permute-start(bf16[16,16,128]{2,1,0:T(8,128)(2,1)S(1)} %get-tuple-element.31), channel_id=1, source_target_pairs={{0,8},{2,10},{4,12},{6,14},{8,0},{10,2},{12,4},{14,6},{1,9},{3,11}... | collective-permute-start | bytes 196616 | tf_op jit(solution)/shard_map/ppermute | solution.py:470
  49.9 4.9 %collective-permute-start.14 = (bf16[16,16,128]{2,1,0:T(8,128)(2,1)S(1)}, bf16[16,16,128]{2,1,0:T(8,128)(2,1)S(1)}, u32[]{:S(2)}, u32[]{:S(2)}) collective-permute-start(bf16[16,16,128]{2,1,0:T(8,128)(2,1)S(1)} %get-tuple-element.31), channel_id=1, source_target_pairs={{0,2},{2,0},{4,6},{6,4},{8,10},{10,8},{12,14},{14,12},{1,3},{3,1},... | collective-permute-start | bytes 196616 | tf_op jit(solution)/shard_map/ppermute | solution.py:470
  54.9 4.9 %collective-permute-start.15 = (bf16[16,16,128]{2,1,0:T(8,128)(2,1)S(1)}, bf16[16,16,128]{2,1,0:T(8,128)(2,1)S(1)}, u32[]{:S(2)}, u32[]{:S(2)}) collective-permute-start(bf16[16,16,128]{2,1,0:T(8,128)(2,1)S(1)} %get-tuple-element.31), channel_id=1, source_target_pairs={{0,4},{2,6},{4,0},{6,2},{8,12},{10,14},{12,8},{14,10},{1,5},{3,7},... | collective-permute-start | bytes 196616 | tf_op jit(solution)/shard_map/ppermute | solution.py:470
  59.8 5.2 %collective-permute-start.16 = (bf16[16,16,128]{2,1,0:T(8,128)(2,1)S(1)}, bf16[16,16,128]{2,1,0:T(8,128)(2,1)S(1)}, u32[]{:S(2)}, u32[]{:S(2)}) collective-permute-start(bf16[16,16,128]{2,1,0:T(8,128)(2,1)S(1)} %get-tuple-element.31), channel_id=1, source_target_pairs={{0,6},{2,4},{4,2},{6,0},{8,14},{10,12},{12,10},{14,8},{1,7},{3,5},... | collective-permute-start | bytes 196616 | tf_op jit(solution)/shard_map/ppermute | solution.py:470
  65.1 17.9 %collective-permute-start.21 = (bf16[128,16,128]{2,1,0:T(8,128)(2,1)S(1)}, bf16[128,16,128]{2,1,0:T(8,128)(2,1)S(1)}, u32[]{:S(2)}, u32[]{:S(2)}) collective-permute-start(bf16[128,16,128]{2,1,0:T(8,128)(2,1)S(1)} %constant_dynamic-update-slice_fusion.mine), channel_id=1, source_target_pairs={{0,1},{1,0},{2,3},{3,2},{4,5},{5,4},{6,7},{7,6},{8,9},{9,8},{10,11... | collective-permute-start | bytes 1572872 | tf_op jit(solution)/shard_map/ppermute | solution.py:498

commit v2 on v1

v2 whole, which is shorter than its diff:
```python
import functools

import jax
import jax.numpy as jnp
from jax import lax
from jax.experimental import pallas as pl
from jax.experimental.pallas import tpu as pltpu
from jax.sharding import PartitionSpec as P

ASTEPS = 3
NU = 0.2
COUPLE = 0.5
LANES = 128
EDGE = 16
GROUPS = LANES // EDGE
UNROLL = 64

VMEM = pl.BlockSpec(memory_space=pltpu.VMEM)
SMEM = pl.BlockSpec(memory_space=pltpu.SMEM)
ANY = pl.BlockSpec(memory_space=pl.ANY)
HBM = pl.BlockSpec(memory_space=pltpu.HBM)
f32 = jnp.float32
bf16 = jnp.bfloat16


def params(limit):
    return pltpu.CompilerParams(vmem_limit_bytes=limit)


def place():
    sizes = lax.axis_size("tile"), lax.axis_size("sub")
    return lax.axis_index("tile"), lax.axis_index("sub"), *sizes


def is_even():
    tile, sub, _, subs = place()
    return (tile * subs + sub) % 2 == 0


def lane_roll(x, shift):
    length = x.shape[-1]
    shift = shift % length
    return x if shift == 0 else pltpu.roll(x, shift, x.ndim - 1)


def coefficients(c):
    d = 1.0 - c
    return c * d * d * (1.0 / 12.0), c * c * d * (1.0 / 12.0), c * c * (3.0 - 2.0 * c)


def advect(q, right, left, own):
    for _ in range(ASTEPS):
        pair = q + lane_roll(q, -1)
        edge = 8.0 * pair - (lane_roll(pair, 1) + lane_roll(pair, -1))
        flux = right * edge - left * lane_roll(edge, 1) + own * q
        q = q - (flux - lane_roll(flux, 1))
    return q


def pack_kernel(
    tracers, levels, q_hbm, c_hbm, a_ref, b_ref, left_t, right_t, left_c, right_c, sems
):
    span = q_hbm.shape[2]
    copies = [
        pltpu.make_async_copy(src, dst, sems.at[i])
        for i, (src, dst) in enumerate(
            (
                (q_hbm.at[:, :, pl.ds(0, LANES)], left_t),
                (q_hbm.at[:, :, pl.ds(span - LANES, LANES)], right_t),
                (c_hbm.at[:, pl.ds(0, LANES)], left_c),
                (c_hbm.at[:, pl.ds(span - LANES, LANES)], right_c),
            )
        )
    ]
    for copy in copies:
        copy.start()
    for copy in copies:
        copy.wait()
    even = is_even()
    lane = lax.broadcasted_iota(jnp.int32, (levels, LANES), 1)
    pad = pl.cdiv(levels, 8) * 8
    for out, from_left in ((a_ref, jnp.logical_not(even)), (b_ref, even)):
        for part in range(pl.cdiv(tracers + 1, GROUPS)):
            total = jnp.zeros((levels, LANES), f32)
            for group in range(GROUPS):
                item = part * GROUPS + group
                if item > tracers:
                    continue
                low = left_t[item] if item < tracers else left_c[...]
                high = right_t[item] if item < tracers else right_c[...]
                moved = jnp.where(
                    from_left,
                    lane_roll(low, EDGE * group),
                    lane_roll(high, EDGE * (group + 1)),
                )
                total = jnp.where(lane // EDGE == group, moved, total)
            out[part * pad : part * pad + levels, :] = total
        top = pl.cdiv(tracers + 1, GROUPS) * pad
        for item in range(tracers):
            out[top + item : top + item + 1, :] = jnp.where(
                from_left, left_t[item, 0:1, :], right_t[item, 0:1, :]
            )
        out[top + tracers : top + tracers + 1, :] = jnp.where(
            from_left, left_c[0:1, :], right_c[0:1, :]
        )


def pack(tracers_t, courant):
    tracers, levels, span = tracers_t.shape
    pad = pl.cdiv(levels, 8) * 8
    rows = pl.cdiv(tracers + 1, GROUPS) * pad + pl.cdiv(tracers + 1, 8) * 8
    message = jax.ShapeDtypeStruct((rows, LANES), f32)
    return pl.pallas_call(
        functools.partial(pack_kernel, tracers, levels),
        out_shape=(message, message),
        in_specs=[HBM, HBM],
        out_specs=(VMEM, VMEM),
        scratch_shapes=[
            pltpu.VMEM((tracers, levels, LANES), f32),
            pltpu.VMEM((tracers, levels, LANES), f32),
            pltpu.VMEM((levels, LANES), f32),
            pltpu.VMEM((levels, LANES), f32),
            pltpu.SemaphoreType.DMA((4,)),
        ],
        compiler_params=params(56 * 1024 * 1024),
        name="pack_edges",
    )(tracers_t, courant)


def high_low(x):
    high = x.astype(bf16)
    return high, (x - high.astype(f32)).astype(bf16)


def forward_kernel(
    dims, slot_ref, patch_ref, level0, courant0, air, msg_a, msg_b, beside,
    weights_hbm, send_ref, keep_hbm, surface, total, weights, sems, keep_sem,
):
    tracers, span, top = dims
    blocks = weights.shape[0]
    copies = [
        pltpu.make_async_copy(
            weights_hbm.at[pl.ds(i, UNROLL)], weights.at[pl.ds(i, UNROLL)], sems.at[i // UNROLL]
        )
        for i in range(0, blocks, UNROLL)
    ]
    for copy in copies:
        copy.start()
    even = is_even()
    a, b = msg_a[top : top + tracers + 1, :], msg_b[top : top + tracers + 1, :]
    left, right = jnp.where(even, b, a), jnp.where(even, a, b)
    q = jnp.concatenate([left[:tracers], level0[...], right[:tracers]], axis=1)
    c = jnp.concatenate([left[tracers:], courant0[0:1, :], right[tracers:]], axis=1)
    advected = advect(q, *coefficients(c))[:, LANES : LANES + span]
    fields = jnp.concatenate([advected, air[...]], axis=0).astype(bf16)
    for p in range(span // LANES):
        surface[p] = fields[:, p * LANES : (p + 1) * LANES]
    total[...] = jnp.zeros_like(total)
    zero = jnp.zeros(surface.shape[1:], bf16)
    height = zero.shape[0]

    def step(g, carry):
        base = g * UNROLL
        pltpu.make_async_copy(
            weights_hbm.at[pl.ds(base, UNROLL)], weights.at[pl.ds(base, UNROLL)], sems.at[g]
        ).wait()
        products = []
        for u in range(0, UNROLL, 2):
            first, second = surface[patch_ref[base + u]], surface[patch_ref[base + u + 1]]
            rows = jnp.concatenate(
                [jnp.concatenate([first, zero], 1), jnp.concatenate([zero, second], 1)], 0
            )
            pair = weights[pl.ds(base + u, 2)].reshape(2 * LANES, LANES)
            both = jnp.dot(rows, pair, preferred_element_type=f32)
            products += [both[:height], both[height:]]
        for u in range(UNROLL):
            total[slot_ref[base + u]] += products[u]
        return carry

    lax.fori_loop(0, blocks // UNROLL, step, 0)
    half = total.shape[0] // 2
    keep = pltpu.make_async_copy(total.at[pl.ds(0, half)], keep_hbm, keep_sem)
    keep.start()
    send_ref[:half] = total[half:].astype(bf16)
    send_ref[half], send_ref[half + 1] = high_low(beside[...])
    keep.wait()


def forward(slot, patch, level0, courant, air, msg_a, msg_b, beside, weights, rows):
    tracers, span = level0.shape
    levels = courant.shape[0]
    fields = tracers + air.shape[0]
    pad = pl.cdiv(levels, 8) * 8
    top = pl.cdiv(tracers + 1, GROUPS) * pad
    return pl.pallas_call(
        functools.partial(forward_kernel, (tracers, span, top)),
        out_shape=(
            jax.ShapeDtypeStruct((rows // 2 + 2, fields, LANES), bf16),
            jax.ShapeDtypeStruct((rows // 2, fields, LANES), f32),
        ),
        in_specs=[SMEM] * 2 + [VMEM] * 6 + [HBM],
        out_specs=(VMEM, HBM),
        scratch_shapes=[
            pltpu.VMEM((span // LANES, fields, LANES), bf16),
            pltpu.VMEM((rows, fields, LANES), f32),
            pltpu.VMEM(weights.shape, bf16),
            pltpu.SemaphoreType.DMA((weights.shape[0] // UNROLL,)),
            pltpu.SemaphoreType.DMA,
        ],
        compiler_params=params(52 * 1024 * 1024),
        name="blocks_to_rows",
    )(slot, patch, level0, courant, air, msg_a, msg_b, beside, weights)


def with_edges(d):
    return d & (d + 1) == 0


def merge_kernel(chunk, keep, got, state, fold, own_ref, beside_ref, *outs):
    rows, fields, lanes = state.shape
    lane = lax.broadcasted_iota(jnp.int32, (fields, lanes), 1)
    edges = jnp.zeros((fields, lanes), f32)
    for r in range(rows):
        edges = jnp.where(lane == r, lane_roll(state[r], r + 1), edges)
        edges = jnp.where(lane == rows + r, lane_roll(state[r], rows + r), edges)
    more = high_low(edges) + high_low(fold[...])
    own_ref[...] = keep[:chunk] + got[:chunk].astype(f32)
    for d, out in enumerate(outs, 1):
        part = slice(d * chunk, (d + 1) * chunk)
        out[:chunk] = (keep[part] + got[part].astype(f32)).astype(bf16)
        if with_edges(d):
            for i, extra in enumerate(more):
                out[chunk + i] = extra
    last = keep.shape[0]
    beside_ref[...] = got[last].astype(f32) + got[last + 1].astype(f32)


def merge(keep, got, state, fold, chunk):
    rows, fields, lanes = keep.shape
    count = rows // chunk
    return pl.pallas_call(
        functools.partial(merge_kernel, chunk),
        out_shape=(
            jax.ShapeDtypeStruct((chunk, fields, lanes), f32),
            jax.ShapeDtypeStruct((fields, lanes), f32),
        )
        + tuple(
            jax.ShapeDtypeStruct((chunk + 4 * with_edges(d), fields, lanes), bf16)
            for d in range(1, count)
        ),
        in_specs=[VMEM] * 4,
        out_specs=(VMEM,) * (count + 1),
        compiler_params=params((10 if count < 16 else 24) * 1024 * 1024),
        name="merge_cores",
    )(keep, got, state, fold)


def ocean_kernel(count, state, beside, rate, wet, own, *rest):
    got, (next_ref, half_ref) = rest[:count], rest[-2:]
    rows, fields, lanes = state.shape
    lane = lax.broadcasted_iota(jnp.int32, (fields, lanes), 1)
    tile, sub, tiles, subs = place()
    to_east, to_west = tile ^ ((tile + 1) % tiles), tile ^ ((tile + tiles - 1) % tiles)

    def extra(chunk, i):
        return chunk[rows + i].astype(f32) + chunk[rows + i + 1].astype(f32)

    from_east = from_west = jnp.zeros((fields, lanes), f32)
    for d, chunk in enumerate(got, 1):
        if with_edges(d):
            edges = extra(chunk, 0)
            from_east = jnp.where(to_east == d, edges, from_east)
            from_west = jnp.where(to_west == d, edges, from_west)
    south = jnp.where(sub == 0, 0.0, beside[...])
    north = jnp.where(sub == subs - 1, extra(got[-1], 2), beside[...])
    for r in range(rows):
        here = state[r]
        west = jnp.where(lane == 0, lane_roll(from_west, -r), lane_roll(here, 1))
        east = jnp.where(
            lane == lanes - 1, lane_roll(from_east, lanes - 1 - rows - r), lane_roll(here, -1)
        )
        below = state[r - 1] if r else south
        above = state[r + 1] if r < rows - 1 else north
        lateral = west + east + below + above - 4.0 * here
        remapped = own[r]
        for chunk in got:
            remapped = remapped + chunk[r].astype(f32)
        new = here + wet[r : r + 1, :].astype(f32) * (
            rate[r : r + 1, :] * (remapped - here) + NU * lateral
        )
        next_ref[r] = new
        half_ref[r] = new.astype(bf16)


def ocean(state, beside, rate, wet, own, got, after):
    rows, fields, lanes = state.shape
    return pl.pallas_call(
        functools.partial(ocean_kernel, len(got)),
        out_shape=(
            jax.ShapeDtypeStruct(state.shape, f32),
            jax.ShapeDtypeStruct(state.shape, bf16),
        ),
        in_specs=[VMEM] * (5 + len(got)) + [ANY],
        out_specs=(VMEM, VMEM),
        compiler_params=params(8 * 1024 * 1024),
        name="ocean_update",
    )(state, beside, rate, wet, own, *got, after)


def gather_kernel(count, *refs):
    out = refs[-1]
    chunk = refs[0].shape[0]
    for i in range(count):
        out[i * chunk : (i + 1) * chunk] = refs[i][...]


def gather_rows(parts, after):
    chunk, fields, lanes = parts[0].shape
    return pl.pallas_call(
        functools.partial(gather_kernel, len(parts)),
        out_shape=jax.ShapeDtypeStruct((chunk * len(parts), fields, lanes), bf16),
        in_specs=[VMEM] * len(parts) + [ANY],
        out_specs=VMEM,
        compiler_params=params(8 * 1024 * 1024),
        name="gather_rows",
    )(*parts, after)


def advect_kernel(
    tracers, levels, first, group, q_ref, c_ref, msg_a, msg_b, *rest
):
    out_ref, flag_ref, right, left, own, state, lhs, band = rest[-8:]
    even = is_even()
    span = q_ref.shape[2]
    pad = pl.cdiv(levels, 8) * 8
    tiles = span // LANES + 2
    rows = group * pad
    tile = lambda i: slice(i * LANES, (i + 1) * LANES)

    def sides(item):
        start = pl.multiple_of(item // GROUPS * pad, 8)
        shift = EDGE * (item % GROUPS)
        a, b = msg_a[pl.ds(start, levels), :], msg_b[pl.ds(start, levels), :]
        before, after = jnp.where(even, b, a), jnp.where(even, a, b)
        return (
            pltpu.roll(before, (2 * LANES - EDGE - shift) % LANES, 1),
            pltpu.roll(after, (LANES - shift) % LANES, 1),
        )

    @pl.when(pl.program_id(0) == 0)
    def _():
        before, after = sides(tracers)
        c = jnp.concatenate([before, c_ref[...], after], axis=1)
        for ref, value in zip((right, left, own), coefficients(c)):
            ref[...] = jnp.zeros_like(ref)
            for i in range(tiles):
                ref[i, :levels] = value[:, tile(i)]
        state[...] = jnp.zeros_like(state)
        r = lax.broadcasted_iota(jnp.int32, band.shape, 0) % (2 * LANES)
        j = lax.broadcasted_iota(jnp.int32, band.shape, 1)
        column = jnp.where(r < LANES, r, jnp.where(r < LANES + LANES // 2, r, r - 2 * LANES))
        d = column - jnp.where(j < LANES, j, j - LANES - 1)
        weight = jnp.where((d == 0) | (d == 1), 7.0, jnp.where((d == -1) | (d == 2), -1.0, 0.0))
        band[...] = weight.astype(bf16)
        flag_ref[...] = jnp.zeros_like(flag_ref)

    for t in range(group):
        before, after = sides(pl.program_id(0) * group + first + t)
        part = slice(t * pad, t * pad + levels)
        state[0, part] = before
        for i in range(1, tiles - 1):
            state[i, part] = q_ref[t, :, tile(i - 1)]
        state[tiles - 1, part] = after

    lane = lax.broadcasted_iota(jnp.int32, (rows, LANES), 1)
    for _ in range(ASTEPS):
        halves = [high_low(state[i]) for i in range(tiles)]
        for i in range(tiles):
            part = slice(i * rows, (i + 1) * rows)
            for h in range(2):
                lhs[part, tile(2 * h)] = halves[i][h]
                lhs[part, tile(2 * h + 1)] = jnp.where(
                    lane < LANES // 2, halves[min(i + 1, tiles - 1)][h], halves[max(i - 1, 0)][h]
                )
        edges = jnp.dot(lhs[...], band[...], preferred_element_type=f32)
        last = None
        for i in range(tiles):
            edge = edges[i * rows : (i + 1) * rows].reshape(group, pad, 2 * LANES)
            q = state[i]
            flux = (
                right[i] * edge[..., :LANES] - left[i] * edge[..., LANES:]
            ).reshape(rows, LANES) + (own[i] * q.reshape(group, pad, LANES)).reshape(rows, LANES)
            moved = pltpu.roll(flux, 1, 1)
            before = moved if last is None else jnp.where(lane == 0, last, moved)
            state[i] = q - (flux - before)
            last = moved

    for t in range(group):
        for i in range(1, tiles - 1):
            out_ref[t, :, tile(i - 1)] = state[i, t * pad : t * pad + levels]


def advect_some(tracers_t, courant, msg_a, msg_b, first, count, after, into=None):
    tracers, levels, span = tracers_t.shape
    group = 2 if count % 2 == 0 and first % 2 == 0 else 1
    tiles, pad = span // LANES + 2, pl.cdiv(levels, 8) * 8
    whole = lambda shape: pl.BlockSpec(shape, lambda i: (0,) * len(shape))
    block = pl.BlockSpec((group, levels, span), lambda i: (i + first // group, 0, 0))
    more = [after] if into is None else [after, into]
    return pl.pallas_call(
        functools.partial(advect_kernel, tracers, levels, first, group),
        grid=(count // group,),
        out_shape=(
            jax.ShapeDtypeStruct(tracers_t.shape, f32),
            jax.ShapeDtypeStruct((8, LANES), f32),
        ),
        in_specs=[
            block,
            whole(courant.shape),
            whole(msg_a.shape),
            whole(msg_b.shape),
        ]
        + [ANY] * len(more),
        out_specs=(block, whole((8, LANES))),
        input_output_aliases={} if into is None else {5: 0},
        scratch_shapes=[pltpu.VMEM((tiles, pad, LANES), f32)] * 3
        + [
            pltpu.VMEM((tiles, group * pad, LANES), f32),
            pltpu.VMEM((tiles * group * pad, 4 * LANES), bf16),
            pltpu.VMEM((4 * LANES, 2 * LANES), bf16),
        ],
        compiler_params=params(12 * 1024 * 1024),
        cost_estimate=pl.CostEstimate(
            flops=200 * count * levels * span,
            bytes_accessed=8 * count * levels * span,
            transcendentals=0,
        ),
        name="advect_levels",
    )(tracers_t, courant, msg_a, msg_b, *more)


def backward_kernel(
    slot_ref, patch_ref, mine, other, weights_hbm, advected_hbm, air_ref, out_hbm,
    rows, total, bottom, sem, weights, sems,
):
    copies = [
        pltpu.make_async_copy(
            weights_hbm.at[pl.ds(i, UNROLL)], weights.at[pl.ds(i, UNROLL)], sems.at[i // UNROLL]
        )
        for i in range(0, weights.shape[0], UNROLL)
    ]
    for copy in copies:
        copy.start()
    fetch = pltpu.make_async_copy(advected_hbm.at[:, pl.ds(0, 8), :], bottom, sem)
    fetch.start()
    tracers, _, span = bottom.shape
    blocks = weights.shape[0]
    half, fields, _ = mine.shape
    rows[:half] = mine[...]
    rows[half:] = other[...]
    total[...] = jnp.zeros_like(total)

    def step(g, carry):
        base = g * UNROLL
        pltpu.make_async_copy(
            weights_hbm.at[pl.ds(base, UNROLL)], weights.at[pl.ds(base, UNROLL)], sems.at[g]
        ).wait()
        products = []
        for u in range(0, UNROLL, 2):
            both = lax.dot_general(
                jnp.concatenate([rows[slot_ref[base + u]], rows[slot_ref[base + u + 1]]], 0),
                weights[pl.ds(base + u, 2)].reshape(2 * LANES, LANES),
                (((1,), (1,)), ((), ())),
                preferred_element_type=f32,
            )
            products += [both[:fields, :LANES], both[fields:, LANES:]]
        for u in range(UNROLL):
            total[patch_ref[base + u]] += products[u]
        return carry

    lax.fori_loop(0, blocks // UNROLL, step, 0)
    fetch.wait()
    for p in range(span // LANES):
        part = slice(p * LANES, (p + 1) * LANES)
        exchange = total[p]
        air_ref[:, part] = exchange
        bottom[:, 0, part] += COUPLE * exchange[:tracers]
    store = pltpu.make_async_copy(bottom, out_hbm.at[:, pl.ds(0, 8), :], sem)
    store.start()
    store.wait()


def backward(slot, patch, mine, other, weights, advected):
    tracers, levels, span = advected.shape
    half, fields, lanes = mine.shape
    return pl.pallas_call(
        backward_kernel,
        out_shape=(
            jax.ShapeDtypeStruct((fields, span), f32),
            jax.ShapeDtypeStruct(advected.shape, f32),
        ),
        in_specs=[SMEM, SMEM, VMEM, VMEM, HBM, HBM],
        out_specs=(VMEM, HBM),
        input_output_aliases={5: 1},
        scratch_shapes=[
            pltpu.VMEM((2 * half, fields, lanes), bf16),
            pltpu.VMEM((span // lanes, fields, lanes), f32),
            pltpu.VMEM((tracers, 8, span), f32),
            pltpu.SemaphoreType.DMA,
            pltpu.VMEM(weights.shape, bf16),
            pltpu.SemaphoreType.DMA((weights.shape[0] // UNROLL,)),
        ],
        compiler_params=params(52 * 1024 * 1024),
        name="rows_to_columns",
    )(slot, patch, mine, other, weights, advected)


def per_device(
    tracers,
    courant,
    air_surface,
    block_weights,
    block_dest,
    block_row,
    block_patch,
    ocean_state,
    exchange_rate,
    sea_mask,
):
    tiles, subs = lax.axis_size("tile"), lax.axis_size("sub")
    devices = tiles * subs
    my_tile, my_sub = lax.axis_index("tile"), lax.axis_index("sub")
    my_index = my_tile * subs + my_sub
    blocks = block_weights.shape[0]
    fields, ocean_rows, lanes = ocean_state.shape
    flat = ("tile", "sub")
    tracers_t = jnp.transpose(tracers, (1, 0, 2))
    pack_a, pack_b = pack(tracers_t, courant)
    msg_b = lax.ppermute(
        pack_b, flat, [(i, (i + 1 if i % 2 else i - 1) % devices) for i in range(devices)]
    )
    msg_a = lax.ppermute(pack_a, flat, [(i, i ^ 1) for i in range(devices)])

    start = my_index * blocks
    dest = lax.dynamic_slice(block_dest.reshape(-1), (start,), (blocks,))
    row = lax.dynamic_slice(block_row, (start,), (blocks,))
    chunk_of = ((dest // subs) ^ my_tile) + tiles * ((dest % subs + subs - my_sub) % subs)
    slot = chunk_of * ocean_rows + row

    state = jnp.transpose(ocean_state, (1, 0, 2))
    sign = jnp.where(jnp.arange(fields) >= fields - 2, -1.0, 1.0).astype(f32)[:, None]
    fold = sign * ocean_state[:, -1, ::-1]
    beside = jnp.where(my_sub == subs - 1, ocean_state[:, 0], ocean_state[:, -1])

    send, keep = forward(
        slot, block_patch, tracers[0], courant, air_surface, msg_a, msg_b, beside,
        block_weights, devices * ocean_rows,
    )
    swap = [(0, 1), (1, 0)]
    got = lax.ppermute(send, "sub", swap)
    own, beside, *partial = merge(keep, got, state, fold, ocean_rows)
    across = lambda x, d: lax.ppermute(x, "tile", [(i, i ^ d) for i in range(tiles)])
    got = [across(x, d) for d, x in enumerate(partial, 1)]

    count = tracers.shape[1] // 2
    some, flag = advect_some(tracers_t, courant, msg_a, msg_b, 0, count, own)
    next_ocean, half = ocean(
        state, beside, exchange_rate, sea_mask, own, got, flag
    )

    first = [1, 2, 3] + list(range(tiles - 1, 5, -1))
    arrived = {d: across(half, d) for d in first}
    for d, behind in ((5, 1), (4, 2)):
        ready, _ = lax.optimization_barrier((half, arrived[behind]))
        arrived[d] = across(ready, d)
    advected, flag = advect_some(
        tracers_t, courant, msg_a, msg_b, count, tracers.shape[1] - count, half, some
    )
    mine = gather_rows([half] + [arrived[d] for d in range(1, tiles)], flag)
    other = lax.ppermute(mine, "sub", swap)
    air_exchange, out_t = backward(slot, block_patch, mine, other, block_weights, advected)
    return jnp.transpose(out_t, (1, 0, 2)), jnp.transpose(next_ocean, (1, 0, 2)), air_exchange


def solution(mesh):
    placed = (
        P("members", None, ("tile", "sub")),
        P("members", ("tile", "sub")),
        P("members", ("tile", "sub")),
        P(("tile", "sub"), None, None),
        P(),
        P(),
        P(("tile", "sub")),
        P("members", "sub", "tile"),
        P("sub", "tile"),
        P("sub", "tile"),
    )
    return jax.shard_map(
        per_device,
        mesh=mesh,
        in_specs=placed,
        out_specs=(
            P("members", None, ("tile", "sub")),
            P("members", "sub", "tile"),
            P("members", ("tile", "sub")),
        ),
        check_vma=False,
    )
```

time: 93 us -> 65.7 us (0.71)
  waiting for transfers between devices: 17.7 us -> 5.95 us
  Pallas kernels: 34.4 us -> 27.1 us
  starting transfers between devices: 33.2 us -> 26.6 us
  local copies, waits for them, and re-layouts: 5.83 us -> 4.03 us
    ppermute x14, waiting for transfers between devices: 17.1 us -> 2.73 us  [per_device(): lax.ppermute(x, 'tile', [(i, i ^ d) for i in range(tiles)])]
    pallas_call x5 -> x6, Pallas kernels: 34.1 us -> 26.7 us  [the longest x2 11.7 us: advect_some(): pl.pallas_call(functools.partial(advect_kernel, tracers, levels, first, g...]
    ppermute x5 -> x1, starting transfers between devices: 6.99 us -> 0.01 us  [per_device(): got = lax.ppermute(send, 'sub', swap)]
    ppermute x5 -> x1, waiting for transfers between devices: 0.01 us -> 1.98 us  [per_device(): got = lax.ppermute(send, 'sub', swap)]
    unnamed x34 -> x21, local copies, waits for them, and re-layouts: 5.68 us -> 3.9 us
    ppermute x1, waiting for transfers between devices: 0.01 us -> 1.2 us  [per_device(): other = lax.ppermute(mine, 'sub', swap)]
  transfers between devices with their start and end apart: 22 -> 18, of which waited for: 8 -> 4; matrix products, arithmetic and copies ran while one was open for 2% -> 4% of each run, Pallas kernels for 26% -> 18%
where the time goes in v2:
time: 65.7 us; the launch traced here: 65.4 us
  Pallas kernels  27.1 us (41%)
  starting transfers between devices  26.6 us (40%)
  waiting for transfers between devices  5.95 us (9%)
  local copies, waits for them, and re-layouts  4.03 us (6%)
  other arithmetic  0.85 us (1%)
  between operations  0.83 us (1%)
    ppermute x14, starting transfers between devices, per_device(): lax.ppermute(x, 'tile', [(i, i ^ d) for i in range(tiles)])  20.4 us
    pallas_call x2, Pallas kernels, advect_some(): pl.pallas_call(functools.partial(advect_kernel, tracers, levels, first, g...  11.7 us
    pallas_call x1, Pallas kernels, backward(): pl.pallas_call(backward_kernel, out_shape=(jax.ShapeDtypeStruct((fields,...  7.15 us
    pallas_call x1, Pallas kernels, forward(): pl.pallas_call(functools.partial(forward_kernel, (tracers, span, top)), o...  5.89 us
    ppermute x1, starting transfers between devices, per_device(): lax.ppermute(pack_b, flat, [(i, (i + 1 if i % 2 else i - 1) % devices) fo...  5.67 us
    unnamed x21, local copies, waits for them, and re-layouts  3.9 us
    ppermute x14, waiting for transfers between devices, per_device(): lax.ppermute(x, 'tile', [(i, i ^ d) for i in range(tiles)])  2.73 us
    pallas_call x1, Pallas kernels, pack(): pl.pallas_call(functools.partial(pack_kernel, tracers, levels), out_shape...  1.98 us
  transfers between devices with their start and end apart: 18, of which 4 were waited for; matrix products, arithmetic and copies ran while one was open for 4% of the time, Pallas kernels for 18%

profile of v2, /device:TPU:0, one launch (start us, length us, event | category | flops | bytes accessed | tf_op | source)
XLA Modules:
  0.0 65.4 jit_solution(6175059504246440452)
XLA Ops:
  0.6 0.0 copy-start
  0.6 0.0 copy-start.2
  0.7 0.0 copy-start.1
  0.7 0.0 copy-start.8
  0.7 0.0 copy-start.5
  0.7 2.0 %pack_edges.1 = (f32[64,128]{1,0:T(8,128)}, f32[64,128]{1,0:T(8,128)}) custom-call(f32[12,20,2048]{2,1,0:T(8,128)} %bitcast.13, f32[20,2048]{1,0:T(8,128)} %c_ref.3), custom_call_target="tpu_custom_call" | custom-call | tf_op jit(solution)/shard_map/pack_edges/pallas_call | solution.py:113
  2.7 0.5 collective-permute-start
  3.2 5.7 %collective-permute-start.1 = (f32[64,128]{1,0:T(8,128)}, f32[64,128]{1,0:T(8,128)S(1)}, u32[]{:S(2)}, u32[]{:S(2)}) collective-permute-start(f32[64,128]{1,0:T(8,128)} %get-tuple-element.27), channel_id=1, source_target_pairs={{0,15},{1,2},{2,1},{3,4},{4,3},{5,6},{6,5},{7,8},{8,7},{9,10},{10,... | collective-permute-start | bytes 98312 | tf_op jit(solution)/shard_map/ppermute | solution.py:539
  8.9 0.9 %copy.25 = f32[16,16,128]{2,0,1:T(8,128)S(1)} copy(f32[16,16,128]{2,1,0:T(8,128)} %param.17) | data formatting | bytes 262144 | tf_op args[7]
  9.8 0.0 copy-done
  9.9 0.8 %dynamic-slice_add_fusion.slot_ref = s32[256]{0:T(256)S(1)} fusion(s32[4096]{0:T(1024)} %param.15, s32[]{:T(128)S(6)} %select_n.38, s32[256]{0:T(256)S(1)} %bitcast.21, s32[]{:T(128)S(6)} %axis_index.25, s32[]{:T(128)S(6)} %axis_index.23), kind=kLoop, calls=%fused_computation.17 | loop fusion | flops 9472 | bytes 3084 | tf_op jit(solution)/shard_map/add | solution.py:548
  10.6 0.0 copy-done.1
  10.6 0.1 slice.10
  10.7 0.0 collective-permute-done.msg_a
  10.7 0.0 collective-permute-done.1.msg_b
  10.8 0.0 copy-done.2
  10.8 0.0 copy-done.8
  10.8 0.0 copy-done.5
  10.8 5.9 %blocks_to_rows.1 = (bf16[130,16,128]{2,1,0:T(8,128)(2,1)}, f32[128,16,128]{2,1,0:T(8,128)S(1)}) custom-call(s32[256]{0:T(256)S(1)} %dynamic-slice_add_fusion.slot_ref, s32[256]{0:T(256)S(1)} %copy-done.8, f32[12,2048]{1,0:T(8,128)S(1)} %bitcast.18, f32[20,2048]{1,0:T(8,128)S(1)} %copy-done.2, f32[4,2048]{1,0:T(4,128)S(1)} %copy-done.5, ...), custom_call_target="tpu_custom_call" | custom-call | tf_op jit(solution)/shard_map/blocks_to_rows/pallas_call | solution.py:195
  16.7 0.0 copy-start.3
  16.7 1.0 %copy-done.3 = f32[128,16,128]{2,1,0:T(8,128)} copy-done((f32[128,16,128]{2,1,0:T(8,128)}, f32[128,16,128]{2,1,0:T(8,128)S(1)}, u32[]{:S(2)}) %copy-start.3) | copy-done | bytes 1048600
  17.7 0.0 collective-permute-start.2
  17.7 0.1 rev.3
  17.7 0.1 bitcast_multiply_fusion.fold
  17.8 2.0 %collective-permute-done.2.got = bf16[130,16,128]{2,1,0:T(8,128)(2,1)S(1)} collective-permute-done((bf16[130,16,128]{2,1,0:T(8,128)(2,1)}, bf16[130,16,128]{2,1,0:T(8,128)(2,1)S(1)}, u32[]{:S(2)}, u32[]{:S(2)}) %collective-permute-start.2) | collective-permute-done | bytes 532512 | tf_op jit(solution)/shard_map/ppermute | solution.py:560
  19.8 1.2 %copy-done.4 = f32[128,16,128]{2,1,0:T(8,128)S(1)} copy-done((f32[128,16,128]{2,1,0:T(8,128)S(1)}, f32[128,16,128]{2,1,0:T(8,128)}, u32[]{:S(2)}) %copy-start.4) | copy-done | bytes 1048600
  21.0 0.2 merge_cores.1
  21.2 0.1 collective-permute-start.4
  21.3 2.2 %collective-permute-start.6 = (bf16[16,16,128]{2,1,0:T(8,128)(2,1)S(1)}, bf16[16,16,128]{2,1,0:T(8,128)(2,1)S(1)}, u32[]{:S(2)}, u32[]{:S(2)}) collective-permute-start(bf16[16,16,128]{2,1,0:T(8,128)(2,1)S(1)} %get-tuple-element.35), channel_id=1, source_target_pairs={{0,8},{2,10},{4,12},{6,14},{8,0},{10,2},{12,4},{14,6},{1,9},{3,11}... | collective-permute-start | bytes 196616 | tf_op jit(solution)/shard_map/ppermute | solution.py:562
  23.4 3.3 %collective-permute-start.3 = (bf16[20,16,128]{2,1,0:T(8,128)(2,1)S(1)}, bf16[20,16,128]{2,1,0:T(8,128)(2,1)S(1)}, u32[]{:S(2)}, u32[]{:S(2)}) collective-permute-start(bf16[20,16,128]{2,1,0:T(8,128)(2,1)S(1)} %get-tuple-element.32), channel_id=1, source_target_pairs={{0,2},{2,0},{4,6},{6,4},{8,10},{10,8},{12,14},{14,12},{1,3},{3,1},... | collective-permute-start | bytes 245768 | tf_op jit(solution)/shard_map/ppermute | solution.py:562
  26.8 0.0 collective-permute-start.5
  26.8 2.4 %collective-permute-start.9 = (bf16[20,16,128]{2,1,0:T(8,128)(2,1)S(1)}, bf16[20,16,128]{2,1,0:T(8,128)(2,1)S(1)}, u32[]{:S(2)}, u32[]{:S(2)}) collective-permute-start(bf16[20,16,128]{2,1,0:T(8,128)(2,1)S(1)} %get-tuple-element.38), channel_id=1, source_target_pairs={{0,14},{2,12},{4,10},{6,8},{8,6},{10,4},{12,2},{14,0},{1,15},{3,13... | collective-permute-start | bytes 245768 | tf_op jit(solution)/shard_map/ppermute | solution.py:562
  29.1 0.0 collective-permute-done.4.rest_1_
  29.1 1.5 %collective-permute-start.7 = (bf16[16,16,128]{2,1,0:T(8,128)(2,1)S(1)}, bf16[16,16,128]{2,1,0:T(8,128)(2,1)S(1)}, u32[]{:S(2)}, u32[]{:S(2)}) collective-permute-start(bf16[16,16,128]{2,1,0:T(8,128)(2,1)S(1)} %get-tuple-element.36), channel_id=1, source_target_pairs={{0,10},{2,8},{4,14},{6,12},{8,2},{10,0},{12,6},{14,4},{1,11},{3,9}... | collective-permute-start | bytes 196616 | tf_op jit(solution)/shard_map/ppermute | solution.py:562
  30.6 0.0 collective-permute-done.6.rest_3_
  30.6 1.5 %collective-permute-start.8 = (bf16[16,16,128]{2,1,0:T(8,128)(2,1)S(1)}, bf16[16,16,128]{2,1,0:T(8,128)(2,1)S(1)}, u32[]{:S(2)}, u32[]{:S(2)}) collective-permute-start(bf16[16,16,128]{2,1,0:T(8,128)(2,1)S(1)} %get-tuple-element.37), channel_id=1, source_target_pairs={{0,12},{2,14},{4,8},{6,10},{8,4},{10,6},{12,0},{14,2},{1,13},{3,15... | collective-permute-start | bytes 196616 | tf_op jit(solution)/shard_map/ppermute | solution.py:562
  32.1 5.8 %advect_levels.2 = (f32[12,20,2048]{2,1,0:T(8,128)}, f32[8,128]{1,0:T(8,128)S(1)}) custom-call(f32[12,20,2048]{2,1,0:T(8,128)S(1)} %bitcast.14, f32[20,2048]{1,0:T(8,128)S(1)} %copy-done.2, f32[64,128]{1,0:T(8,128)S(1)} %collective-permute-done.msg_a, f32[64,128]{1,0:T(8,128)S(1)} %collective-permute-done.1.msg_b, ...), custom_call_target="tpu_custom_call" | custom-call | flops 49152000 | bytes 1966080 | tf_op jit(solution)/shard_map/advect_levels/pallas_call | solution.py:410
  37.9 1.2 %collective-permute-done.7.rest_4_ = bf16[16,16,128]{2,1,0:T(8,128)(2,1)S(1)} collective-permute-done((bf16[16,16,128]{2,1,0:T(8,128)(2,1)S(1)}, bf16[16,16,128]{2,1,0:T(8,128)(2,1)S(1)}, u32[]{:S(2)}, u32[]{:S(2)}) %collective-permute-start.7) | collective-permute-done | bytes 65568 | tf_op jit(solution)/shard_map/ppermute | solution.py:562
  39.1 0.0 collective-permute-done.8.rest_5_
  39.1 0.0 collective-permute-done.3.rest_0_
  39.1 0.0 collective-permute-done.5.rest_2_
  39.1 0.0 collective-permute-done.9.rest_6_
  39.1 0.0 copy-done.6
  39.1 0.0 copy-done.7
  39.2 0.2 ocean_update.1
  39.4 1.6 %collective-permute-start.11 = (bf16[16,16,128]{2,1,0:T(8,128)(2,1)S(1)}, bf16[16,16,128]{2,1,0:T(8,128)(2,1)S(1)}, u32[]{:S(2)}, u32[]{:S(2)}) collective-permute-start(bf16[16,16,128]{2,1,0:T(8,128)(2,1)S(1)} %get-tuple-element.42.rest_0_.refs_0_), channel_id=1, source_target_pairs={{0,4},{2,6},{4,0},{6,2},{8,12},{10,14},{12,8},{14,10},{1,5},{3,7},... | collective-permute-start | bytes 196616 | tf_op jit(solution)/shard_map/ppermute | solution.py:562
  41.0 0.3 collective-permute-start.10
  41.3 1.8 %collective-permute-start.16 = (bf16[16,16,128]{2,1,0:T(8,128)(2,1)S(1)}, bf16[16,16,128]{2,1,0:T(8,128)(2,1)S(1)}, u32[]{:S(2)}, u32[]{:S(2)}) collective-permute-start(bf16[16,16,128]{2,1,0:T(8,128)(2,1)S(1)} %get-tuple-element.42.rest_0_.refs_0_), channel_id=1, source_target_pairs={{0,14},{2,12},{4,10},{6,8},{8,6},{10,4},{12,2},{14,0},{1,15},{3,13... | collective-permute-start | bytes 196616 | tf_op jit(solution)/shard_map/ppermute | solution.py:562
  43.1 3.2 %collective-permute-start.15 = (bf16[16,16,128]{2,1,0:T(8,128)(2,1)S(1)}, bf16[16,16,128]{2,1,0:T(8,128)(2,1)S(1)}, u32[]{:S(2)}, u32[]{:S(2)}) collective-permute-start(bf16[16,16,128]{2,1,0:T(8,128)(2,1)S(1)} %get-tuple-element.42.rest_0_.refs_0_), channel_id=1, source_target_pairs={{0,12},{2,14},{4,8},{6,10},{8,4},{10,6},{12,0},{14,2},{1,13},{3,15... | collective-permute-start | bytes 196616 | tf_op jit(solution)/shard_map/ppermute | solution.py:562
  46.3 0.0 collective-permute-start.12
  46.3 0.0 collective-permute-done.11.refs_2_
  46.3 2.1 %collective-permute-start.13 = (bf16[16,16,128]{2,1,0:T(8,128)(2,1)S(1)}, bf16[16,16,128]{2,1,0:T(8,128)(2,1)S(1)}, u32[]{:S(2)}, u32[]{:S(2)}) collective-permute-start(bf16[16,16,128]{2,1,0:T(8,128)(2,1)S(1)} %get-tuple-element.42.rest_0_.refs_0_), channel_id=1, source_target_pairs={{0,8},{2,10},{4,12},{6,14},{8,0},{10,2},{12,4},{14,6},{1,9},{3,11}... | collective-permute-start | bytes 196616 | tf_op jit(solution)/shard_map/ppermute | solution.py:562
  48.4 0.0 collective-permute-done.10.refs_1_
  48.4 0.6 collective-permute-start.14
  48.9 5.8 %advect_levels.3 = (f32[12,20,2048]{2,1,0:T(8,128)}, f32[8,128]{1,0:T(8,128)S(1)}) custom-call(f32[12,20,2048]{2,1,0:T(8,128)S(1)} %bitcast.15, f32[20,2048]{1,0:T(8,128)S(1)} %copy-done.2, f32[64,128]{1,0:T(8,128)S(1)} %collective-permute-done.msg_a, f32[64,128]{1,0:T(8,128)S(1)} %collective-permute-done.1.msg_b, ...), custom_call_target="tpu_custom_call", output_to_operand_aliasing={{0}: (5, {})} | custom-call | flops 49152000 | bytes 1966080 | tf_op jit(solution)/shard_map/advect_levels/pallas_call | solution.py:410
  54.8 0.0 collective-permute-done.16.refs_7_
  54.8 0.0 collective-permute-done.15.refs_6_
  54.8 0.0 collective-permute-done.12.refs_3_
  54.8 0.0 collective-permute-done.13.refs_4_
  54.8 1.5 %collective-permute-done.14.refs_5_ = bf16[16,16,128]{2,1,0:T(8,128)(2,1)S(1)} collective-permute-done((bf16[16,16,128]{2,1,0:T(8,128)(2,1)S(1)}, bf16[16,16,128]{2,1,0:T(8,128)(2,1)S(1)}, u32[]{:S(2)}, u32[]{:S(2)}) %collective-permute-start.14) | collective-permute-done | bytes 65568 | tf_op jit(solution)/shard_map/ppermute | solution.py:562
  56.3 0.1 collective-permute-start.17
  56.4 0.7 %copy.19 = f32[16,16,128]{2,1,0:T(8,128)} copy(f32[16,16,128]{2,0,1:T(8,128)S(1)} %bitcast.19) | data formatting | bytes 262144
  57.1 1.2 %collective-permute-done.17.other = bf16[128,16,128]{2,1,0:T(8,128)(2,1)S(1)} collective-permute-done((bf16[128,16,128]{2,1,0:T(8,128)(2,1)S(1)}, bf16[128,16,128]{2,1,0:T(8,128)(2,1)S(1)}, u32[]{:S(2)}, u32[]{:S(2)}) %collective-permute-start.17) | collective-permute-done | bytes 524320 | tf_op jit(solution)/shard_map/ppermute | solution.py:580
  58.3 7.1 %rows_to_columns.1 = (f32[16,2048]{1,0:T(8,128)}, f32[12,20,2048]{2,1,0:T(8,128)}) custom-call(s32[256]{0:T(256)S(1)} %dynamic-slice_add_fusion.slot_ref, s32[256]{0:T(256)S(1)} %copy-done.8, bf16[128,16,128]{2,1,0:T(8,128)(2,1)S(1)} %gather_rows.1.mine, bf16[128,16,128]{2,1,0:T(8,128)(2,1)S(1)} %collective-permute-done.17.other, ...), custom_call_target="tpu_custom_call", output_to_operand_aliasing={{1}: (5, {})} | custom-call | tf_op jit(solution)/shard_map/rows_to_columns/pallas_call | solution.py:496
  (8 shorter events, 0.1 us)
Async XLA Ops:
  0.6 9.2 %copy-start = (s32[4096,1]{0,1:T(1,128)S(1)}, s32[4096,1]{0,1:T(1,128)}, u32[]{:S(2)}) copy-start(s32[4096,1]{0,1:T(1,128)} %param.14) | copy-start | bytes 49156
  0.6 10.1 %copy-start.2 = (f32[20,2048]{1,0:T(8,128)S(1)}, f32[20,2048]{1,0:T(8,128)}, u32[]{:S(2)}) copy-start(f32[20,2048]{1,0:T(8,128)} %c_ref.3) | copy-start | bytes 491524
  0.7 10.0 %copy-start.1 = (f32[20,12,2048]{2,0,1:T(8,128)S(1)}, f32[20,12,2048]{2,0,1:T(8,128)}, u32[]{:S(2)}) copy-start(f32[20,12,2048]{2,0,1:T(8,128)} %param.10) | copy-start | bytes 5898244
  0.7 10.1 %copy-start.8 = (s32[256]{0:T(256)S(1)}, s32[256]{0:T(256)}, u32[]{:S(2)}) copy-start(s32[256]{0:T(256)} %patch_ref.3) | copy-start | bytes 3076
  0.7 10.1 %copy-start.5 = (f32[4,2048]{1,0:T(4,128)S(1)}, f32[4,2048]{1,0:T(4,128)}, u32[]{:S(2)}) copy-start(f32[4,2048]{1,0:T(4,128)} %air.1) | copy-start | bytes 98308
  2.7 8.0 %collective-permute-start = (f32[64,128]{1,0:T(8,128)}, f32[64,128]{1,0:T(8,128)S(1)}, u32[]{:S(2)}, u32[]{:S(2)}) collective-permute-start(f32[64,128]{1,0:T(8,128)} %get-tuple-element.26), channel_id=1, source_target_pairs={{0,1},{1,0},{2,3},{3,2},{4,5},{5,4},{6,7},{7,6},{8,9},{9,8},{10,11... | collective-permute-start | bytes 98312 | tf_op jit(solution)/shard_map/ppermute | solution.py:542
  3.2 7.6 %collective-permute-start.1 = (f32[64,128]{1,0:T(8,128)}, f32[64,128]{1,0:T(8,128)S(1)}, u32[]{:S(2)}, u32[]{:S(2)}) collective-permute-start(f32[64,128]{1,0:T(8,128)} %get-tuple-element.27), channel_id=1, source_target_pairs={{0,15},{1,2},{2,1},{3,4},{4,3},{5,6},{6,5},{7,8},{8,7},{9,10},{10,... | collective-permute-start | bytes 98312 | tf_op jit(solution)/shard_map/ppermute | solution.py:539
  16.7 1.0 %copy-start.3 = (f32[128,16,128]{2,1,0:T(8,128)}, f32[128,16,128]{2,1,0:T(8,128)S(1)}, u32[]{:S(2)}) copy-start(f32[128,16,128]{2,1,0:T(8,128)S(1)} %get-tuple-element.28.keep) | copy-start | bytes 3145732
  17.7 21.5 %copy-start.6 = (f32[16,128]{1,0:T(8,128)S(1)}, f32[16,128]{1,0:T(8,128)}, u32[]{:S(2)}) copy-start(f32[16,128]{1,0:T(8,128)} %rate.1) | copy-start | bytes 24580
  17.7 21.5 %copy-start.7 = (s32[16,128]{1,0:T(8,128)S(1)}, s32[16,128]{1,0:T(8,128)}, u32[]{:S(2)}) copy-start(s32[16,128]{1,0:T(8,128)} %wet.1) | copy-start | bytes 24580
  17.7 2.1 %collective-permute-start.2 = (bf16[130,16,128]{2,1,0:T(8,128)(2,1)}, bf16[130,16,128]{2,1,0:T(8,128)(2,1)S(1)}, u32[]{:S(2)}, u32[]{:S(2)}) collective-permute-start(bf16[130,16,128]{2,1,0:T(8,128)(2,1)} %get-tuple-element.29), channel_id=1, source_target_pairs={{0,1},{1,0},{2,3},{3,2},{4,5},{5,4},{6,7},{7,6},{8,9},{9,8},{10,11... | collective-permute-start | bytes 1597448 | tf_op jit(solution)/shard_map/ppermute | solution.py:560
  19.8 1.2 %copy-start.4 = (f32[128,16,128]{2,1,0:T(8,128)S(1)}, f32[128,16,128]{2,1,0:T(8,128)}, u32[]{:S(2)}) copy-start(f32[128,16,128]{2,1,0:T(8,128)} %copy-done.3) | copy-start | bytes 3145732
  21.2 7.9 %collective-permute-start.4 = (bf16[16,16,128]{2,1,0:T(8,128)(2,1)S(1)}, bf16[16,16,128]{2,1,0:T(8,128)(2,1)S(1)}, u32[]{:S(2)}, u32[]{:S(2)}) collective-permute-start(bf16[16,16,128]{2,1,0:T(8,128)(2,1)S(1)} %get-tuple-element.33), channel_id=1, source_target_pairs={{0,4},{2,6},{4,0},{6,2},{8,12},{10,14},{12,8},{14,10},{1,5},{3,7},... | collective-permute-start | bytes 196616 | tf_op jit(solution)/shard_map/ppermute | solution.py:562
  21.3 9.3 %collective-permute-start.6 = (bf16[16,16,128]{2,1,0:T(8,128)(2,1)S(1)}, bf16[16,16,128]{2,1,0:T(8,128)(2,1)S(1)}, u32[]{:S(2)}, u32[]{:S(2)}) collective-permute-start(bf16[16,16,128]{2,1,0:T(8,128)(2,1)S(1)} %get-tuple-element.35), channel_id=1, source_target_pairs={{0,8},{2,10},{4,12},{6,14},{8,0},{10,2},{12,4},{14,6},{1,9},{3,11}... | collective-permute-start | bytes 196616 | tf_op jit(solution)/shard_map/ppermute | solution.py:562
  23.4 15.7 %collective-permute-start.3 = (bf16[20,16,128]{2,1,0:T(8,128)(2,1)S(1)}, bf16[20,16,128]{2,1,0:T(8,128)(2,1)S(1)}, u32[]{:S(2)}, u32[]{:S(2)}) collective-permute-start(bf16[20,16,128]{2,1,0:T(8,128)(2,1)S(1)} %get-tuple-element.32), channel_id=1, source_target_pairs={{0,2},{2,0},{4,6},{6,4},{8,10},{10,8},{12,14},{14,12},{1,3},{3,1},... | collective-permute-start | bytes 245768 | tf_op jit(solution)/shard_map/ppermute | solution.py:562
  26.8 12.4 %collective-permute-start.5 = (bf16[20,16,128]{2,1,0:T(8,128)(2,1)S(1)}, bf16[20,16,128]{2,1,0:T(8,128)(2,1)S(1)}, u32[]{:S(2)}, u32[]{:S(2)}) collective-permute-start(bf16[20,16,128]{2,1,0:T(8,128)(2,1)S(1)} %get-tuple-element.34), channel_id=1, source_target_pairs={{0,6},{2,4},{4,2},{6,0},{8,14},{10,12},{12,10},{14,8},{1,7},{3,5},... | collective-permute-start | bytes 245768 | tf_op jit(solution)/shard_map/ppermute | solution.py:562
  26.8 12.4 %collective-permute-start.9 = (bf16[20,16,128]{2,1,0:T(8,128)(2,1)S(1)}, bf16[20,16,128]{2,1,0:T(8,128)(2,1)S(1)}, u32[]{:S(2)}, u32[]{:S(2)}) collective-permute-start(bf16[20,16,128]{2,1,0:T(8,128)(2,1)S(1)} %get-tuple-element.38), channel_id=1, source_target_pairs={{0,14},{2,12},{4,10},{6,8},{8,6},{10,4},{12,2},{14,0},{1,15},{3,13... | collective-permute-start | bytes 245768 | tf_op jit(solution)/shard_map/ppermute | solution.py:562
  29.1 10.0 %collective-permute-start.7 = (bf16[16,16,128]{2,1,0:T(8,128)(2,1)S(1)}, bf16[16,16,128]{2,1,0:T(8,128)(2,1)S(1)}, u32[]{:S(2)}, u32[]{:S(2)}) collective-permute-start(bf16[16,16,128]{2,1,0:T(8,128)(2,1)S(1)} %get-tuple-element.36), channel_id=1, source_target_pairs={{0,10},{2,8},{4,14},{6,12},{8,2},{10,0},{12,6},{14,4},{1,11},{3,9}... | collective-permute-start | bytes 196616 | tf_op jit(solution)/shard_map/ppermute | solution.py:562
  30.6 8.5 %collective-permute-start.8 = (bf16[16,16,128]{2,1,0:T(8,128)(2,1)S(1)}, bf16[16,16,128]{2,1,0:T(8,128)(2,1)S(1)}, u32[]{:S(2)}, u32[]{:S(2)}) collective-permute-start(bf16[16,16,128]{2,1,0:T(8,128)(2,1)S(1)} %get-tuple-element.37), channel_id=1, source_target_pairs={{0,12},{2,14},{4,8},{6,10},{8,4},{10,6},{12,0},{14,2},{1,13},{3,15... | collective-permute-start | bytes 196616 | tf_op jit(solution)/shard_map/ppermute | solution.py:562
  39.4 6.9 %collective-permute-start.11 = (bf16[16,16,128]{2,1,0:T(8,128)(2,1)S(1)}, bf16[16,16,128]{2,1,0:T(8,128)(2,1)S(1)}, u32[]{:S(2)}, u32[]{:S(2)}) collective-permute-start(bf16[16,16,128]{2,1,0:T(8,128)(2,1)S(1)} %get-tuple-element.42.rest_0_.refs_0_), channel_id=1, source_target_pairs={{0,4},{2,6},{4,0},{6,2},{8,12},{10,14},{12,8},{14,10},{1,5},{3,7},... | collective-permute-start | bytes 196616 | tf_op jit(solution)/shard_map/ppermute | solution.py:562
  41.0 7.4 %collective-permute-start.10 = (bf16[16,16,128]{2,1,0:T(8,128)(2,1)S(1)}, bf16[16,16,128]{2,1,0:T(8,128)(2,1)S(1)}, u32[]{:S(2)}, u32[]{:S(2)}) collective-permute-start(bf16[16,16,128]{2,1,0:T(8,128)(2,1)S(1)} %get-tuple-element.42.rest_0_.refs_0_), channel_id=1, source_target_pairs={{0,2},{2,0},{4,6},{6,4},{8,10},{10,8},{12,14},{14,12},{1,3},{3,1},... | collective-permute-start | bytes 196616 | tf_op jit(solution)/shard_map/ppermute | solution.py:562
  41.3 13.5 %collective-permute-start.16 = (bf16[16,16,128]{2,1,0:T(8,128)(2,1)S(1)}, bf16[16,16,128]{2,1,0:T(8,128)(2,1)S(1)}, u32[]{:S(2)}, u32[]{:S(2)}) collective-permute-start(bf16[16,16,128]{2,1,0:T(8,128)(2,1)S(1)} %get-tuple-element.42.rest_0_.refs_0_), channel_id=1, source_target_pairs={{0,14},{2,12},{4,10},{6,8},{8,6},{10,4},{12,2},{14,0},{1,15},{3,13... | collective-permute-start | bytes 196616 | tf_op jit(solution)/shard_map/ppermute | solution.py:562
  43.1 11.7 %collective-permute-start.15 = (bf16[16,16,128]{2,1,0:T(8,128)(2,1)S(1)}, bf16[16,16,128]{2,1,0:T(8,128)(2,1)S(1)}, u32[]{:S(2)}, u32[]{:S(2)}) collective-permute-start(bf16[16,16,128]{2,1,0:T(8,128)(2,1)S(1)} %get-tuple-element.42.rest_0_.refs_0_), channel_id=1, source_target_pairs={{0,12},{2,14},{4,8},{6,10},{8,4},{10,6},{12,0},{14,2},{1,13},{3,15... | collective-permute-start | bytes 196616 | tf_op jit(solution)/shard_map/ppermute | solution.py:562
  46.3 8.5 %collective-permute-start.12 = (bf16[16,16,128]{2,1,0:T(8,128)(2,1)S(1)}, bf16[16,16,128]{2,1,0:T(8,128)(2,1)S(1)}, u32[]{:S(2)}, u32[]{:S(2)}) collective-permute-start(bf16[16,16,128]{2,1,0:T(8,128)(2,1)S(1)} %get-tuple-element.42.rest_0_.refs_0_), channel_id=1, source_target_pairs={{0,6},{2,4},{4,2},{6,0},{8,14},{10,12},{12,10},{14,8},{1,7},{3,5},... | collective-permute-start | bytes 196616 | tf_op jit(solution)/shard_map/ppermute | solution.py:562
  46.3 8.5 %collective-permute-start.13 = (bf16[16,16,128]{2,1,0:T(8,128)(2,1)S(1)}, bf16[16,16,128]{2,1,0:T(8,128)(2,1)S(1)}, u32[]{:S(2)}, u32[]{:S(2)}) collective-permute-start(bf16[16,16,128]{2,1,0:T(8,128)(2,1)S(1)} %get-tuple-element.42.rest_0_.refs_0_), channel_id=1, source_target_pairs={{0,8},{2,10},{4,12},{6,14},{8,0},{10,2},{12,4},{14,6},{1,9},{3,11}... | collective-permute-start | bytes 196616 | tf_op jit(solution)/shard_map/ppermute | solution.py:562
  48.4 7.9 %collective-permute-start.14 = (bf16[16,16,128]{2,1,0:T(8,128)(2,1)S(1)}, bf16[16,16,128]{2,1,0:T(8,128)(2,1)S(1)}, u32[]{:S(2)}, u32[]{:S(2)}) collective-permute-start(bf16[16,16,128]{2,1,0:T(8,128)(2,1)S(1)} %get-tuple-element.42.rest_0_.refs_0_), channel_id=1, source_target_pairs={{0,10},{2,8},{4,14},{6,12},{8,2},{10,0},{12,6},{14,4},{1,11},{3,9}... | collective-permute-start | bytes 196616 | tf_op jit(solution)/shard_map/ppermute | solution.py:562
  56.3 2.0 %collective-permute-start.17 = (bf16[128,16,128]{2,1,0:T(8,128)(2,1)S(1)}, bf16[128,16,128]{2,1,0:T(8,128)(2,1)S(1)}, u32[]{:S(2)}, u32[]{:S(2)}) collective-permute-start(bf16[128,16,128]{2,1,0:T(8,128)(2,1)S(1)} %gather_rows.1.mine), channel_id=1, source_target_pairs={{0,1},{1,0},{2,3},{3,2},{4,5},{5,4},{6,7},{7,6},{8,9},{9,8},{10,11... | collective-permute-start | bytes 1572872 | tf_op jit(solution)/shard_map/ppermute | solution.py:580

commit v3 on v2

--- a/solution.py
+++ b/solution.py
@@ -14,6 +14,7 @@
 EDGE = 16
 GROUPS = LANES // EDGE
 UNROLL = 64
+SPLIT = (6, 2, 4)
 
 VMEM = pl.BlockSpec(memory_space=pltpu.VMEM)
 SMEM = pl.BlockSpec(memory_space=pltpu.SMEM)
@@ -127,25 +128,42 @@
     )(tracers_t, courant)
 
 
+def slot_kernel(chunk, dest_ref, row_ref, _, slot_ref, back_ref):
+    tile, sub, tiles, subs = place()
+    count = slot_ref.shape[0]
+    mine = pl.ds((tile * subs + sub) * count, count)
+    dest = dest_ref[mine, :]
+    apart = (dest // subs) ^ tile
+    core = (dest % subs + subs - sub) % subs * tiles
+    row = row_ref[mine, :]
+    slot_ref[...] = (core + apart) * chunk + row
+    back_ref[...] = (core + apart % 2 * (tiles // 2) + apart // 2) * chunk + row
+
+
+def find_slots(dest, row, weights, chunk):
+    blocks = weights.shape[0]
+    whole = (dest.size // LANES, LANES)
+    return pl.pallas_call(
+        functools.partial(slot_kernel, chunk),
+        out_shape=(jax.ShapeDtypeStruct((blocks // LANES, LANES), jnp.int32),) * 2,
+        in_specs=[VMEM, VMEM, VMEM],
+        out_specs=(VMEM, VMEM),
+        compiler_params=params(28 * 1024 * 1024),
+        name="find_slots",
+    )(dest.reshape(whole), row.reshape(whole), weights)
+
+
 def high_low(x):
     high = x.astype(bf16)
     return high, (x - high.astype(f32)).astype(bf16)
 
 
 def forward_kernel(
-    dims, slot_ref, patch_ref, level0, courant0, air, msg_a, msg_b, beside,
-    weights_hbm, send_ref, keep_hbm, surface, total, weights, sems, keep_sem,
+    dims, slot_ref, patch_ref, level0, courant0, air, msg_a, msg_b, state, weights,
+    send_ref, keep_ref, surface, total,
 ):
     tracers, span, top = dims
     blocks = weights.shape[0]
-    copies = [
-        pltpu.make_async_copy(
-            weights_hbm.at[pl.ds(i, UNROLL)], weights.at[pl.ds(i, UNROLL)], sems.at[i // UNROLL]
-        )
-        for i in range(0, blocks, UNROLL)
-    ]
-    for copy in copies:
-        copy.start()
     even = is_even()
     a, b = msg_a[top : top + tracers + 1, :], msg_b[top : top + tracers + 1, :]
     left, right = jnp.where(even, b, a), jnp.where(even, a, b)
@@ -161,9 +179,6 @@
 
     def step(g, carry):
         base = g * UNROLL
-        pltpu.make_async_copy(
-            weights_hbm.at[pl.ds(base, UNROLL)], weights.at[pl.ds(base, UNROLL)], sems.at[g]
-        ).wait()
         products = []
         for u in range(0, UNROLL, 2):
             first, second = surface[patch_ref[base + u]], surface[patch_ref[base + u + 1]]
@@ -174,19 +189,19 @@
             both = jnp.dot(rows, pair, preferred_element_type=f32)
             products += [both[:height], both[height:]]
         for u in range(UNROLL):
-            total[slot_ref[base + u]] += products[u]
+            total[slot_ref[(base + u) // LANES, (base + u) % LANES]] += products[u]
         return carry
 
     lax.fori_loop(0, blocks // UNROLL, step, 0)
     half = total.shape[0] // 2
-    keep = pltpu.make_async_copy(total.at[pl.ds(0, half)], keep_hbm, keep_sem)
-    keep.start()
+    keep_ref[...] = total[:half]
     send_ref[:half] = total[half:].astype(bf16)
-    send_ref[half], send_ref[half + 1] = high_low(beside[...])
-    keep.wait()
-
-
-def forward(slot, patch, level0, courant, air, msg_a, msg_b, beside, weights, rows):
+    _, sub, _, subs = place()
+    beside = jnp.where(sub == subs - 1, state[0], state[state.shape[0] - 1])
+    send_ref[half], send_ref[half + 1] = high_low(beside)
+
+
+def forward(slot, patch, level0, courant, air, msg_a, msg_b, state, weights, rows):
     tracers, span = level0.shape
     levels = courant.shape[0]
     fields = tracers + air.shape[0]
@@ -198,32 +213,38 @@
             jax.ShapeDtypeStruct((rows // 2 + 2, fields, LANES), bf16),
             jax.ShapeDtypeStruct((rows // 2, fields, LANES), f32),
         ),
-        in_specs=[SMEM] * 2 + [VMEM] * 6 + [HBM],
-        out_specs=(VMEM, HBM),
+        in_specs=[SMEM] * 2 + [VMEM] * 7,
+        out_specs=(VMEM, VMEM),
         scratch_shapes=[
             pltpu.VMEM((span // LANES, fields, LANES), bf16),
             pltpu.VMEM((rows, fields, LANES), f32),
-            pltpu.VMEM(weights.shape, bf16),
-            pltpu.SemaphoreType.DMA((weights.shape[0] // UNROLL,)),
-            pltpu.SemaphoreType.DMA,
         ],
-        compiler_params=params(52 * 1024 * 1024),
+        compiler_params=params(28 * 1024 * 1024),
         name="blocks_to_rows",
-    )(slot, patch, level0, courant, air, msg_a, msg_b, beside, weights)
+    )(slot, patch, level0, courant, air, msg_a, msg_b, state, weights)
 
 
 def with_edges(d):
     return d & (d + 1) == 0
 
 
-def merge_kernel(chunk, keep, got, state, fold, own_ref, beside_ref, *outs):
+def merge_kernel(chunk, keep, got, state, own_ref, beside_ref, *outs):
     rows, fields, lanes = state.shape
     lane = lax.broadcasted_iota(jnp.int32, (fields, lanes), 1)
     edges = jnp.zeros((fields, lanes), f32)
     for r in range(rows):
         edges = jnp.where(lane == r, lane_roll(state[r], r + 1), edges)
         edges = jnp.where(lane == rows + r, lane_roll(state[r], rows + r), edges)
-    more = high_low(edges) + high_low(fold[...])
+    sign = jnp.where(lax.broadcasted_iota(jnp.int32, (fields, lanes), 0) < fields - 2, 1.0, -1.0)
+    mirror = lax.broadcasted_iota(jnp.int32, (lanes, lanes), 0) + lax.broadcasted_iota(
+        jnp.int32, (lanes, lanes), 1
+    )
+    mirror = jnp.where(mirror == lanes - 1, 1.0, 0.0).astype(bf16)
+    fold = [
+        (jnp.dot(part, mirror, preferred_element_type=f32) * sign).astype(bf16)
+        for part in high_low(state[rows - 1])
+    ]
+    more = [*high_low(edges), *fold]
     own_ref[...] = keep[:chunk] + got[:chunk].astype(f32)
     for d, out in enumerate(outs, 1):
         part = slice(d * chunk, (d + 1) * chunk)
@@ -235,7 +256,7 @@
     beside_ref[...] = got[last].astype(f32) + got[last + 1].astype(f32)
 
 
-def merge(keep, got, state, fold, chunk):
+def merge(keep, got, state, chunk):
     rows, fields, lanes = keep.shape
     count = rows // chunk
     return pl.pallas_call(
@@ -248,11 +269,11 @@
             jax.ShapeDtypeStruct((chunk + 4 * with_edges(d), fields, lanes), bf16)
             for d in range(1, count)
         ),
-        in_specs=[VMEM] * 4,
+        in_specs=[VMEM] * 3,
         out_specs=(VMEM,) * (count + 1),
         compiler_params=params((10 if count < 16 else 24) * 1024 * 1024),
         name="merge_cores",
-    )(keep, got, state, fold)
+    )(keep, got, state)
 
 
 def ocean_kernel(count, state, beside, rate, wet, own, *rest):
@@ -440,35 +461,25 @@
 
 
 def backward_kernel(
-    slot_ref, patch_ref, mine, other, weights_hbm, advected_hbm, air_ref, out_hbm,
-    rows, total, bottom, sem, weights, sems,
+    slot_ref, patch_ref, even, odd, even_other, odd_other, weights, advected_hbm, air_hbm, out_hbm,
+    rows, total, bottom, air, sem, air_sem,
 ):
-    copies = [
-        pltpu.make_async_copy(
-            weights_hbm.at[pl.ds(i, UNROLL)], weights.at[pl.ds(i, UNROLL)], sems.at[i // UNROLL]
-        )
-        for i in range(0, weights.shape[0], UNROLL)
-    ]
-    for copy in copies:
-        copy.start()
     fetch = pltpu.make_async_copy(advected_hbm.at[:, pl.ds(0, 8), :], bottom, sem)
     fetch.start()
     tracers, _, span = bottom.shape
     blocks = weights.shape[0]
-    half, fields, _ = mine.shape
-    rows[:half] = mine[...]
-    rows[half:] = other[...]
+    part, fields, _ = even.shape
+    for i, some in enumerate((even, odd, even_other, odd_other)):
+        rows[i * part : (i + 1) * part] = some[...]
     total[...] = jnp.zeros_like(total)
+    slot_of = lambda b: slot_ref[b // LANES, b % LANES]
 
     def step(g, carry):
         base = g * UNROLL
-        pltpu.make_async_copy(
-            weights_hbm.at[pl.ds(base, UNROLL)], weights.at[pl.ds(base, UNROLL)], sems.at[g]
-        ).wait()
         products = []
         for u in range(0, UNROLL, 2):
             both = lax.dot_general(
-                jnp.concatenate([rows[slot_ref[base + u]], rows[slot_ref[base + u + 1]]], 0),
+                jnp.concatenate([rows[slot_of(base + u)], rows[slot_of(base + u + 1)]], 0),
                 weights[pl.ds(base + u, 2)].reshape(2 * LANES, LANES),
                 (((1,), (1,)), ((), ())),
                 preferred_element_type=f32,
@@ -483,36 +494,41 @@
     for p in range(span // LANES):
         part = slice(p * LANES, (p + 1) * LANES)
         exchange = total[p]
-        air_ref[:, part] = exchange
+        air[:, part] = exchange
         bottom[:, 0, part] += COUPLE * exchange[:tracers]
-    store = pltpu.make_async_copy(bottom, out_hbm.at[:, pl.ds(0, 8), :], sem)
-    store.start()
-    store.wait()
-
-
-def backward(slot, patch, mine, other, weights, advected):
+    stores = (
+        pltpu.make_async_copy(bottom, out_hbm.at[:, pl.ds(0, 8), :], sem),
+        pltpu.make_async_copy(air, air_hbm, air_sem),
+    )
+    for store in stores:
+        store.start()
+    for store in stores:
+        store.wait()
+
+
+def backward(slot, patch, parts, weights, advected):
     tracers, levels, span = advected.shape
-    half, fields, lanes = mine.shape
+    part, fields, lanes = parts[0].shape
     return pl.pallas_call(
         backward_kernel,
         out_shape=(
             jax.ShapeDtypeStruct((fields, span), f32),
             jax.ShapeDtypeStruct(advected.shape, f32),
         ),
-        in_specs=[SMEM, SMEM, VMEM, VMEM, HBM, HBM],
-        out_specs=(VMEM, HBM),
-        input_output_aliases={5: 1},
+        in_specs=[SMEM, SMEM] + [VMEM] * 5 + [HBM],
+        out_specs=(HBM, HBM),
+        input_output_aliases={7: 1},
         scratch_shapes=[
-            pltpu.VMEM((2 * half, fields, lanes), bf16),
+            pltpu.VMEM((4 * part, fields, lanes), bf16),
             pltpu.VMEM((span // lanes, fields, lanes), f32),
             pltpu.VMEM((tracers, 8, span), f32),
+            pltpu.VMEM((fields, span), f32),
             pltpu.SemaphoreType.DMA,
-            pltpu.VMEM(weights.shape, bf16),
-            pltpu.SemaphoreType.DMA((weights.shape[0] // UNROLL,)),
+            pltpu.SemaphoreType.DMA,
         ],
-        compiler_params=params(52 * 1024 * 1024),
+        compiler_params=params(16 * 1024 * 1024),
         name="rows_to_columns",
-    )(slot, patch, mine, other, weights, advected)
+    )(slot, patch, *parts, weights, advected)
 
 
 def per_device(
@@ -529,10 +545,7 @@
 ):
     tiles, subs = lax.axis_size("tile"), lax.axis_size("sub")
     devices = tiles * subs
-    my_tile, my_sub = lax.axis_index("tile"), lax.axis_index("sub")
-    my_index = my_tile * subs + my_sub
-    blocks = block_weights.shape[0]
-    fields, ocean_rows, lanes = ocean_state.shape
+    ocean_rows = ocean_state.shape[1]
     flat = ("tile", "sub")
     tracers_t = jnp.transpose(tracers, (1, 0, 2))
     pack_a, pack_b = pack(tracers_t, courant)
@@ -541,44 +554,36 @@
     )
     msg_a = lax.ppermute(pack_a, flat, [(i, i ^ 1) for i in range(devices)])
 
-    start = my_index * blocks
-    dest = lax.dynamic_slice(block_dest.reshape(-1), (start,), (blocks,))
-    row = lax.dynamic_slice(block_row, (start,), (blocks,))
-    chunk_of = ((dest // subs) ^ my_tile) + tiles * ((dest % subs + subs - my_sub) % subs)
-    slot = chunk_of * ocean_rows + row
-
+    slot, slot_back = find_slots(block_dest, block_row, block_weights, ocean_rows)
     state = jnp.transpose(ocean_state, (1, 0, 2))
-    sign = jnp.where(jnp.arange(fields) >= fields - 2, -1.0, 1.0).astype(f32)[:, None]
-    fold = sign * ocean_state[:, -1, ::-1]
-    beside = jnp.where(my_sub == subs - 1, ocean_state[:, 0], ocean_state[:, -1])
-
     send, keep = forward(
-        slot, block_patch, tracers[0], courant, air_surface, msg_a, msg_b, beside,
+        slot, block_patch, tracers[0], courant, air_surface, msg_a, msg_b, state,
         block_weights, devices * ocean_rows,
     )
     swap = [(0, 1), (1, 0)]
     got = lax.ppermute(send, "sub", swap)
-    own, beside, *partial = merge(keep, got, state, fold, ocean_rows)
+    own, beside, *partial = merge(keep, got, state, ocean_rows)
     across = lambda x, d: lax.ppermute(x, "tile", [(i, i ^ d) for i in range(tiles)])
     got = [across(x, d) for d, x in enumerate(partial, 1)]
 
-    count = tracers.shape[1] // 2
-    some, flag = advect_some(tracers_t, courant, msg_a, msg_b, 0, count, own)
+    first, second, third = SPLIT
+    advance = functools.partial(advect_some, tracers_t, courant, msg_a, msg_b)
+    some, flag = advance(0, first, own)
     next_ocean, half = ocean(
         state, beside, exchange_rate, sea_mask, own, got, flag
     )
 
-    first = [1, 2, 3] + list(range(tiles - 1, 5, -1))
-    arrived = {d: across(half, d) for d in first}
-    for d, behind in ((5, 1), (4, 2)):
-        ready, _ = lax.optimization_barrier((half, arrived[behind]))
-        arrived[d] = across(ready, d)
-    advected, flag = advect_some(
-        tracers_t, courant, msg_a, msg_b, count, tracers.shape[1] - count, half, some
-    )
-    mine = gather_rows([half] + [arrived[d] for d in range(1, tiles)], flag)
-    other = lax.ppermute(mine, "sub", swap)
-    air_exchange, out_t = backward(slot, block_patch, mine, other, block_weights, advected)
+    arrived = [across(half, d) for d in range(tiles - 2, 0, -2)]
+    some, flag = advance(first, second, half, some)
+    even = gather_rows([half] + arrived[::-1], flag)
+    odd = across(even, 1)
+    even_other = lax.ppermute(even, "sub", swap)
+    advected, flag = advance(first + second, third, even, some)
+    odd = gather_rows([odd], flag)
+    odd_other = lax.ppermute(odd, "sub", swap)
+    air_exchange, out_t = backward(
+        slot_back, block_patch, (even, odd, even_other, odd_other), block_weights, advected
+    )
     return jnp.transpose(out_t, (1, 0, 2)), jnp.transpose(next_ocean, (1, 0, 2)), air_exchange
 
 

time: 65.7 us -> 61.3 us (0.933)
  starting transfers between devices: 26.6 us -> 21.3 us
  local copies, waits for them, and re-layouts: 4.03 us -> 7.6 us
  Pallas kernels: 27.1 us -> 23.9 us
  waiting for transfers between devices: 5.95 us -> 7.48 us
  other arithmetic: 0.85 us -> 0 us
    ppermute x14 -> x11, starting transfers between devices: 20.4 us -> 15 us  [per_device(): lax.ppermute(x, 'tile', [(i, i ^ d) for i in range(tiles)])]
    unnamed x21 -> x25, local copies, waits for them, and re-layouts: 3.9 us -> 7.55 us
    pallas_call x1, Pallas kernels: 7.15 us -> 4.6 us  [backward(): pl.pallas_call(backward_kernel, out_shape=(jax.ShapeDtypeStruct((fields,...]
    ppermute x14 -> x11, waiting for transfers between devices: 2.73 us -> 4.74 us  [per_device(): lax.ppermute(x, 'tile', [(i, i ^ d) for i in range(tiles)])]
    pallas_call x1, Pallas kernels: 5.89 us -> 4.31 us  [forward(): pl.pallas_call(functools.partial(forward_kernel, (tracers, span, top)), o...]
    pallas_call x2 -> x3, Pallas kernels: 11.7 us -> 12.5 us  [advect_some(): pl.pallas_call(functools.partial(advect_kernel, tracers, levels, first, g...]
    add x1 -> x0, other arithmetic: 0.77 us -> none  [per_device(): slot = chunk_of * ocean_rows + row]
  transfers between devices with their start and end apart: 18 -> 16, of which waited for: 4 -> 5; matrix products, arithmetic and copies ran while one was open for 4% -> 1% of each run, Pallas kernels for 18% -> 21%
where the time goes in v3:
time: 61.3 us; the launch traced here: 61.1 us
  Pallas kernels  23.9 us (39%)
  starting transfers between devices  21.3 us (35%)
  local copies, waits for them, and re-layouts  7.6 us (12%)
  waiting for transfers between devices  7.48 us (12%)
  between operations  0.87 us (1%)
    ppermute x11, starting transfers between devices, per_device(): lax.ppermute(x, 'tile', [(i, i ^ d) for i in range(tiles)])  15 us
    pallas_call x3, Pallas kernels, advect_some(): pl.pallas_call(functools.partial(advect_kernel, tracers, levels, first, g...  12.5 us
    unnamed x25, local copies, waits for them, and re-layouts  7.55 us
    ppermute x1, starting transfers between devices, per_device(): lax.ppermute(pack_b, flat, [(i, (i + 1 if i % 2 else i - 1) % devices) fo...  5.67 us
    ppermute x11, waiting for transfers between devices, per_device(): lax.ppermute(x, 'tile', [(i, i ^ d) for i in range(tiles)])  4.74 us
    pallas_call x1, Pallas kernels, backward(): pl.pallas_call(backward_kernel, out_shape=(jax.ShapeDtypeStruct((fields,...  4.6 us
    pallas_call x1, Pallas kernels, forward(): pl.pallas_call(functools.partial(forward_kernel, (tracers, span, top)), o...  4.31 us
    pallas_call x1, Pallas kernels, pack(): pl.pallas_call(functools.partial(pack_kernel, tracers, levels), out_shape...  1.98 us
  transfers between devices with their start and end apart: 16, of which 5 were waited for; matrix products, arithmetic and copies ran while one was open for 1% of the time, Pallas kernels for 21%

profile of v3, /device:TPU:0, one launch (start us, length us, event | category | flops | bytes accessed | tf_op | source)
XLA Modules:
  0.0 61.1 jit_solution(729659726208785142)
XLA Ops:
  0.6 0.0 copy-start.2
  0.6 0.0 copy-start.10
  0.7 0.0 copy-start.6
  0.7 0.0 copy-start.5
  0.7 2.0 %pack_edges.1 = (f32[64,128]{1,0:T(8,128)}, f32[64,128]{1,0:T(8,128)}) custom-call(f32[12,20,2048]{2,1,0:T(8,128)} %bitcast.11, f32[20,2048]{1,0:T(8,128)} %c_ref.5), custom_call_target="tpu_custom_call" | custom-call | tf_op jit(solution)/shard_map/pack_edges/pallas_call | solution.py:114
  2.7 0.5 collective-permute-start
  3.2 5.7 %collective-permute-start.1 = (f32[64,128]{1,0:T(8,128)}, f32[64,128]{1,0:T(8,128)S(1)}, u32[]{:S(2)}, u32[]{:S(2)}) collective-permute-start(f32[64,128]{1,0:T(8,128)} %get-tuple-element.31), channel_id=1, source_target_pairs={{0,15},{1,2},{2,1},{3,4},{4,3},{5,6},{6,5},{7,8},{8,7},{9,10},{10,... | collective-permute-start | bytes 98312 | tf_op jit(solution)/shard_map/ppermute | solution.py:552
  8.8 0.0 copy-done.2
  8.8 0.1 slice.3
  8.9 0.0 copy-done.10
  9.0 0.0 copy-start.3
  9.0 0.0 copy-done.6
  9.0 0.0 copy-done.5
  9.0 0.0 copy-start
  9.1 3.4 %copy-done = bf16[256,128,128]{2,1,0:T(8,128)(2,1)S(1)} copy-done((bf16[256,128,128]{2,1,0:T(8,128)(2,1)S(1)}, bf16[256,128,128]{2,1,0:T(8,128)(2,1)}, u32[]{:S(2)}) %copy-start) | copy-done | bytes 8388632
  12.5 0.0 copy-start.1
  12.5 0.0 copy-start.4
  12.5 0.0 copy-start.9
  12.5 0.0 collective-permute-done.msg_a
  12.5 0.0 collective-permute-done.1.msg_b
  12.5 0.0 copy-done.3
  12.5 3.3 %copy-done.1 = bf16[256,128,128]{2,1,0:T(8,128)(2,1)S(1)} copy-done((bf16[256,128,128]{2,1,0:T(8,128)(2,1)S(1)}, bf16[256,128,128]{2,1,0:T(8,128)(2,1)}, u32[]{:S(2)}) %copy-start.1) | copy-done | bytes 8388632
  15.8 0.0 copy-done.4
  15.8 0.0 copy-done.9
  15.8 4.3 %blocks_to_rows.1 = (bf16[130,16,128]{2,1,0:T(8,128)(2,1)S(1)}, f32[128,16,128]{2,1,0:T(8,128)S(1)}) custom-call(s32[2,128]{1,0:T(2,128)S(1)} %get-tuple-element.29.slot_ref, s32[256]{0:T(256)S(1)} %copy-done.9, f32[12,2048]{1,0:T(8,128)S(1)} %bitcast.18, f32[20,2048]{1,0:T(8,128)S(1)} %copy-done.3, f32[4,2048]{1,0:T(4,128)S(1)} %copy-done.4, ...), custom_call_target="tpu_custom_call" | custom-call | tf_op jit(solution)/shard_map/blocks_to_rows/pallas_call | solution.py:210
  20.2 0.0 copy-start.7
  20.2 0.0 copy-start.8
  20.2 0.1 collective-permute-start.2
  20.3 1.9 %collective-permute-done.2.got = bf16[130,16,128]{2,1,0:T(8,128)(2,1)S(1)} collective-permute-done((bf16[130,16,128]{2,1,0:T(8,128)(2,1)S(1)}, bf16[130,16,128]{2,1,0:T(8,128)(2,1)S(1)}, u32[]{:S(2)}, u32[]{:S(2)}) %collective-permute-start.2) | collective-permute-done | bytes 532512 | tf_op jit(solution)/shard_map/ppermute | solution.py:564
  22.2 0.2 merge_cores.1
  22.3 0.1 collective-permute-start.4
  22.4 1.0 %collective-permute-start.6 = (bf16[16,16,128]{2,1,0:T(8,128)(2,1)S(1)}, bf16[16,16,128]{2,1,0:T(8,128)(2,1)S(1)}, u32[]{:S(2)}, u32[]{:S(2)}) collective-permute-start(bf16[16,16,128]{2,1,0:T(8,128)(2,1)S(1)} %get-tuple-element.39), channel_id=1, source_target_pairs={{0,8},{2,10},{4,12},{6,14},{8,0},{10,2},{12,4},{14,6},{1,9},{3,11}... | collective-permute-start | bytes 196616 | tf_op jit(solution)/shard_map/ppermute | solution.py:566
  23.4 0.6 %collective-permute-start.3 = (bf16[20,16,128]{2,1,0:T(8,128)(2,1)S(1)}, bf16[20,16,128]{2,1,0:T(8,128)(2,1)S(1)}, u32[]{:S(2)}, u32[]{:S(2)}) collective-permute-start(bf16[20,16,128]{2,1,0:T(8,128)(2,1)S(1)} %get-tuple-element.36), channel_id=1, source_target_pairs={{0,2},{2,0},{4,6},{6,4},{8,10},{10,8},{12,14},{14,12},{1,3},{3,1},... | collective-permute-start | bytes 245768 | tf_op jit(solution)/shard_map/ppermute | solution.py:566
  24.1 1.9 %collective-permute-start.5 = (bf16[20,16,128]{2,1,0:T(8,128)(2,1)S(1)}, bf16[20,16,128]{2,1,0:T(8,128)(2,1)S(1)}, u32[]{:S(2)}, u32[]{:S(2)}) collective-permute-start(bf16[20,16,128]{2,1,0:T(8,128)(2,1)S(1)} %get-tuple-element.38), channel_id=1, source_target_pairs={{0,6},{2,4},{4,2},{6,0},{8,14},{10,12},{12,10},{14,8},{1,7},{3,5},... | collective-permute-start | bytes 245768 | tf_op jit(solution)/shard_map/ppermute | solution.py:566
  25.9 2.4 %collective-permute-start.9 = (bf16[20,16,128]{2,1,0:T(8,128)(2,1)S(1)}, bf16[20,16,128]{2,1,0:T(8,128)(2,1)S(1)}, u32[]{:S(2)}, u32[]{:S(2)}) collective-permute-start(bf16[20,16,128]{2,1,0:T(8,128)(2,1)S(1)} %get-tuple-element.42), channel_id=1, source_target_pairs={{0,14},{2,12},{4,10},{6,8},{8,6},{10,4},{12,2},{14,0},{1,15},{3,13... | collective-permute-start | bytes 245768 | tf_op jit(solution)/shard_map/ppermute | solution.py:566
  28.3 0.3 collective-permute-done.4.rest_1_
  28.5 0.7 %collective-permute-start.7 = (bf16[16,16,128]{2,1,0:T(8,128)(2,1)S(1)}, bf16[16,16,128]{2,1,0:T(8,128)(2,1)S(1)}, u32[]{:S(2)}, u32[]{:S(2)}) collective-permute-start(bf16[16,16,128]{2,1,0:T(8,128)(2,1)S(1)} %get-tuple-element.40), channel_id=1, source_target_pairs={{0,10},{2,8},{4,14},{6,12},{8,2},{10,0},{12,6},{14,4},{1,11},{3,9}... | collective-permute-start | bytes 196616 | tf_op jit(solution)/shard_map/ppermute | solution.py:566
  29.3 0.0 collective-permute-done.6.rest_3_
  29.3 3.4 %collective-permute-start.8 = (bf16[16,16,128]{2,1,0:T(8,128)(2,1)S(1)}, bf16[16,16,128]{2,1,0:T(8,128)(2,1)S(1)}, u32[]{:S(2)}, u32[]{:S(2)}) collective-permute-start(bf16[16,16,128]{2,1,0:T(8,128)(2,1)S(1)} %get-tuple-element.41), channel_id=1, source_target_pairs={{0,12},{2,14},{4,8},{6,10},{8,4},{10,6},{12,0},{14,2},{1,13},{3,15... | collective-permute-start | bytes 196616 | tf_op jit(solution)/shard_map/ppermute | solution.py:566
  32.7 5.8 %advect_levels.3 = (f32[12,20,2048]{2,1,0:T(8,128)}, f32[8,128]{1,0:T(8,128)S(1)}) custom-call(f32[12,20,2048]{2,1,0:T(8,128)S(1)} %bitcast.12, f32[20,2048]{1,0:T(8,128)S(1)} %copy-done.3, f32[64,128]{1,0:T(8,128)S(1)} %collective-permute-done.msg_a, f32[64,128]{1,0:T(8,128)S(1)} %collective-permute-done.1.msg_b, ...), custom_call_target="tpu_custom_call" | custom-call | flops 49152000 | bytes 1966080 | tf_op jit(solution)/shard_map/advect_levels/pallas_call | solution.py:431
  38.5 0.0 collective-permute-done.7.rest_4_
  38.5 0.0 collective-permute-done.8.rest_5_
  38.5 0.0 collective-permute-done.3.rest_0_
  38.5 0.0 collective-permute-done.5.rest_2_
  38.5 0.0 collective-permute-done.9.rest_6_
  38.5 0.0 copy-done.7
  38.5 0.0 copy-done.8
  38.6 0.2 ocean_update.1
  38.8 2.2 %collective-permute-start.12 = (bf16[16,16,128]{2,1,0:T(8,128)(2,1)S(1)}, bf16[16,16,128]{2,1,0:T(8,128)(2,1)S(1)}, u32[]{:S(2)}, u32[]{:S(2)}) collective-permute-start(bf16[16,16,128]{2,1,0:T(8,128)(2,1)S(1)} %get-tuple-element.44.rest_0_.refs_0_), channel_id=1, source_target_pairs={{0,12},{2,14},{4,8},{6,10},{8,4},{10,6},{12,0},{14,2},{1,13},{3,15... | collective-permute-start | bytes 196616 | tf_op jit(solution)/shard_map/ppermute | solution.py:566
  41.0 0.0 collective-permute-start.11
  41.0 2.2 %collective-permute-start.10 = (bf16[16,16,128]{2,1,0:T(8,128)(2,1)S(1)}, bf16[16,16,128]{2,1,0:T(8,128)(2,1)S(1)}, u32[]{:S(2)}, u32[]{:S(2)}) collective-permute-start(bf16[16,16,128]{2,1,0:T(8,128)(2,1)S(1)} %get-tuple-element.44.rest_0_.refs_0_), channel_id=1, source_target_pairs={{0,4},{2,6},{4,0},{6,2},{8,12},{10,14},{12,8},{14,10},{1,5},{3,7},... | collective-permute-start | bytes 196616 | tf_op jit(solution)/shard_map/ppermute | solution.py:566
  43.2 2.4 %advect_levels.4 = (f32[12,20,2048]{2,1,0:T(8,128)}, f32[8,128]{1,0:T(8,128)S(1)}) custom-call(f32[12,20,2048]{2,1,0:T(8,128)S(1)} %bitcast.13, f32[20,2048]{1,0:T(8,128)S(1)} %copy-done.3, f32[64,128]{1,0:T(8,128)S(1)} %collective-permute-done.msg_a, f32[64,128]{1,0:T(8,128)S(1)} %collective-permute-done.1.msg_b, ...), custom_call_target="tpu_custom_call", output_to_operand_aliasing={{0}: (5, {})} | custom-call | flops 16384000 | bytes 655360 | tf_op jit(solution)/shard_map/advect_levels/pallas_call | solution.py:431
  45.7 0.0 collective-permute-done.12.refs_3_
  45.7 1.2 %collective-permute-done.11.refs_2_ = bf16[16,16,128]{2,1,0:T(8,128)(2,1)S(1)} collective-permute-done((bf16[16,16,128]{2,1,0:T(8,128)(2,1)S(1)}, bf16[16,16,128]{2,1,0:T(8,128)(2,1)S(1)}, u32[]{:S(2)}, u32[]{:S(2)}) %collective-permute-start.11) | collective-permute-done | bytes 65568 | tf_op jit(solution)/shard_map/ppermute | solution.py:566
  46.9 0.0 collective-permute-done.10.refs_1_
  46.9 0.5 collective-permute-start.13
  47.4 0.0 collective-permute-start.14
  47.4 4.2 %advect_levels.5 = (f32[12,20,2048]{2,1,0:T(8,128)}, f32[8,128]{1,0:T(8,128)S(1)}) custom-call(f32[12,20,2048]{2,1,0:T(8,128)S(1)} %bitcast.14, f32[20,2048]{1,0:T(8,128)S(1)} %copy-done.3, f32[64,128]{1,0:T(8,128)S(1)} %collective-permute-done.msg_a, f32[64,128]{1,0:T(8,128)S(1)} %collective-permute-done.1.msg_b, ...), custom_call_target="tpu_custom_call", output_to_operand_aliasing={{0}: (5, {})} | custom-call | flops 32768000 | bytes 1310720 | tf_op jit(solution)/shard_map/advect_levels/pallas_call | solution.py:431
  51.7 3.3 %collective-permute-done.13.refs_0_ = bf16[64,16,128]{2,1,0:T(8,128)(2,1)S(1)} collective-permute-done((bf16[64,16,128]{2,1,0:T(8,128)(2,1)S(1)}, bf16[64,16,128]{2,1,0:T(8,128)(2,1)S(1)}, u32[]{:S(2)}, u32[]{:S(2)}) %collective-permute-start.13) | collective-permute-done | bytes 262176 | tf_op jit(solution)/shard_map/ppermute | solution.py:566
  54.9 0.1 collective-permute-start.15
  55.0 0.7 %copy.18 = f32[16,16,128]{2,1,0:T(8,128)} copy(f32[16,16,128]{2,0,1:T(8,128)S(1)} %bitcast.19) | data formatting | bytes 262144
  55.7 0.0 collective-permute-done.14.even_other
  55.7 0.8 %collective-permute-done.15.odd_other = bf16[64,16,128]{2,1,0:T(8,128)(2,1)S(1)} collective-permute-done((bf16[64,16,128]{2,1,0:T(8,128)(2,1)S(1)}, bf16[64,16,128]{2,1,0:T(8,128)(2,1)S(1)}, u32[]{:S(2)}, u32[]{:S(2)}) %collective-permute-start.15) | collective-permute-done | bytes 262176 | tf_op jit(solution)/shard_map/ppermute | solution.py:583
  56.5 4.6 %rows_to_columns.1 = (f32[16,2048]{1,0:T(8,128)}, f32[12,20,2048]{2,1,0:T(8,128)}) custom-call(s32[2,128]{1,0:T(2,128)S(1)} %get-tuple-element.28.slot_ref, s32[256]{0:T(256)S(1)} %copy-done.9, bf16[64,16,128]{2,1,0:T(8,128)(2,1)S(1)} %gather_rows.2.rest_0_.even, bf16[64,16,128]{2,1,0:T(8,128)(2,1)S(1)} %gather_rows.3.odd, ...), custom_call_target="tpu_custom_call", output_to_operand_aliasing={{1}: (7, {})} | custom-call | tf_op jit(solution)/shard_map/rows_to_columns/pallas_call | solution.py:512
  (5 shorter events, 0.1 us)
Async XLA Ops:
  0.6 8.2 %copy-start.2 = (f32[20,12,2048]{2,0,1:T(8,128)S(1)}, f32[20,12,2048]{2,0,1:T(8,128)}, u32[]{:S(2)}) copy-start(f32[20,12,2048]{2,0,1:T(8,128)} %param.10) | copy-start | bytes 5898244
  0.6 8.3 %copy-start.10 = (f32[16,16,128]{2,1,0:T(8,128)S(1)}, f32[16,16,128]{2,1,0:T(8,128)}, u32[]{:S(2)}) copy-start(f32[16,16,128]{2,1,0:T(8,128)} %param.17) | copy-start | bytes 393220
  0.7 8.4 %copy-start.6 = (s32[4096]{0:T(1024)S(1)}, s32[4096]{0:T(1024)}, u32[]{:S(2)}) copy-start(s32[4096]{0:T(1024)} %param.15) | copy-start | bytes 49156
  0.7 8.4 %copy-start.5 = (s32[4096,1]{0,1:T(1,128)S(1)}, s32[4096,1]{0,1:T(1,128)}, u32[]{:S(2)}) copy-start(s32[4096,1]{0,1:T(1,128)} %param.14) | copy-start | bytes 49156
  2.7 9.8 %collective-permute-start = (f32[64,128]{1,0:T(8,128)}, f32[64,128]{1,0:T(8,128)S(1)}, u32[]{:S(2)}, u32[]{:S(2)}) collective-permute-start(f32[64,128]{1,0:T(8,128)} %get-tuple-element.30), channel_id=1, source_target_pairs={{0,1},{1,0},{2,3},{3,2},{4,5},{5,4},{6,7},{7,6},{8,9},{9,8},{10,11... | collective-permute-start | bytes 98312 | tf_op jit(solution)/shard_map/ppermute | solution.py:555
  3.2 9.3 %collective-permute-start.1 = (f32[64,128]{1,0:T(8,128)}, f32[64,128]{1,0:T(8,128)S(1)}, u32[]{:S(2)}, u32[]{:S(2)}) collective-permute-start(f32[64,128]{1,0:T(8,128)} %get-tuple-element.31), channel_id=1, source_target_pairs={{0,15},{1,2},{2,1},{3,4},{4,3},{5,6},{6,5},{7,8},{8,7},{9,10},{10,... | collective-permute-start | bytes 98312 | tf_op jit(solution)/shard_map/ppermute | solution.py:552
  9.0 3.6 %copy-start.3 = (f32[20,2048]{1,0:T(8,128)S(1)}, f32[20,2048]{1,0:T(8,128)}, u32[]{:S(2)}) copy-start(f32[20,2048]{1,0:T(8,128)} %c_ref.5) | copy-start | bytes 491524
  9.0 3.4 %copy-start = (bf16[256,128,128]{2,1,0:T(8,128)(2,1)S(1)}, bf16[256,128,128]{2,1,0:T(8,128)(2,1)}, u32[]{:S(2)}) copy-start(bf16[256,128,128]{2,1,0:T(8,128)(2,1)} %weights.3) | copy-start | bytes 25165828
  12.5 3.4 %copy-start.1 = (bf16[256,128,128]{2,1,0:T(8,128)(2,1)S(1)}, bf16[256,128,128]{2,1,0:T(8,128)(2,1)}, u32[]{:S(2)}) copy-start(bf16[256,128,128]{2,1,0:T(8,128)(2,1)} %weights.3) | copy-start | bytes 25165828
  12.5 3.4 %copy-start.4 = (f32[4,2048]{1,0:T(4,128)S(1)}, f32[4,2048]{1,0:T(4,128)}, u32[]{:S(2)}) copy-start(f32[4,2048]{1,0:T(4,128)} %air.1) | copy-start | bytes 98308
  12.5 3.4 %copy-start.9 = (s32[256]{0:T(256)S(1)}, s32[256]{0:T(256)}, u32[]{:S(2)}) copy-start(s32[256]{0:T(256)} %patch_ref.3) | copy-start | bytes 3076
  20.2 18.4 %copy-start.7 = (f32[16,128]{1,0:T(8,128)S(1)}, f32[16,128]{1,0:T(8,128)}, u32[]{:S(2)}) copy-start(f32[16,128]{1,0:T(8,128)} %rate.1) | copy-start | bytes 24580
  20.2 18.4 %copy-start.8 = (s32[16,128]{1,0:T(8,128)S(1)}, s32[16,128]{1,0:T(8,128)}, u32[]{:S(2)}) copy-start(s32[16,128]{1,0:T(8,128)} %wet.1) | copy-start | bytes 24580
  20.2 2.0 %collective-permute-start.2 = (bf16[130,16,128]{2,1,0:T(8,128)(2,1)S(1)}, bf16[130,16,128]{2,1,0:T(8,128)(2,1)S(1)}, u32[]{:S(2)}, u32[]{:S(2)}) collective-permute-start(bf16[130,16,128]{2,1,0:T(8,128)(2,1)S(1)} %get-tuple-element.33), channel_id=1, source_target_pairs={{0,1},{1,0},{2,3},{3,2},{4,5},{5,4},{6,7},{7,6},{8,9},{9,8},{10,11... | collective-permute-start | bytes 1597448 | tf_op jit(solution)/shard_map/ppermute | solution.py:564
  22.3 6.2 %collective-permute-start.4 = (bf16[16,16,128]{2,1,0:T(8,128)(2,1)S(1)}, bf16[16,16,128]{2,1,0:T(8,128)(2,1)S(1)}, u32[]{:S(2)}, u32[]{:S(2)}) collective-permute-start(bf16[16,16,128]{2,1,0:T(8,128)(2,1)S(1)} %get-tuple-element.37), channel_id=1, source_target_pairs={{0,4},{2,6},{4,0},{6,2},{8,12},{10,14},{12,8},{14,10},{1,5},{3,7},... | collective-permute-start | bytes 196616 | tf_op jit(solution)/shard_map/ppermute | solution.py:566
  22.4 6.9 %collective-permute-start.6 = (bf16[16,16,128]{2,1,0:T(8,128)(2,1)S(1)}, bf16[16,16,128]{2,1,0:T(8,128)(2,1)S(1)}, u32[]{:S(2)}, u32[]{:S(2)}) collective-permute-start(bf16[16,16,128]{2,1,0:T(8,128)(2,1)S(1)} %get-tuple-element.39), channel_id=1, source_target_pairs={{0,8},{2,10},{4,12},{6,14},{8,0},{10,2},{12,4},{14,6},{1,9},{3,11}... | collective-permute-start | bytes 196616 | tf_op jit(solution)/shard_map/ppermute | solution.py:566
  23.4 15.1 %collective-permute-start.3 = (bf16[20,16,128]{2,1,0:T(8,128)(2,1)S(1)}, bf16[20,16,128]{2,1,0:T(8,128)(2,1)S(1)}, u32[]{:S(2)}, u32[]{:S(2)}) collective-permute-start(bf16[20,16,128]{2,1,0:T(8,128)(2,1)S(1)} %get-tuple-element.36), channel_id=1, source_target_pairs={{0,2},{2,0},{4,6},{6,4},{8,10},{10,8},{12,14},{14,12},{1,3},{3,1},... | collective-permute-start | bytes 245768 | tf_op jit(solution)/shard_map/ppermute | solution.py:566
  24.1 14.5 %collective-permute-start.5 = (bf16[20,16,128]{2,1,0:T(8,128)(2,1)S(1)}, bf16[20,16,128]{2,1,0:T(8,128)(2,1)S(1)}, u32[]{:S(2)}, u32[]{:S(2)}) collective-permute-start(bf16[20,16,128]{2,1,0:T(8,128)(2,1)S(1)} %get-tuple-element.38), channel_id=1, source_target_pairs={{0,6},{2,4},{4,2},{6,0},{8,14},{10,12},{12,10},{14,8},{1,7},{3,5},... | collective-permute-start | bytes 245768 | tf_op jit(solution)/shard_map/ppermute | solution.py:566
  25.9 12.6 %collective-permute-start.9 = (bf16[20,16,128]{2,1,0:T(8,128)(2,1)S(1)}, bf16[20,16,128]{2,1,0:T(8,128)(2,1)S(1)}, u32[]{:S(2)}, u32[]{:S(2)}) collective-permute-start(bf16[20,16,128]{2,1,0:T(8,128)(2,1)S(1)} %get-tuple-element.42), channel_id=1, source_target_pairs={{0,14},{2,12},{4,10},{6,8},{8,6},{10,4},{12,2},{14,0},{1,15},{3,13... | collective-permute-start | bytes 245768 | tf_op jit(solution)/shard_map/ppermute | solution.py:566
  28.5 10.0 %collective-permute-start.7 = (bf16[16,16,128]{2,1,0:T(8,128)(2,1)S(1)}, bf16[16,16,128]{2,1,0:T(8,128)(2,1)S(1)}, u32[]{:S(2)}, u32[]{:S(2)}) collective-permute-start(bf16[16,16,128]{2,1,0:T(8,128)(2,1)S(1)} %get-tuple-element.40), channel_id=1, source_target_pairs={{0,10},{2,8},{4,14},{6,12},{8,2},{10,0},{12,6},{14,4},{1,11},{3,9}... | collective-permute-start | bytes 196616 | tf_op jit(solution)/shard_map/ppermute | solution.py:566
  29.3 9.2 %collective-permute-start.8 = (bf16[16,16,128]{2,1,0:T(8,128)(2,1)S(1)}, bf16[16,16,128]{2,1,0:T(8,128)(2,1)S(1)}, u32[]{:S(2)}, u32[]{:S(2)}) collective-permute-start(bf16[16,16,128]{2,1,0:T(8,128)(2,1)S(1)} %get-tuple-element.41), channel_id=1, source_target_pairs={{0,12},{2,14},{4,8},{6,10},{8,4},{10,6},{12,0},{14,2},{1,13},{3,15... | collective-permute-start | bytes 196616 | tf_op jit(solution)/shard_map/ppermute | solution.py:566
  38.8 6.9 %collective-permute-start.12 = (bf16[16,16,128]{2,1,0:T(8,128)(2,1)S(1)}, bf16[16,16,128]{2,1,0:T(8,128)(2,1)S(1)}, u32[]{:S(2)}, u32[]{:S(2)}) collective-permute-start(bf16[16,16,128]{2,1,0:T(8,128)(2,1)S(1)} %get-tuple-element.44.rest_0_.refs_0_), channel_id=1, source_target_pairs={{0,12},{2,14},{4,8},{6,10},{8,4},{10,6},{12,0},{14,2},{1,13},{3,15... | collective-permute-start | bytes 196616 | tf_op jit(solution)/shard_map/ppermute | solution.py:566
  41.0 5.9 %collective-permute-start.11 = (bf16[16,16,128]{2,1,0:T(8,128)(2,1)S(1)}, bf16[16,16,128]{2,1,0:T(8,128)(2,1)S(1)}, u32[]{:S(2)}, u32[]{:S(2)}) collective-permute-start(bf16[16,16,128]{2,1,0:T(8,128)(2,1)S(1)} %get-tuple-element.44.rest_0_.refs_0_), channel_id=1, source_target_pairs={{0,8},{2,10},{4,12},{6,14},{8,0},{10,2},{12,4},{14,6},{1,9},{3,11}... | collective-permute-start | bytes 196616 | tf_op jit(solution)/shard_map/ppermute | solution.py:566
  41.0 5.9 %collective-permute-start.10 = (bf16[16,16,128]{2,1,0:T(8,128)(2,1)S(1)}, bf16[16,16,128]{2,1,0:T(8,128)(2,1)S(1)}, u32[]{:S(2)}, u32[]{:S(2)}) collective-permute-start(bf16[16,16,128]{2,1,0:T(8,128)(2,1)S(1)} %get-tuple-element.44.rest_0_.refs_0_), channel_id=1, source_target_pairs={{0,4},{2,6},{4,0},{6,2},{8,12},{10,14},{12,8},{14,10},{1,5},{3,7},... | collective-permute-start | bytes 196616 | tf_op jit(solution)/shard_map/ppermute | solution.py:566
  46.9 8.0 %collective-permute-start.13 = (bf16[64,16,128]{2,1,0:T(8,128)(2,1)S(1)}, bf16[64,16,128]{2,1,0:T(8,128)(2,1)S(1)}, u32[]{:S(2)}, u32[]{:S(2)}) collective-permute-start(bf16[64,16,128]{2,1,0:T(8,128)(2,1)S(1)} %gather_rows.2.rest_0_.even), channel_id=1, source_target_pairs={{0,2},{2,0},{4,6},{6,4},{8,10},{10,8},{12,14},{14,12},{1,3},{3,1},... | collective-permute-start | bytes 786440 | tf_op jit(solution)/shard_map/ppermute | solution.py:566
  47.4 8.3 %collective-permute-start.14 = (bf16[64,16,128]{2,1,0:T(8,128)(2,1)S(1)}, bf16[64,16,128]{2,1,0:T(8,128)(2,1)S(1)}, u32[]{:S(2)}, u32[]{:S(2)}) collective-permute-start(bf16[64,16,128]{2,1,0:T(8,128)(2,1)S(1)} %gather_rows.2.rest_0_.even), channel_id=1, source_target_pairs={{0,1},{1,0},{2,3},{3,2},{4,5},{5,4},{6,7},{7,6},{8,9},{9,8},{10,11... | collective-permute-start | bytes 786440 | tf_op jit(solution)/shard_map/ppermute | solution.py:580
  54.9 1.6 %collective-permute-start.15 = (bf16[64,16,128]{2,1,0:T(8,128)(2,1)S(1)}, bf16[64,16,128]{2,1,0:T(8,128)(2,1)S(1)}, u32[]{:S(2)}, u32[]{:S(2)}) collective-permute-start(bf16[64,16,128]{2,1,0:T(8,128)(2,1)S(1)} %gather_rows.3.odd), channel_id=1, source_target_pairs={{0,1},{1,0},{2,3},{3,2},{4,5},{5,4},{6,7},{7,6},{8,9},{9,8},{10,11... | collective-permute-start | bytes 786440 | tf_op jit(solution)/shard_map/ppermute | solution.py:583

commit v4 on v3

--- a/solution.py
+++ b/solution.py
@@ -14,7 +14,8 @@
 EDGE = 16
 GROUPS = LANES // EDGE
 UNROLL = 64
-SPLIT = (6, 2, 4)
+GROUP = 4
+SETS = 2
 
 VMEM = pl.BlockSpec(memory_space=pltpu.VMEM)
 SMEM = pl.BlockSpec(memory_space=pltpu.SMEM)
@@ -128,7 +129,9 @@
     )(tracers_t, courant)
 
 
-def slot_kernel(chunk, dest_ref, row_ref, _, slot_ref, back_ref):
+def prepare_kernel(chunk, dest_ref, row_ref, weights_hbm, _, slot_ref, back_ref, weights, sem):
+    copy = pltpu.make_async_copy(weights_hbm, weights, sem)
+    copy.start()
     tile, sub, tiles, subs = place()
     count = slot_ref.shape[0]
     mine = pl.ds((tile * subs + sub) * count, count)
@@ -138,19 +141,22 @@
     row = row_ref[mine, :]
     slot_ref[...] = (core + apart) * chunk + row
     back_ref[...] = (core + apart % 2 * (tiles // 2) + apart // 2) * chunk + row
-
-
-def find_slots(dest, row, weights, chunk):
+    copy.wait()
+
+
+def prepare(dest, row, weights, after, chunk):
     blocks = weights.shape[0]
     whole = (dest.size // LANES, LANES)
     return pl.pallas_call(
-        functools.partial(slot_kernel, chunk),
-        out_shape=(jax.ShapeDtypeStruct((blocks // LANES, LANES), jnp.int32),) * 2,
-        in_specs=[VMEM, VMEM, VMEM],
-        out_specs=(VMEM, VMEM),
-        compiler_params=params(28 * 1024 * 1024),
-        name="find_slots",
-    )(dest.reshape(whole), row.reshape(whole), weights)
+        functools.partial(prepare_kernel, chunk),
+        out_shape=(jax.ShapeDtypeStruct((blocks // LANES, LANES), jnp.int32),) * 2
+        + (jax.ShapeDtypeStruct(weights.shape, weights.dtype),),
+        in_specs=[VMEM, VMEM, HBM, ANY],
+        out_specs=(VMEM, VMEM, VMEM),
+        scratch_shapes=[pltpu.SemaphoreType.DMA],
+        compiler_params=params(44 * 1024 * 1024),
+        name="prepare_blocks",
+    )(dest.reshape(whole), row.reshape(whole), weights, after)
 
 
 def high_low(x):
@@ -335,27 +341,26 @@
         out[i * chunk : (i + 1) * chunk] = refs[i][...]
 
 
-def gather_rows(parts, after):
+def gather_rows(parts, *after):
     chunk, fields, lanes = parts[0].shape
     return pl.pallas_call(
         functools.partial(gather_kernel, len(parts)),
         out_shape=jax.ShapeDtypeStruct((chunk * len(parts), fields, lanes), bf16),
-        in_specs=[VMEM] * len(parts) + [ANY],
+        in_specs=[VMEM] * len(parts) + [ANY] * len(after),
         out_specs=VMEM,
         compiler_params=params(8 * 1024 * 1024),
         name="gather_rows",
-    )(*parts, after)
+    )(*parts, *after)
 
 
 def advect_kernel(
     tracers, levels, first, group, q_ref, c_ref, msg_a, msg_b, *rest
 ):
-    out_ref, flag_ref, right, left, own, state, lhs, band = rest[-8:]
+    out_ref, flag_ref, right, left, own, band, *scratch = rest[-6 - 2 * SETS :]
     even = is_even()
     span = q_ref.shape[2]
     pad = pl.cdiv(levels, 8) * 8
     tiles = span // LANES + 2
-    rows = group * pad
     tile = lambda i: slice(i * LANES, (i + 1) * LANES)
 
     def sides(item):
@@ -376,7 +381,8 @@
             ref[...] = jnp.zeros_like(ref)
             for i in range(tiles):
                 ref[i, :levels] = value[:, tile(i)]
-        state[...] = jnp.zeros_like(state)
+        for state in scratch[:SETS]:
+            state[...] = jnp.zeros_like(state)
         r = lax.broadcasted_iota(jnp.int32, band.shape, 0) % (2 * LANES)
         j = lax.broadcasted_iota(jnp.int32, band.shape, 1)
         column = jnp.where(r < LANES, r, jnp.where(r < LANES + LANES // 2, r, r - 2 * LANES))
@@ -385,16 +391,22 @@
         band[...] = weight.astype(bf16)
         flag_ref[...] = jnp.zeros_like(flag_ref)
 
+    sets = SETS
+    states, operands = scratch[:sets], scratch[sets:]
+    each = group // sets
     for t in range(group):
+        state, at = states[t // each], t % each
         before, after = sides(pl.program_id(0) * group + first + t)
-        part = slice(t * pad, t * pad + levels)
+        part = slice(at * pad, at * pad + levels)
         state[0, part] = before
         for i in range(1, tiles - 1):
             state[i, part] = q_ref[t, :, tile(i - 1)]
         state[tiles - 1, part] = after
 
+    rows = each * pad
     lane = lax.broadcasted_iota(jnp.int32, (rows, LANES), 1)
-    for _ in range(ASTEPS):
+
+    def edge_values(state, lhs):
         halves = [high_low(state[i]) for i in range(tiles)]
         for i in range(tiles):
             part = slice(i * rows, (i + 1) * rows)
@@ -403,27 +415,41 @@
                 lhs[part, tile(2 * h + 1)] = jnp.where(
                     lane < LANES // 2, halves[min(i + 1, tiles - 1)][h], halves[max(i - 1, 0)][h]
                 )
-        edges = jnp.dot(lhs[...], band[...], preferred_element_type=f32)
+        return jnp.dot(lhs[...], band[...], preferred_element_type=f32)
+
+    def advance(state, edges):
         last = None
         for i in range(tiles):
-            edge = edges[i * rows : (i + 1) * rows].reshape(group, pad, 2 * LANES)
+            edge = edges[i * rows : (i + 1) * rows].reshape(each, pad, 2 * LANES)
             q = state[i]
             flux = (
-                right[i] * edge[..., :LANES] - left[i] * edge[..., LANES:]
-            ).reshape(rows, LANES) + (own[i] * q.reshape(group, pad, LANES)).reshape(rows, LANES)
+                right[i] * edge[..., :LANES]
+                - left[i] * edge[..., LANES:]
+                + own[i] * q.reshape(each, pad, LANES)
+            ).reshape(rows, LANES)
             moved = pltpu.roll(flux, 1, 1)
             before = moved if last is None else jnp.where(lane == 0, last, moved)
             state[i] = q - (flux - before)
             last = moved
 
+    pending = None
+    for step in range(ASTEPS):
+        for k in range(sets):
+            edges = edge_values(states[k], operands[k])
+            if pending is not None:
+                advance(*pending)
+            pending = (states[k], edges)
+    advance(*pending)
+
     for t in range(group):
         for i in range(1, tiles - 1):
-            out_ref[t, :, tile(i - 1)] = state[i, t * pad : t * pad + levels]
+            at = t % each * pad
+            out_ref[t, :, tile(i - 1)] = states[t // each][i, at : at + levels]
 
 
 def advect_some(tracers_t, courant, msg_a, msg_b, first, count, after, into=None):
     tracers, levels, span = tracers_t.shape
-    group = 2 if count % 2 == 0 and first % 2 == 0 else 1
+    group = GROUP
     tiles, pad = span // LANES + 2, pl.cdiv(levels, 8) * 8
     whole = lambda shape: pl.BlockSpec(shape, lambda i: (0,) * len(shape))
     block = pl.BlockSpec((group, levels, span), lambda i: (i + first // group, 0, 0))
@@ -445,11 +471,9 @@
         out_specs=(block, whole((8, LANES))),
         input_output_aliases={} if into is None else {5: 0},
         scratch_shapes=[pltpu.VMEM((tiles, pad, LANES), f32)] * 3
-        + [
-            pltpu.VMEM((tiles, group * pad, LANES), f32),
-            pltpu.VMEM((tiles * group * pad, 4 * LANES), bf16),
-            pltpu.VMEM((4 * LANES, 2 * LANES), bf16),
-        ],
+        + [pltpu.VMEM((4 * LANES, 2 * LANES), bf16)]
+        + [pltpu.VMEM((tiles, group // SETS * pad, LANES), f32)] * SETS
+        + [pltpu.VMEM((tiles * group // SETS * pad, 4 * LANES), bf16)] * SETS,
         compiler_params=params(12 * 1024 * 1024),
         cost_estimate=pl.CostEstimate(
             flops=200 * count * levels * span,
@@ -554,11 +578,13 @@
     )
     msg_a = lax.ppermute(pack_a, flat, [(i, i ^ 1) for i in range(devices)])
 
-    slot, slot_back = find_slots(block_dest, block_row, block_weights, ocean_rows)
+    slot, slot_back, weights = prepare(
+        block_dest, block_row, block_weights, pack_b, ocean_rows
+    )
     state = jnp.transpose(ocean_state, (1, 0, 2))
     send, keep = forward(
         slot, block_patch, tracers[0], courant, air_surface, msg_a, msg_b, state,
-        block_weights, devices * ocean_rows,
+        weights, devices * ocean_rows,
     )
     swap = [(0, 1), (1, 0)]
     got = lax.ppermute(send, "sub", swap)
@@ -566,23 +592,23 @@
     across = lambda x, d: lax.ppermute(x, "tile", [(i, i ^ d) for i in range(tiles)])
     got = [across(x, d) for d, x in enumerate(partial, 1)]
 
-    first, second, third = SPLIT
     advance = functools.partial(advect_some, tracers_t, courant, msg_a, msg_b)
-    some, flag = advance(0, first, own)
+    count = tracers.shape[1] // 3
+    some, flag = advance(0, count, own)
     next_ocean, half = ocean(
         state, beside, exchange_rate, sea_mask, own, got, flag
     )
 
     arrived = [across(half, d) for d in range(tiles - 2, 0, -2)]
-    some, flag = advance(first, second, half, some)
+    some, flag = advance(count, count, half, some)
     even = gather_rows([half] + arrived[::-1], flag)
     odd = across(even, 1)
     even_other = lax.ppermute(even, "sub", swap)
-    advected, flag = advance(first + second, third, even, some)
+    advected, flag = advance(2 * count, tracers.shape[1] - 2 * count, even, some)
     odd = gather_rows([odd], flag)
     odd_other = lax.ppermute(odd, "sub", swap)
     air_exchange, out_t = backward(
-        slot_back, block_patch, (even, odd, even_other, odd_other), block_weights, advected
+        slot_back, block_patch, (even, odd, even_other, odd_other), weights, advected
     )
     return jnp.transpose(out_t, (1, 0, 2)), jnp.transpose(next_ocean, (1, 0, 2)), air_exchange
 

time: 61.3 us -> 57.1 us (0.931)
  local copies, waits for them, and re-layouts: 7.6 us -> 1.62 us
  starting transfers between devices: 21.3 us -> 22.3 us
  Pallas kernels: 23.9 us -> 24.7 us
    unnamed x25 -> x23, local copies, waits for them, and re-layouts: 7.55 us -> 1.57 us
    pallas_call x1, Pallas kernels: 0.02 us -> 3.43 us  [prepare(): pl.pallas_call(functools.partial(prepare_kernel, chunk), out_shape=(jax.S...]
    pallas_call x3, Pallas kernels: 12.5 us -> 9.91 us  [advect_some(): pl.pallas_call(functools.partial(advect_kernel, tracers, levels, first, g...]
    ppermute x11, starting transfers between devices: 15 us -> 15.9 us  [per_device(): lax.ppermute(x, 'tile', [(i, i ^ d) for i in range(tiles)])]
  transfers between devices with their start and end apart: 16 -> 16, of which waited for: 5 -> 6; matrix products, arithmetic and copies ran while one was open for 1% -> 1% of each run, Pallas kernels for 21% -> 23%
where the time goes in v4:
time: 57.1 us; the launch traced here: 56.9 us
  Pallas kernels  24.7 us (43%)
  starting transfers between devices  22.3 us (39%)
  waiting for transfers between devices  7.42 us (13%)
  local copies, waits for them, and re-layouts  1.62 us (3%)
  between operations  0.88 us (2%)
    ppermute x11, starting transfers between devices, per_device(): lax.ppermute(x, 'tile', [(i, i ^ d) for i in range(tiles)])  15.9 us
    pallas_call x3, Pallas kernels, advect_some(): pl.pallas_call(functools.partial(advect_kernel, tracers, levels, first, g...  9.91 us
    ppermute x1, starting transfers between devices, per_device(): lax.ppermute(pack_b, flat, [(i, (i + 1 if i % 2 else i - 1) % devices) fo...  5.67 us
    ppermute x11, waiting for transfers between devices, per_device(): lax.ppermute(x, 'tile', [(i, i ^ d) for i in range(tiles)])  4.68 us
    pallas_call x1, Pallas kernels, backward(): pl.pallas_call(backward_kernel, out_shape=(jax.ShapeDtypeStruct((fields,...  4.61 us
    pallas_call x1, Pallas kernels, forward(): pl.pallas_call(functools.partial(forward_kernel, (tracers, span, top)), o...  4.32 us
    pallas_call x1, Pallas kernels, prepare(): pl.pallas_call(functools.partial(prepare_kernel, chunk), out_shape=(jax.S...  3.43 us
    pallas_call x1, Pallas kernels, pack(): pl.pallas_call(functools.partial(pack_kernel, tracers, levels), out_shape...  1.98 us
  transfers between devices with their start and end apart: 16, of which 6 were waited for; matrix products, arithmetic and copies ran while one was open for 1% of the time, Pallas kernels for 23%

profile of v4, /device:TPU:0, one launch (start us, length us, event | category | flops | bytes accessed | tf_op | source)
XLA Modules:
  0.0 56.9 jit_solution(4223654025269591947)
XLA Ops:
  0.6 0.0 copy-start
  0.6 0.0 copy-start.9
  0.7 0.0 copy-start.5
  0.7 0.0 copy-start.4
  0.7 2.0 %pack_edges.1 = (f32[64,128]{1,0:T(8,128)}, f32[64,128]{1,0:T(8,128)}) custom-call(f32[12,20,2048]{2,1,0:T(8,128)} %bitcast.11, f32[20,2048]{1,0:T(8,128)} %c_ref.5), custom_call_target="tpu_custom_call" | custom-call | tf_op jit(solution)/shard_map/pack_edges/pallas_call | solution.py:115
  2.7 0.5 collective-permute-start
  3.2 5.7 %collective-permute-start.1 = (f32[64,128]{1,0:T(8,128)}, f32[64,128]{1,0:T(8,128)S(1)}, u32[]{:S(2)}, u32[]{:S(2)}) collective-permute-start(f32[64,128]{1,0:T(8,128)} %get-tuple-element.29._), channel_id=1, source_target_pairs={{0,15},{1,2},{2,1},{3,4},{4,3},{5,6},{6,5},{7,8},{8,7},{9,10},{10,... | collective-permute-start | bytes 98312 | tf_op jit(solution)/shard_map/ppermute | solution.py:576
  8.8 0.0 copy-done
  8.8 0.1 slice.3
  8.9 0.0 copy-done.9
  9.0 0.0 copy-done.5
  9.0 0.0 copy-done.4
  9.0 0.0 copy-start.3
  9.0 0.7 %copy-done.3 = f32[64,128]{1,0:T(8,128)S(1)} copy-done((f32[64,128]{1,0:T(8,128)S(1)}, f32[64,128]{1,0:T(8,128)}, u32[]{:S(2)}) %copy-start.3) | copy-done | bytes 32792
  9.8 0.0 copy-start.1
  9.8 0.0 copy-start.2
  9.8 0.0 copy-start.8
  9.8 3.4 %prepare_blocks.1 = (s32[2,128]{1,0:T(2,128)S(1)}, s32[2,128]{1,0:T(2,128)S(1)}, bf16[256,128,128]{2,1,0:T(8,128)(2,1)S(1)}) custom-call(s32[32,128]{1,0:T(8,128)S(1)} %bitcast.20, s32[32,128]{1,0:T(8,128)S(1)} %bitcast.21, bf16[256,128,128]{2,1,0:T(8,128)(2,1)} %weights_hbm.1, f32[64,128]{1,0:T(8,128)S(1)} %copy-done.3), custom_call_target="tpu_custom_call" | custom-call | tf_op jit(solution)/shard_map/prepare_blocks/pallas_call | solution.py:150
  13.2 0.0 collective-permute-done.msg_a
  13.2 0.0 collective-permute-done.1.msg_b
  13.3 0.0 copy-done.1
  13.3 0.0 copy-done.2
  13.3 0.0 copy-done.8
  13.3 4.3 %blocks_to_rows.1 = (bf16[130,16,128]{2,1,0:T(8,128)(2,1)S(1)}, f32[128,16,128]{2,1,0:T(8,128)S(1)}) custom-call(s32[2,128]{1,0:T(2,128)S(1)} %get-tuple-element.31.slot_ref, s32[256]{0:T(256)S(1)} %copy-done.8, f32[12,2048]{1,0:T(8,128)S(1)} %bitcast.18, f32[20,2048]{1,0:T(8,128)S(1)} %copy-done.1, f32[4,2048]{1,0:T(4,128)S(1)} %copy-done.2, ...), custom_call_target="tpu_custom_call" | custom-call | tf_op jit(solution)/shard_map/blocks_to_rows/pallas_call | solution.py:216
  17.6 0.0 copy-start.6
  17.6 0.0 copy-start.7
  17.6 0.1 collective-permute-start.2
  17.7 1.9 %collective-permute-done.2.got = bf16[130,16,128]{2,1,0:T(8,128)(2,1)S(1)} collective-permute-done((bf16[130,16,128]{2,1,0:T(8,128)(2,1)S(1)}, bf16[130,16,128]{2,1,0:T(8,128)(2,1)S(1)}, u32[]{:S(2)}, u32[]{:S(2)}) %collective-permute-start.2) | collective-permute-done | bytes 532512 | tf_op jit(solution)/shard_map/ppermute | solution.py:590
  19.6 0.2 merge_cores.1
  19.8 0.1 collective-permute-start.4
  19.9 1.0 %collective-permute-start.6 = (bf16[16,16,128]{2,1,0:T(8,128)(2,1)S(1)}, bf16[16,16,128]{2,1,0:T(8,128)(2,1)S(1)}, u32[]{:S(2)}, u32[]{:S(2)}) collective-permute-start(bf16[16,16,128]{2,1,0:T(8,128)(2,1)S(1)} %get-tuple-element.41), channel_id=1, source_target_pairs={{0,8},{2,10},{4,12},{6,14},{8,0},{10,2},{12,4},{14,6},{1,9},{3,11}... | collective-permute-start | bytes 196616 | tf_op jit(solution)/shard_map/ppermute | solution.py:592
  20.9 2.0 %collective-permute-start.3 = (bf16[20,16,128]{2,1,0:T(8,128)(2,1)S(1)}, bf16[20,16,128]{2,1,0:T(8,128)(2,1)S(1)}, u32[]{:S(2)}, u32[]{:S(2)}) collective-permute-start(bf16[20,16,128]{2,1,0:T(8,128)(2,1)S(1)} %get-tuple-element.38), channel_id=1, source_target_pairs={{0,2},{2,0},{4,6},{6,4},{8,10},{10,8},{12,14},{14,12},{1,3},{3,1},... | collective-permute-start | bytes 245768 | tf_op jit(solution)/shard_map/ppermute | solution.py:592
  22.8 0.5 collective-permute-start.5
  23.4 2.4 %collective-permute-start.9 = (bf16[20,16,128]{2,1,0:T(8,128)(2,1)S(1)}, bf16[20,16,128]{2,1,0:T(8,128)(2,1)S(1)}, u32[]{:S(2)}, u32[]{:S(2)}) collective-permute-start(bf16[20,16,128]{2,1,0:T(8,128)(2,1)S(1)} %get-tuple-element.44), channel_id=1, source_target_pairs={{0,14},{2,12},{4,10},{6,8},{8,6},{10,4},{12,2},{14,0},{1,15},{3,13... | collective-permute-start | bytes 245768 | tf_op jit(solution)/shard_map/ppermute | solution.py:592
  25.7 0.2 collective-permute-done.4.rest_1_
  25.9 0.8 %collective-permute-start.7 = (bf16[16,16,128]{2,1,0:T(8,128)(2,1)S(1)}, bf16[16,16,128]{2,1,0:T(8,128)(2,1)S(1)}, u32[]{:S(2)}, u32[]{:S(2)}) collective-permute-start(bf16[16,16,128]{2,1,0:T(8,128)(2,1)S(1)} %get-tuple-element.42), channel_id=1, source_target_pairs={{0,10},{2,8},{4,14},{6,12},{8,2},{10,0},{12,6},{14,4},{1,11},{3,9}... | collective-permute-start | bytes 196616 | tf_op jit(solution)/shard_map/ppermute | solution.py:592
  26.7 0.0 collective-permute-done.6.rest_3_
  26.7 3.4 %collective-permute-start.8 = (bf16[16,16,128]{2,1,0:T(8,128)(2,1)S(1)}, bf16[16,16,128]{2,1,0:T(8,128)(2,1)S(1)}, u32[]{:S(2)}, u32[]{:S(2)}) collective-permute-start(bf16[16,16,128]{2,1,0:T(8,128)(2,1)S(1)} %get-tuple-element.43), channel_id=1, source_target_pairs={{0,12},{2,14},{4,8},{6,10},{8,4},{10,6},{12,0},{14,2},{1,13},{3,15... | collective-permute-start | bytes 196616 | tf_op jit(solution)/shard_map/ppermute | solution.py:592
  30.1 3.3 %advect_levels.3 = (f32[12,20,2048]{2,1,0:T(8,128)}, f32[8,128]{1,0:T(8,128)S(1)}) custom-call(f32[12,20,2048]{2,1,0:T(8,128)S(1)} %bitcast.12, f32[20,2048]{1,0:T(8,128)S(1)} %copy-done.1, f32[64,128]{1,0:T(8,128)S(1)} %collective-permute-done.msg_a, f32[64,128]{1,0:T(8,128)S(1)} %collective-permute-done.1.msg_b, ...), custom_call_target="tpu_custom_call" | custom-call | flops 32768000 | bytes 1310720 | tf_op jit(solution)/shard_map/advect_levels/pallas_call | solution.py:457
  33.4 2.2 %collective-permute-done.7.rest_4_ = bf16[16,16,128]{2,1,0:T(8,128)(2,1)S(1)} collective-permute-done((bf16[16,16,128]{2,1,0:T(8,128)(2,1)S(1)}, bf16[16,16,128]{2,1,0:T(8,128)(2,1)S(1)}, u32[]{:S(2)}, u32[]{:S(2)}) %collective-permute-start.7) | collective-permute-done | bytes 65568 | tf_op jit(solution)/shard_map/ppermute | solution.py:592
  35.6 0.0 collective-permute-done.8.rest_5_
  35.6 0.0 collective-permute-done.3.rest_0_
  35.6 0.0 collective-permute-done.5.rest_2_
  35.6 0.0 collective-permute-done.9.rest_6_
  35.6 0.0 copy-done.6
  35.7 0.0 copy-done.7
  35.7 0.2 ocean_update.1
  35.9 2.6 %collective-permute-start.12 = (bf16[16,16,128]{2,1,0:T(8,128)(2,1)S(1)}, bf16[16,16,128]{2,1,0:T(8,128)(2,1)S(1)}, u32[]{:S(2)}, u32[]{:S(2)}) collective-permute-start(bf16[16,16,128]{2,1,0:T(8,128)(2,1)S(1)} %get-tuple-element.46.rest_0_.refs_0_), channel_id=1, source_target_pairs={{0,12},{2,14},{4,8},{6,10},{8,4},{10,6},{12,0},{14,2},{1,13},{3,15... | collective-permute-start | bytes 196616 | tf_op jit(solution)/shard_map/ppermute | solution.py:592
  38.5 0.4 collective-permute-start.11
  38.8 1.5 %collective-permute-start.10 = (bf16[16,16,128]{2,1,0:T(8,128)(2,1)S(1)}, bf16[16,16,128]{2,1,0:T(8,128)(2,1)S(1)}, u32[]{:S(2)}, u32[]{:S(2)}) collective-permute-start(bf16[16,16,128]{2,1,0:T(8,128)(2,1)S(1)} %get-tuple-element.46.rest_0_.refs_0_), channel_id=1, source_target_pairs={{0,4},{2,6},{4,0},{6,2},{8,12},{10,14},{12,8},{14,10},{1,5},{3,7},... | collective-permute-start | bytes 196616 | tf_op jit(solution)/shard_map/ppermute | solution.py:592
  40.4 3.3 %advect_levels.4 = (f32[12,20,2048]{2,1,0:T(8,128)}, f32[8,128]{1,0:T(8,128)S(1)}) custom-call(f32[12,20,2048]{2,1,0:T(8,128)S(1)} %bitcast.13, f32[20,2048]{1,0:T(8,128)S(1)} %copy-done.1, f32[64,128]{1,0:T(8,128)S(1)} %collective-permute-done.msg_a, f32[64,128]{1,0:T(8,128)S(1)} %collective-permute-done.1.msg_b, ...), custom_call_target="tpu_custom_call", output_to_operand_aliasing={{0}: (5, {})} | custom-call | flops 32768000 | bytes 1310720 | tf_op jit(solution)/shard_map/advect_levels/pallas_call | solution.py:457
  43.7 0.0 collective-permute-done.12.refs_3_
  43.7 0.3 collective-permute-done.11.refs_2_
  44.0 0.0 collective-permute-done.10.refs_1_
  44.0 1.4 %collective-permute-start.13 = (bf16[64,16,128]{2,1,0:T(8,128)(2,1)S(1)}, bf16[64,16,128]{2,1,0:T(8,128)(2,1)S(1)}, u32[]{:S(2)}, u32[]{:S(2)}) collective-permute-start(bf16[64,16,128]{2,1,0:T(8,128)(2,1)S(1)} %gather_rows.2.rest_0_.even), channel_id=1, source_target_pairs={{0,2},{2,0},{4,6},{6,4},{8,10},{10,8},{12,14},{14,12},{1,3},{3,1},... | collective-permute-start | bytes 786440 | tf_op jit(solution)/shard_map/ppermute | solution.py:592
  45.4 0.0 collective-permute-start.14
  45.4 3.3 %advect_levels.5 = (f32[12,20,2048]{2,1,0:T(8,128)}, f32[8,128]{1,0:T(8,128)S(1)}) custom-call(f32[12,20,2048]{2,1,0:T(8,128)S(1)} %bitcast.14, f32[20,2048]{1,0:T(8,128)S(1)} %copy-done.1, f32[64,128]{1,0:T(8,128)S(1)} %collective-permute-done.msg_a, f32[64,128]{1,0:T(8,128)S(1)} %collective-permute-done.1.msg_b, ...), custom_call_target="tpu_custom_call", output_to_operand_aliasing={{0}: (5, {})} | custom-call | flops 32768000 | bytes 1310720 | tf_op jit(solution)/shard_map/advect_levels/pallas_call | solution.py:457
  48.7 2.0 %collective-permute-done.13.refs_0_ = bf16[64,16,128]{2,1,0:T(8,128)(2,1)S(1)} collective-permute-done((bf16[64,16,128]{2,1,0:T(8,128)(2,1)S(1)}, bf16[64,16,128]{2,1,0:T(8,128)(2,1)S(1)}, u32[]{:S(2)}, u32[]{:S(2)}) %collective-permute-start.13) | collective-permute-done | bytes 262176 | tf_op jit(solution)/shard_map/ppermute | solution.py:592
  50.7 0.1 collective-permute-start.15
  50.7 0.7 %copy.18 = f32[16,16,128]{2,1,0:T(8,128)} copy(f32[16,16,128]{2,0,1:T(8,128)S(1)} %bitcast.19) | data formatting | bytes 262144
  51.4 0.0 collective-permute-done.14.even_other
  51.4 0.8 %collective-permute-done.15.odd_other = bf16[64,16,128]{2,1,0:T(8,128)(2,1)S(1)} collective-permute-done((bf16[64,16,128]{2,1,0:T(8,128)(2,1)S(1)}, bf16[64,16,128]{2,1,0:T(8,128)(2,1)S(1)}, u32[]{:S(2)}, u32[]{:S(2)}) %collective-permute-start.15) | collective-permute-done | bytes 262176 | tf_op jit(solution)/shard_map/ppermute | solution.py:609
  52.3 4.6 %rows_to_columns.1 = (f32[16,2048]{1,0:T(8,128)}, f32[12,20,2048]{2,1,0:T(8,128)}) custom-call(s32[2,128]{1,0:T(2,128)S(1)} %get-tuple-element.30.slot_ref, s32[256]{0:T(256)S(1)} %copy-done.8, bf16[64,16,128]{2,1,0:T(8,128)(2,1)S(1)} %gather_rows.2.rest_0_.even, bf16[64,16,128]{2,1,0:T(8,128)(2,1)S(1)} %gather_rows.3.odd, ...), custom_call_target="tpu_custom_call", output_to_operand_aliasing={{1}: (7, {})} | custom-call | tf_op jit(solution)/shard_map/rows_to_columns/pallas_call | solution.py:536
  (4 shorter events, 0.1 us)
Async XLA Ops:
  0.6 8.2 %copy-start = (f32[20,12,2048]{2,0,1:T(8,128)S(1)}, f32[20,12,2048]{2,0,1:T(8,128)}, u32[]{:S(2)}) copy-start(f32[20,12,2048]{2,0,1:T(8,128)} %param.10) | copy-start | bytes 5898244
  0.6 8.3 %copy-start.9 = (f32[16,16,128]{2,1,0:T(8,128)S(1)}, f32[16,16,128]{2,1,0:T(8,128)}, u32[]{:S(2)}) copy-start(f32[16,16,128]{2,1,0:T(8,128)} %param.17) | copy-start | bytes 393220
  0.7 8.4 %copy-start.5 = (s32[4096]{0:T(1024)S(1)}, s32[4096]{0:T(1024)}, u32[]{:S(2)}) copy-start(s32[4096]{0:T(1024)} %param.15) | copy-start | bytes 49156
  0.7 8.4 %copy-start.4 = (s32[4096,1]{0,1:T(1,128)S(1)}, s32[4096,1]{0,1:T(1,128)}, u32[]{:S(2)}) copy-start(s32[4096,1]{0,1:T(1,128)} %param.14) | copy-start | bytes 49156
  2.7 10.6 %collective-permute-start = (f32[64,128]{1,0:T(8,128)}, f32[64,128]{1,0:T(8,128)S(1)}, u32[]{:S(2)}, u32[]{:S(2)}) collective-permute-start(f32[64,128]{1,0:T(8,128)} %get-tuple-element.32), channel_id=1, source_target_pairs={{0,1},{1,0},{2,3},{3,2},{4,5},{5,4},{6,7},{7,6},{8,9},{9,8},{10,11... | collective-permute-start | bytes 98312 | tf_op jit(solution)/shard_map/ppermute | solution.py:579
  3.2 10.1 %collective-permute-start.1 = (f32[64,128]{1,0:T(8,128)}, f32[64,128]{1,0:T(8,128)S(1)}, u32[]{:S(2)}, u32[]{:S(2)}) collective-permute-start(f32[64,128]{1,0:T(8,128)} %get-tuple-element.29._), channel_id=1, source_target_pairs={{0,15},{1,2},{2,1},{3,4},{4,3},{5,6},{6,5},{7,8},{8,7},{9,10},{10,... | collective-permute-start | bytes 98312 | tf_op jit(solution)/shard_map/ppermute | solution.py:576
  9.0 0.8 %copy-start.3 = (f32[64,128]{1,0:T(8,128)S(1)}, f32[64,128]{1,0:T(8,128)}, u32[]{:S(2)}) copy-start(f32[64,128]{1,0:T(8,128)} %get-tuple-element.29._) | copy-start | bytes 98308
  9.8 3.5 %copy-start.1 = (f32[20,2048]{1,0:T(8,128)S(1)}, f32[20,2048]{1,0:T(8,128)}, u32[]{:S(2)}) copy-start(f32[20,2048]{1,0:T(8,128)} %c_ref.5) | copy-start | bytes 491524
  9.8 3.5 %copy-start.2 = (f32[4,2048]{1,0:T(4,128)S(1)}, f32[4,2048]{1,0:T(4,128)}, u32[]{:S(2)}) copy-start(f32[4,2048]{1,0:T(4,128)} %air.1) | copy-start | bytes 98308
  9.8 3.5 %copy-start.8 = (s32[256]{0:T(256)S(1)}, s32[256]{0:T(256)}, u32[]{:S(2)}) copy-start(s32[256]{0:T(256)} %patch_ref.3) | copy-start | bytes 3076
  17.6 18.0 %copy-start.6 = (f32[16,128]{1,0:T(8,128)S(1)}, f32[16,128]{1,0:T(8,128)}, u32[]{:S(2)}) copy-start(f32[16,128]{1,0:T(8,128)} %rate.1) | copy-start | bytes 24580
  17.6 18.0 %copy-start.7 = (s32[16,128]{1,0:T(8,128)S(1)}, s32[16,128]{1,0:T(8,128)}, u32[]{:S(2)}) copy-start(s32[16,128]{1,0:T(8,128)} %wet.1) | copy-start | bytes 24580
  17.6 2.0 %collective-permute-start.2 = (bf16[130,16,128]{2,1,0:T(8,128)(2,1)S(1)}, bf16[130,16,128]{2,1,0:T(8,128)(2,1)S(1)}, u32[]{:S(2)}, u32[]{:S(2)}) collective-permute-start(bf16[130,16,128]{2,1,0:T(8,128)(2,1)S(1)} %get-tuple-element.35), channel_id=1, source_target_pairs={{0,1},{1,0},{2,3},{3,2},{4,5},{5,4},{6,7},{7,6},{8,9},{9,8},{10,11... | collective-permute-start | bytes 1597448 | tf_op jit(solution)/shard_map/ppermute | solution.py:590
  19.8 6.1 %collective-permute-start.4 = (bf16[16,16,128]{2,1,0:T(8,128)(2,1)S(1)}, bf16[16,16,128]{2,1,0:T(8,128)(2,1)S(1)}, u32[]{:S(2)}, u32[]{:S(2)}) collective-permute-start(bf16[16,16,128]{2,1,0:T(8,128)(2,1)S(1)} %get-tuple-element.39), channel_id=1, source_target_pairs={{0,4},{2,6},{4,0},{6,2},{8,12},{10,14},{12,8},{14,10},{1,5},{3,7},... | collective-permute-start | bytes 196616 | tf_op jit(solution)/shard_map/ppermute | solution.py:592
  19.9 6.9 %collective-permute-start.6 = (bf16[16,16,128]{2,1,0:T(8,128)(2,1)S(1)}, bf16[16,16,128]{2,1,0:T(8,128)(2,1)S(1)}, u32[]{:S(2)}, u32[]{:S(2)}) collective-permute-start(bf16[16,16,128]{2,1,0:T(8,128)(2,1)S(1)} %get-tuple-element.41), channel_id=1, source_target_pairs={{0,8},{2,10},{4,12},{6,14},{8,0},{10,2},{12,4},{14,6},{1,9},{3,11}... | collective-permute-start | bytes 196616 | tf_op jit(solution)/shard_map/ppermute | solution.py:592
  20.9 14.8 %collective-permute-start.3 = (bf16[20,16,128]{2,1,0:T(8,128)(2,1)S(1)}, bf16[20,16,128]{2,1,0:T(8,128)(2,1)S(1)}, u32[]{:S(2)}, u32[]{:S(2)}) collective-permute-start(bf16[20,16,128]{2,1,0:T(8,128)(2,1)S(1)} %get-tuple-element.38), channel_id=1, source_target_pairs={{0,2},{2,0},{4,6},{6,4},{8,10},{10,8},{12,14},{14,12},{1,3},{3,1},... | collective-permute-start | bytes 245768 | tf_op jit(solution)/shard_map/ppermute | solution.py:592
  22.8 12.8 %collective-permute-start.5 = (bf16[20,16,128]{2,1,0:T(8,128)(2,1)S(1)}, bf16[20,16,128]{2,1,0:T(8,128)(2,1)S(1)}, u32[]{:S(2)}, u32[]{:S(2)}) collective-permute-start(bf16[20,16,128]{2,1,0:T(8,128)(2,1)S(1)} %get-tuple-element.40), channel_id=1, source_target_pairs={{0,6},{2,4},{4,2},{6,0},{8,14},{10,12},{12,10},{14,8},{1,7},{3,5},... | collective-permute-start | bytes 245768 | tf_op jit(solution)/shard_map/ppermute | solution.py:592
  23.4 12.3 %collective-permute-start.9 = (bf16[20,16,128]{2,1,0:T(8,128)(2,1)S(1)}, bf16[20,16,128]{2,1,0:T(8,128)(2,1)S(1)}, u32[]{:S(2)}, u32[]{:S(2)}) collective-permute-start(bf16[20,16,128]{2,1,0:T(8,128)(2,1)S(1)} %get-tuple-element.44), channel_id=1, source_target_pairs={{0,14},{2,12},{4,10},{6,8},{8,6},{10,4},{12,2},{14,0},{1,15},{3,13... | collective-permute-start | bytes 245768 | tf_op jit(solution)/shard_map/ppermute | solution.py:592
  25.9 9.7 %collective-permute-start.7 = (bf16[16,16,128]{2,1,0:T(8,128)(2,1)S(1)}, bf16[16,16,128]{2,1,0:T(8,128)(2,1)S(1)}, u32[]{:S(2)}, u32[]{:S(2)}) collective-permute-start(bf16[16,16,128]{2,1,0:T(8,128)(2,1)S(1)} %get-tuple-element.42), channel_id=1, source_target_pairs={{0,10},{2,8},{4,14},{6,12},{8,2},{10,0},{12,6},{14,4},{1,11},{3,9}... | collective-permute-start | bytes 196616 | tf_op jit(solution)/shard_map/ppermute | solution.py:592
  26.7 8.9 %collective-permute-start.8 = (bf16[16,16,128]{2,1,0:T(8,128)(2,1)S(1)}, bf16[16,16,128]{2,1,0:T(8,128)(2,1)S(1)}, u32[]{:S(2)}, u32[]{:S(2)}) collective-permute-start(bf16[16,16,128]{2,1,0:T(8,128)(2,1)S(1)} %get-tuple-element.43), channel_id=1, source_target_pairs={{0,12},{2,14},{4,8},{6,10},{8,4},{10,6},{12,0},{14,2},{1,13},{3,15... | collective-permute-start | bytes 196616 | tf_op jit(solution)/shard_map/ppermute | solution.py:592
  35.9 7.8 %collective-permute-start.12 = (bf16[16,16,128]{2,1,0:T(8,128)(2,1)S(1)}, bf16[16,16,128]{2,1,0:T(8,128)(2,1)S(1)}, u32[]{:S(2)}, u32[]{:S(2)}) collective-permute-start(bf16[16,16,128]{2,1,0:T(8,128)(2,1)S(1)} %get-tuple-element.46.rest_0_.refs_0_), channel_id=1, source_target_pairs={{0,12},{2,14},{4,8},{6,10},{8,4},{10,6},{12,0},{14,2},{1,13},{3,15... | collective-permute-start | bytes 196616 | tf_op jit(solution)/shard_map/ppermute | solution.py:592
  38.5 5.5 %collective-permute-start.11 = (bf16[16,16,128]{2,1,0:T(8,128)(2,1)S(1)}, bf16[16,16,128]{2,1,0:T(8,128)(2,1)S(1)}, u32[]{:S(2)}, u32[]{:S(2)}) collective-permute-start(bf16[16,16,128]{2,1,0:T(8,128)(2,1)S(1)} %get-tuple-element.46.rest_0_.refs_0_), channel_id=1, source_target_pairs={{0,8},{2,10},{4,12},{6,14},{8,0},{10,2},{12,4},{14,6},{1,9},{3,11}... | collective-permute-start | bytes 196616 | tf_op jit(solution)/shard_map/ppermute | solution.py:592
  38.8 5.2 %collective-permute-start.10 = (bf16[16,16,128]{2,1,0:T(8,128)(2,1)S(1)}, bf16[16,16,128]{2,1,0:T(8,128)(2,1)S(1)}, u32[]{:S(2)}, u32[]{:S(2)}) collective-permute-start(bf16[16,16,128]{2,1,0:T(8,128)(2,1)S(1)} %get-tuple-element.46.rest_0_.refs_0_), channel_id=1, source_target_pairs={{0,4},{2,6},{4,0},{6,2},{8,12},{10,14},{12,8},{14,10},{1,5},{3,7},... | collective-permute-start | bytes 196616 | tf_op jit(solution)/shard_map/ppermute | solution.py:592
  44.0 6.6 %collective-permute-start.13 = (bf16[64,16,128]{2,1,0:T(8,128)(2,1)S(1)}, bf16[64,16,128]{2,1,0:T(8,128)(2,1)S(1)}, u32[]{:S(2)}, u32[]{:S(2)}) collective-permute-start(bf16[64,16,128]{2,1,0:T(8,128)(2,1)S(1)} %gather_rows.2.rest_0_.even), channel_id=1, source_target_pairs={{0,2},{2,0},{4,6},{6,4},{8,10},{10,8},{12,14},{14,12},{1,3},{3,1},... | collective-permute-start | bytes 786440 | tf_op jit(solution)/shard_map/ppermute | solution.py:592
  45.4 6.1 %collective-permute-start.14 = (bf16[64,16,128]{2,1,0:T(8,128)(2,1)S(1)}, bf16[64,16,128]{2,1,0:T(8,128)(2,1)S(1)}, u32[]{:S(2)}, u32[]{:S(2)}) collective-permute-start(bf16[64,16,128]{2,1,0:T(8,128)(2,1)S(1)} %gather_rows.2.rest_0_.even), channel_id=1, source_target_pairs={{0,1},{1,0},{2,3},{3,2},{4,5},{5,4},{6,7},{7,6},{8,9},{9,8},{10,11... | collective-permute-start | bytes 786440 | tf_op jit(solution)/shard_map/ppermute | solution.py:606
  50.7 1.6 %collective-permute-start.15 = (bf16[64,16,128]{2,1,0:T(8,128)(2,1)S(1)}, bf16[64,16,128]{2,1,0:T(8,128)(2,1)S(1)}, u32[]{:S(2)}, u32[]{:S(2)}) collective-permute-start(bf16[64,16,128]{2,1,0:T(8,128)(2,1)S(1)} %gather_rows.3.odd), channel_id=1, source_target_pairs={{0,1},{1,0},{2,3},{3,2},{4,5},{5,4},{6,7},{7,6},{8,9},{9,8},{10,11... | collective-permute-start | bytes 786440 | tf_op jit(solution)/shard_map/ppermute | solution.py:609

commit v5 on v4

--- a/solution.py
+++ b/solution.py
@@ -13,7 +13,7 @@
 LANES = 128
 EDGE = 16
 GROUPS = LANES // EDGE
-UNROLL = 64
+UNROLL = 128
 GROUP = 4
 SETS = 2
 
@@ -32,6 +32,21 @@
 def place():
     sizes = lax.axis_size("tile"), lax.axis_size("sub")
     return lax.axis_index("tile"), lax.axis_index("sub"), *sizes
+
+
+def pass_kernel(x_ref, out_ref):
+    out_ref[...] = x_ref[...]
+
+
+def pass_on(x):
+    return pl.pallas_call(
+        pass_kernel,
+        out_shape=jax.ShapeDtypeStruct(x.shape, x.dtype),
+        in_specs=[VMEM],
+        out_specs=VMEM,
+        compiler_params=params(2 * 1024 * 1024),
+        name="pass_on",
+    )(x)
 
 
 def is_even():
@@ -129,7 +144,7 @@
     )(tracers_t, courant)
 
 
-def prepare_kernel(chunk, dest_ref, row_ref, weights_hbm, _, slot_ref, back_ref, weights, sem):
+def prepare_kernel(chunk, dest_ref, row_ref, weights_hbm, slot_ref, back_ref, weights, sem):
     copy = pltpu.make_async_copy(weights_hbm, weights, sem)
     copy.start()
     tile, sub, tiles, subs = place()
@@ -140,23 +155,25 @@
     core = (dest % subs + subs - sub) % subs * tiles
     row = row_ref[mine, :]
     slot_ref[...] = (core + apart) * chunk + row
-    back_ref[...] = (core + apart % 2 * (tiles // 2) + apart // 2) * chunk + row
+    far = tiles // 2
+    back = jnp.where(apart < far, apart, far + apart % 2 * (far // 2) + (apart - far) // 2)
+    back_ref[...] = (core + back) * chunk + row
     copy.wait()
 
 
-def prepare(dest, row, weights, after, chunk):
+def prepare(dest, row, weights, chunk):
     blocks = weights.shape[0]
     whole = (dest.size // LANES, LANES)
     return pl.pallas_call(
         functools.partial(prepare_kernel, chunk),
         out_shape=(jax.ShapeDtypeStruct((blocks // LANES, LANES), jnp.int32),) * 2
         + (jax.ShapeDtypeStruct(weights.shape, weights.dtype),),
-        in_specs=[VMEM, VMEM, HBM, ANY],
+        in_specs=[VMEM, VMEM, HBM],
         out_specs=(VMEM, VMEM, VMEM),
         scratch_shapes=[pltpu.SemaphoreType.DMA],
         compiler_params=params(44 * 1024 * 1024),
         name="prepare_blocks",
-    )(dest.reshape(whole), row.reshape(whole), weights, after)
+    )(dest.reshape(whole), row.reshape(whole), weights)
 
 
 def high_low(x):
@@ -335,17 +352,18 @@
 
 
 def gather_kernel(count, *refs):
-    out = refs[-1]
-    chunk = refs[0].shape[0]
-    for i in range(count):
-        out[i * chunk : (i + 1) * chunk] = refs[i][...]
+    out, start = refs[-1], 0
+    for ref in refs[:count]:
+        out[start : start + ref.shape[0]] = ref[...]
+        start += ref.shape[0]
 
 
 def gather_rows(parts, *after):
-    chunk, fields, lanes = parts[0].shape
+    fields, lanes = parts[0].shape[1:]
+    rows = sum(part.shape[0] for part in parts)
     return pl.pallas_call(
         functools.partial(gather_kernel, len(parts)),
-        out_shape=jax.ShapeDtypeStruct((chunk * len(parts), fields, lanes), bf16),
+        out_shape=jax.ShapeDtypeStruct((rows, fields, lanes), bf16),
         in_specs=[VMEM] * len(parts) + [ANY] * len(after),
         out_specs=VMEM,
         compiler_params=params(8 * 1024 * 1024),
@@ -485,16 +503,18 @@
 
 
 def backward_kernel(
-    slot_ref, patch_ref, even, odd, even_other, odd_other, weights, advected_hbm, air_hbm, out_hbm,
+    slot_ref, patch_ref, mine, odd, other, other_odd, weights, advected_hbm, air_hbm, out_hbm,
     rows, total, bottom, air, sem, air_sem,
 ):
     fetch = pltpu.make_async_copy(advected_hbm.at[:, pl.ds(0, 8), :], bottom, sem)
     fetch.start()
     tracers, _, span = bottom.shape
     blocks = weights.shape[0]
-    part, fields, _ = even.shape
-    for i, some in enumerate((even, odd, even_other, odd_other)):
-        rows[i * part : (i + 1) * part] = some[...]
+    fields = mine.shape[1]
+    start = 0
+    for some in (mine, odd, other, other_odd):
+        rows[start : start + some.shape[0]] = some[...]
+        start += some.shape[0]
     total[...] = jnp.zeros_like(total)
     slot_of = lambda b: slot_ref[b // LANES, b % LANES]
 
@@ -532,7 +552,7 @@
 
 def backward(slot, patch, parts, weights, advected):
     tracers, levels, span = advected.shape
-    part, fields, lanes = parts[0].shape
+    fields, lanes = parts[0].shape[1:]
     return pl.pallas_call(
         backward_kernel,
         out_shape=(
@@ -543,7 +563,7 @@
         out_specs=(HBM, HBM),
         input_output_aliases={7: 1},
         scratch_shapes=[
-            pltpu.VMEM((4 * part, fields, lanes), bf16),
+            pltpu.VMEM((sum(part.shape[0] for part in parts), fields, lanes), bf16),
             pltpu.VMEM((span // lanes, fields, lanes), f32),
             pltpu.VMEM((tracers, 8, span), f32),
             pltpu.VMEM((fields, span), f32),
@@ -573,13 +593,13 @@
     flat = ("tile", "sub")
     tracers_t = jnp.transpose(tracers, (1, 0, 2))
     pack_a, pack_b = pack(tracers_t, courant)
-    msg_b = lax.ppermute(
+    msg_b = pass_on(lax.ppermute(
         pack_b, flat, [(i, (i + 1 if i % 2 else i - 1) % devices) for i in range(devices)]
-    )
+    ))
     msg_a = lax.ppermute(pack_a, flat, [(i, i ^ 1) for i in range(devices)])
 
     slot, slot_back, weights = prepare(
-        block_dest, block_row, block_weights, pack_b, ocean_rows
+        block_dest, block_row, block_weights, ocean_rows
     )
     state = jnp.transpose(ocean_state, (1, 0, 2))
     send, keep = forward(
@@ -599,16 +619,19 @@
         state, beside, exchange_rate, sea_mask, own, got, flag
     )
 
-    arrived = [across(half, d) for d in range(tiles - 2, 0, -2)]
+    far = [d for d in range(tiles // 2, tiles) if d % 2 == 0]
+    near = list(range(1, tiles // 2))
+    arrived = {d: across(half, d) for d in far[::-1] + near[::-1]}
     some, flag = advance(count, count, half, some)
-    even = gather_rows([half] + arrived[::-1], flag)
+    even = gather_rows([arrived[d] for d in far], flag)
     odd = across(even, 1)
-    even_other = lax.ppermute(even, "sub", swap)
+    mine = gather_rows([half] + [arrived[d] for d in near] + [even])
+    other = lax.ppermute(mine, "sub", swap)
     advected, flag = advance(2 * count, tracers.shape[1] - 2 * count, even, some)
     odd = gather_rows([odd], flag)
-    odd_other = lax.ppermute(odd, "sub", swap)
+    other_odd = lax.ppermute(odd, "sub", swap)
     air_exchange, out_t = backward(
-        slot_back, block_patch, (even, odd, even_other, odd_other), weights, advected
+        slot_back, block_patch, (mine, odd, other, other_odd), weights, advected
     )
     return jnp.transpose(out_t, (1, 0, 2)), jnp.transpose(next_ocean, (1, 0, 2)), air_exchange
 

time: 57.1 us -> 56.4 us (0.988)
  starting transfers between devices: 22.3 us -> 24.3 us
  waiting for transfers between devices: 7.42 us -> 5.99 us
  local copies, waits for them, and re-layouts: 1.62 us -> 0.88 us
    ppermute x11 -> x13, starting transfers between devices: 15.9 us -> 18.1 us  [per_device(): lax.ppermute(x, 'tile', [(i, i ^ d) for i in range(tiles)])]
    ppermute x11 -> x13, waiting for transfers between devices: 4.68 us -> 3.8 us  [per_device(): lax.ppermute(x, 'tile', [(i, i ^ d) for i in range(tiles)])]
    unnamed x23 -> x21, local copies, waits for them, and re-layouts: 1.57 us -> 0.82 us
  transfers between devices with their start and end apart: 16 -> 18, of which waited for: 6 -> 4; matrix products, arithmetic and copies ran while one was open for 1% -> 1% of each run, Pallas kernels for 23% -> 24%
where the time goes in v5:
time: 56.4 us; the launch traced here: 56.3 us
  starting transfers between devices  24.3 us (43%)
  Pallas kernels  24.2 us (43%)
  waiting for transfers between devices  5.99 us (11%)
  between operations  0.93 us (2%)
  local copies, waits for them, and re-layouts  0.88 us (2%)
    ppermute x13, starting transfers between devices, per_device(): lax.ppermute(x, 'tile', [(i, i ^ d) for i in range(tiles)])  18.1 us
    pallas_call x3, Pallas kernels, advect_some(): pl.pallas_call(functools.partial(advect_kernel, tracers, levels, first, g...  9.91 us
    ppermute x1, starting transfers between devices, per_device(): lax.ppermute(pack_b, flat, [(i, (i + 1 if i % 2 else i - 1) % devices) fo...  5.51 us
    pallas_call x1, Pallas kernels, backward(): pl.pallas_call(backward_kernel, out_shape=(jax.ShapeDtypeStruct((fields,...  4.28 us
    pallas_call x1, Pallas kernels, forward(): pl.pallas_call(functools.partial(forward_kernel, (tracers, span, top)), o...  4.14 us
    ppermute x13, waiting for transfers between devices, per_device(): lax.ppermute(x, 'tile', [(i, i ^ d) for i in range(tiles)])  3.8 us
    pallas_call x1, Pallas kernels, prepare(): pl.pallas_call(functools.partial(prepare_kernel, chunk), out_shape=(jax.S...  3.44 us
    pallas_call x1, Pallas kernels, pack(): pl.pallas_call(functools.partial(pack_kernel, tracers, levels), out_shape...  1.98 us
  transfers between devices with their start and end apart: 18, of which 4 were waited for; matrix products, arithmetic and copies ran while one was open for 1% of the time, Pallas kernels for 24%

profile of v5, /device:TPU:0, one launch (start us, length us, event | category | flops | bytes accessed | tf_op | source)
XLA Modules:
  0.0 56.3 jit_solution(15276974880878485742)
XLA Ops:
  0.6 0.0 copy-start
  0.6 0.0 copy-start.8
  0.7 0.0 copy-start.4
  0.7 0.0 copy-start.3
  0.7 2.0 %pack_edges.1 = (f32[64,128]{1,0:T(8,128)}, f32[64,128]{1,0:T(8,128)}) custom-call(f32[12,20,2048]{2,1,0:T(8,128)} %bitcast.11, f32[20,2048]{1,0:T(8,128)} %c_ref.5), custom_call_target="tpu_custom_call" | custom-call | tf_op jit(solution)/shard_map/pack_edges/pallas_call | solution.py:130
  2.7 5.5 %collective-permute-start.1 = (f32[64,128]{1,0:T(8,128)}, f32[64,128]{1,0:T(8,128)S(1)}, u32[]{:S(2)}, u32[]{:S(2)}) collective-permute-start(f32[64,128]{1,0:T(8,128)} %get-tuple-element.32), channel_id=1, source_target_pairs={{0,15},{1,2},{2,1},{3,4},{4,3},{5,6},{6,5},{7,8},{8,7},{9,10},{10,... | collective-permute-start | bytes 98312 | tf_op jit(solution)/shard_map/ppermute | solution.py:596
  8.2 0.0 collective-permute-start
  8.2 0.0 copy-done
  8.2 0.1 slice.3
  8.3 0.0 copy-done.8
  8.3 0.0 copy-done.4
  8.3 0.0 copy-done.3
  8.4 0.0 copy-start.1
  8.4 0.0 copy-start.2
  8.4 0.0 copy-start.7
  8.4 3.4 %prepare_blocks.1 = (s32[2,128]{1,0:T(2,128)S(1)}, s32[2,128]{1,0:T(2,128)S(1)}, bf16[256,128,128]{2,1,0:T(8,128)(2,1)S(1)}) custom-call(s32[32,128]{1,0:T(8,128)S(1)} %bitcast.20, s32[32,128]{1,0:T(8,128)S(1)} %bitcast.21, bf16[256,128,128]{2,1,0:T(8,128)(2,1)} %weights_hbm.1), custom_call_target="tpu_custom_call" | custom-call | tf_op jit(solution)/shard_map/prepare_blocks/pallas_call | solution.py:167
  11.8 0.0 collective-permute-done.1.x_ref
  11.9 0.0 collective-permute-done.msg_a
  11.9 0.0 copy-done.1
  11.9 0.0 copy-done.2
  11.9 0.0 copy-done.7
  11.9 4.1 %blocks_to_rows.1 = (bf16[130,16,128]{2,1,0:T(8,128)(2,1)S(1)}, f32[128,16,128]{2,1,0:T(8,128)S(1)}) custom-call(s32[2,128]{1,0:T(2,128)S(1)} %get-tuple-element.30.slot_ref, s32[256]{0:T(256)S(1)} %copy-done.7, f32[12,2048]{1,0:T(8,128)S(1)} %bitcast.18, f32[20,2048]{1,0:T(8,128)S(1)} %copy-done.1, f32[4,2048]{1,0:T(4,128)S(1)} %copy-done.2, ...), custom_call_target="tpu_custom_call" | custom-call | tf_op jit(solution)/shard_map/blocks_to_rows/pallas_call | solution.py:233
  16.1 0.0 copy-start.5
  16.1 0.0 copy-start.6
  16.1 0.6 %collective-permute-start.2 = (bf16[130,16,128]{2,1,0:T(8,128)(2,1)S(1)}, bf16[130,16,128]{2,1,0:T(8,128)(2,1)S(1)}, u32[]{:S(2)}, u32[]{:S(2)}) collective-permute-start(bf16[130,16,128]{2,1,0:T(8,128)(2,1)S(1)} %get-tuple-element.35), channel_id=1, source_target_pairs={{0,1},{1,0},{2,3},{3,2},{4,5},{5,4},{6,7},{7,6},{8,9},{9,8},{10,11... | collective-permute-start | bytes 1597448 | tf_op jit(solution)/shard_map/ppermute | solution.py:610
  16.6 1.5 %collective-permute-done.2.got = bf16[130,16,128]{2,1,0:T(8,128)(2,1)S(1)} collective-permute-done((bf16[130,16,128]{2,1,0:T(8,128)(2,1)S(1)}, bf16[130,16,128]{2,1,0:T(8,128)(2,1)S(1)}, u32[]{:S(2)}, u32[]{:S(2)}) %collective-permute-start.2) | collective-permute-done | bytes 532512 | tf_op jit(solution)/shard_map/ppermute | solution.py:610
  18.2 0.2 merge_cores.1
  18.4 0.1 collective-permute-start.4
  18.5 1.7 %collective-permute-start.6 = (bf16[16,16,128]{2,1,0:T(8,128)(2,1)S(1)}, bf16[16,16,128]{2,1,0:T(8,128)(2,1)S(1)}, u32[]{:S(2)}, u32[]{:S(2)}) collective-permute-start(bf16[16,16,128]{2,1,0:T(8,128)(2,1)S(1)} %get-tuple-element.41), channel_id=1, source_target_pairs={{0,8},{2,10},{4,12},{6,14},{8,0},{10,2},{12,4},{14,6},{1,9},{3,11}... | collective-permute-start | bytes 196616 | tf_op jit(solution)/shard_map/ppermute | solution.py:612
  20.1 1.9 %collective-permute-start.3 = (bf16[20,16,128]{2,1,0:T(8,128)(2,1)S(1)}, bf16[20,16,128]{2,1,0:T(8,128)(2,1)S(1)}, u32[]{:S(2)}, u32[]{:S(2)}) collective-permute-start(bf16[20,16,128]{2,1,0:T(8,128)(2,1)S(1)} %get-tuple-element.38), channel_id=1, source_target_pairs={{0,2},{2,0},{4,6},{6,4},{8,10},{10,8},{12,14},{14,12},{1,3},{3,1},... | collective-permute-start | bytes 245768 | tf_op jit(solution)/shard_map/ppermute | solution.py:612
  22.0 0.0 collective-permute-start.5
  22.0 2.4 %collective-permute-start.9 = (bf16[20,16,128]{2,1,0:T(8,128)(2,1)S(1)}, bf16[20,16,128]{2,1,0:T(8,128)(2,1)S(1)}, u32[]{:S(2)}, u32[]{:S(2)}) collective-permute-start(bf16[20,16,128]{2,1,0:T(8,128)(2,1)S(1)} %get-tuple-element.44), channel_id=1, source_target_pairs={{0,14},{2,12},{4,10},{6,8},{8,6},{10,4},{12,2},{14,0},{1,15},{3,13... | collective-permute-start | bytes 245768 | tf_op jit(solution)/shard_map/ppermute | solution.py:612
  24.4 0.0 collective-permute-done.4.rest_1_
  24.4 1.6 %collective-permute-start.7 = (bf16[16,16,128]{2,1,0:T(8,128)(2,1)S(1)}, bf16[16,16,128]{2,1,0:T(8,128)(2,1)S(1)}, u32[]{:S(2)}, u32[]{:S(2)}) collective-permute-start(bf16[16,16,128]{2,1,0:T(8,128)(2,1)S(1)} %get-tuple-element.42), channel_id=1, source_target_pairs={{0,10},{2,8},{4,14},{6,12},{8,2},{10,0},{12,6},{14,4},{1,11},{3,9}... | collective-permute-start | bytes 196616 | tf_op jit(solution)/shard_map/ppermute | solution.py:612
  26.0 0.0 collective-permute-done.6.rest_3_
  26.0 2.7 %collective-permute-start.8 = (bf16[16,16,128]{2,1,0:T(8,128)(2,1)S(1)}, bf16[16,16,128]{2,1,0:T(8,128)(2,1)S(1)}, u32[]{:S(2)}, u32[]{:S(2)}) collective-permute-start(bf16[16,16,128]{2,1,0:T(8,128)(2,1)S(1)} %get-tuple-element.43), channel_id=1, source_target_pairs={{0,12},{2,14},{4,8},{6,10},{8,4},{10,6},{12,0},{14,2},{1,13},{3,15... | collective-permute-start | bytes 196616 | tf_op jit(solution)/shard_map/ppermute | solution.py:612
  28.7 3.3 %advect_levels.3 = (f32[12,20,2048]{2,1,0:T(8,128)}, f32[8,128]{1,0:T(8,128)S(1)}) custom-call(f32[12,20,2048]{2,1,0:T(8,128)S(1)} %bitcast.12, f32[20,2048]{1,0:T(8,128)S(1)} %copy-done.1, f32[64,128]{1,0:T(8,128)S(1)} %collective-permute-done.msg_a, f32[64,128]{1,0:T(8,128)S(1)} %pass_on.1.msg_b, f32[16,16,128]{2,1,0:T(8,128)S(1)} %get-tuple-element.37.rest_0_.own), custom_call_target="tpu_custom_call" | custom-call | flops 32768000 | bytes 1310720 | tf_op jit(solution)/shard_map/advect_levels/pallas_call | solution.py:475
  32.0 2.3 %collective-permute-done.7.rest_4_ = bf16[16,16,128]{2,1,0:T(8,128)(2,1)S(1)} collective-permute-done((bf16[16,16,128]{2,1,0:T(8,128)(2,1)S(1)}, bf16[16,16,128]{2,1,0:T(8,128)(2,1)S(1)}, u32[]{:S(2)}, u32[]{:S(2)}) %collective-permute-start.7) | collective-permute-done | bytes 65568 | tf_op jit(solution)/shard_map/ppermute | solution.py:612
  34.3 0.0 collective-permute-done.8.rest_5_
  34.3 0.0 collective-permute-done.3.rest_0_
  34.3 0.0 collective-permute-done.5.rest_2_
  34.3 0.0 collective-permute-done.9.rest_6_
  34.3 0.0 copy-done.5
  34.4 0.2 ocean_update.1
  34.6 2.6 %collective-permute-start.14 = (bf16[16,16,128]{2,1,0:T(8,128)(2,1)S(1)}, bf16[16,16,128]{2,1,0:T(8,128)(2,1)S(1)}, u32[]{:S(2)}, u32[]{:S(2)}) collective-permute-start(bf16[16,16,128]{2,1,0:T(8,128)(2,1)S(1)} %get-tuple-element.46.rest_0_.refs_0_), channel_id=1, source_target_pairs={{0,12},{2,14},{4,8},{6,10},{8,4},{10,6},{12,0},{14,2},{1,13},{3,15... | collective-permute-start | bytes 196616 | tf_op jit(solution)/shard_map/ppermute | solution.py:612
  37.2 0.5 collective-permute-start.13
  37.7 2.6 %collective-permute-start.12 = (bf16[16,16,128]{2,1,0:T(8,128)(2,1)S(1)}, bf16[16,16,128]{2,1,0:T(8,128)(2,1)S(1)}, u32[]{:S(2)}, u32[]{:S(2)}) collective-permute-start(bf16[16,16,128]{2,1,0:T(8,128)(2,1)S(1)} %get-tuple-element.46.rest_0_.refs_0_), channel_id=1, source_target_pairs={{0,6},{2,4},{4,2},{6,0},{8,14},{10,12},{12,10},{14,8},{1,7},{3,5},... | collective-permute-start | bytes 196616 | tf_op jit(solution)/shard_map/ppermute | solution.py:612
  40.3 0.0 collective-permute-start.11
  40.3 0.9 %collective-permute-start.10 = (bf16[16,16,128]{2,1,0:T(8,128)(2,1)S(1)}, bf16[16,16,128]{2,1,0:T(8,128)(2,1)S(1)}, u32[]{:S(2)}, u32[]{:S(2)}) collective-permute-start(bf16[16,16,128]{2,1,0:T(8,128)(2,1)S(1)} %get-tuple-element.46.rest_0_.refs_0_), channel_id=1, source_target_pairs={{0,2},{2,0},{4,6},{6,4},{8,10},{10,8},{12,14},{14,12},{1,3},{3,1},... | collective-permute-start | bytes 196616 | tf_op jit(solution)/shard_map/ppermute | solution.py:612
  41.2 3.3 %advect_levels.4 = (f32[12,20,2048]{2,1,0:T(8,128)}, f32[8,128]{1,0:T(8,128)S(1)}) custom-call(f32[12,20,2048]{2,1,0:T(8,128)S(1)} %bitcast.13, f32[20,2048]{1,0:T(8,128)S(1)} %copy-done.1, f32[64,128]{1,0:T(8,128)S(1)} %collective-permute-done.msg_a, f32[64,128]{1,0:T(8,128)S(1)} %pass_on.1.msg_b, ...), custom_call_target="tpu_custom_call", output_to_operand_aliasing={{0}: (5, {})} | custom-call | flops 32768000 | bytes 1310720 | tf_op jit(solution)/shard_map/advect_levels/pallas_call | solution.py:475
  44.5 0.0 collective-permute-done.14.refs_1_
  44.5 0.0 collective-permute-done.13.refs_0_
  44.5 0.0 collective-permute-done.12.refs_3_
  44.5 0.0 collective-permute-done.11.refs_2_
  44.6 0.0 collective-permute-done.10.refs_1_
  44.6 0.1 collective-permute-start.16
  44.7 1.2 %collective-permute-start.15 = (bf16[32,16,128]{2,1,0:T(8,128)(2,1)S(1)}, bf16[32,16,128]{2,1,0:T(8,128)(2,1)S(1)}, u32[]{:S(2)}, u32[]{:S(2)}) collective-permute-start(bf16[32,16,128]{2,1,0:T(8,128)(2,1)S(1)} %gather_rows.3.refs_4_.rest_0_), channel_id=1, source_target_pairs={{0,2},{2,0},{4,6},{6,4},{8,10},{10,8},{12,14},{14,12},{1,3},{3,1},... | collective-permute-start | bytes 393224 | tf_op jit(solution)/shard_map/ppermute | solution.py:612
  45.9 3.3 %advect_levels.5 = (f32[12,20,2048]{2,1,0:T(8,128)}, f32[8,128]{1,0:T(8,128)S(1)}) custom-call(f32[12,20,2048]{2,1,0:T(8,128)S(1)} %bitcast.14, f32[20,2048]{1,0:T(8,128)S(1)} %copy-done.1, f32[64,128]{1,0:T(8,128)S(1)} %collective-permute-done.msg_a, f32[64,128]{1,0:T(8,128)S(1)} %pass_on.1.msg_b, ...), custom_call_target="tpu_custom_call", output_to_operand_aliasing={{0}: (5, {})} | custom-call | flops 32768000 | bytes 1310720 | tf_op jit(solution)/shard_map/advect_levels/pallas_call | solution.py:475
  49.1 1.4 %collective-permute-done.15.refs_0_ = bf16[32,16,128]{2,1,0:T(8,128)(2,1)S(1)} collective-permute-done((bf16[32,16,128]{2,1,0:T(8,128)(2,1)S(1)}, bf16[32,16,128]{2,1,0:T(8,128)(2,1)S(1)}, u32[]{:S(2)}, u32[]{:S(2)}) %collective-permute-start.15) | collective-permute-done | bytes 131104 | tf_op jit(solution)/shard_map/ppermute | solution.py:612
  50.6 0.1 collective-permute-start.17
  50.7 0.7 %copy.18 = f32[16,16,128]{2,1,0:T(8,128)} copy(f32[16,16,128]{2,0,1:T(8,128)S(1)} %bitcast.19) | data formatting | bytes 262144
  51.4 0.6 %collective-permute-done.17.other_odd = bf16[32,16,128]{2,1,0:T(8,128)(2,1)S(1)} collective-permute-done((bf16[32,16,128]{2,1,0:T(8,128)(2,1)S(1)}, bf16[32,16,128]{2,1,0:T(8,128)(2,1)S(1)}, u32[]{:S(2)}, u32[]{:S(2)}) %collective-permute-start.17) | collective-permute-done | bytes 131104 | tf_op jit(solution)/shard_map/ppermute | solution.py:632
  52.0 0.0 collective-permute-done.16.other
  52.0 4.3 %rows_to_columns.1 = (f32[16,2048]{1,0:T(8,128)}, f32[12,20,2048]{2,1,0:T(8,128)}) custom-call(s32[2,128]{1,0:T(2,128)S(1)} %get-tuple-element.29.slot_ref, s32[256]{0:T(256)S(1)} %copy-done.7, bf16[96,16,128]{2,1,0:T(8,128)(2,1)S(1)} %gather_rows.4.mine, bf16[32,16,128]{2,1,0:T(8,128)(2,1)S(1)} %gather_rows.5.odd, ...), custom_call_target="tpu_custom_call", output_to_operand_aliasing={{1}: (7, {})} | custom-call | tf_op jit(solution)/shard_map/rows_to_columns/pallas_call | solution.py:556
  (7 shorter events, 0.1 us)
Async XLA Ops:
  0.6 7.5 %copy-start = (f32[20,12,2048]{2,0,1:T(8,128)S(1)}, f32[20,12,2048]{2,0,1:T(8,128)}, u32[]{:S(2)}) copy-start(f32[20,12,2048]{2,0,1:T(8,128)} %param.10) | copy-start | bytes 5898244
  0.6 7.6 %copy-start.8 = (f32[16,16,128]{2,1,0:T(8,128)S(1)}, f32[16,16,128]{2,1,0:T(8,128)}, u32[]{:S(2)}) copy-start(f32[16,16,128]{2,1,0:T(8,128)} %param.17) | copy-start | bytes 393220
  0.7 7.7 %copy-start.4 = (s32[4096]{0:T(1024)S(1)}, s32[4096]{0:T(1024)}, u32[]{:S(2)}) copy-start(s32[4096]{0:T(1024)} %param.15) | copy-start | bytes 49156
  0.7 7.7 %copy-start.3 = (s32[4096,1]{0,1:T(1,128)S(1)}, s32[4096,1]{0,1:T(1,128)}, u32[]{:S(2)}) copy-start(s32[4096,1]{0,1:T(1,128)} %param.14) | copy-start | bytes 49156
  2.7 9.2 %collective-permute-start.1 = (f32[64,128]{1,0:T(8,128)}, f32[64,128]{1,0:T(8,128)S(1)}, u32[]{:S(2)}, u32[]{:S(2)}) collective-permute-start(f32[64,128]{1,0:T(8,128)} %get-tuple-element.32), channel_id=1, source_target_pairs={{0,15},{1,2},{2,1},{3,4},{4,3},{5,6},{6,5},{7,8},{8,7},{9,10},{10,... | collective-permute-start | bytes 98312 | tf_op jit(solution)/shard_map/ppermute | solution.py:596
  8.2 3.7 %collective-permute-start = (f32[64,128]{1,0:T(8,128)}, f32[64,128]{1,0:T(8,128)S(1)}, u32[]{:S(2)}, u32[]{:S(2)}) collective-permute-start(f32[64,128]{1,0:T(8,128)} %get-tuple-element.31), channel_id=1, source_target_pairs={{0,1},{1,0},{2,3},{3,2},{4,5},{5,4},{6,7},{7,6},{8,9},{9,8},{10,11... | collective-permute-start | bytes 98312 | tf_op jit(solution)/shard_map/ppermute | solution.py:599
  8.4 3.5 %copy-start.1 = (f32[20,2048]{1,0:T(8,128)S(1)}, f32[20,2048]{1,0:T(8,128)}, u32[]{:S(2)}) copy-start(f32[20,2048]{1,0:T(8,128)} %c_ref.5) | copy-start | bytes 491524
  8.4 3.5 %copy-start.2 = (f32[4,2048]{1,0:T(4,128)S(1)}, f32[4,2048]{1,0:T(4,128)}, u32[]{:S(2)}) copy-start(f32[4,2048]{1,0:T(4,128)} %air.1) | copy-start | bytes 98308
  8.4 3.5 %copy-start.7 = (s32[256]{0:T(256)S(1)}, s32[256]{0:T(256)}, u32[]{:S(2)}) copy-start(s32[256]{0:T(256)} %patch_ref.3) | copy-start | bytes 3076
  16.1 18.3 %copy-start.5 = (f32[16,128]{1,0:T(8,128)S(1)}, f32[16,128]{1,0:T(8,128)}, u32[]{:S(2)}) copy-start(f32[16,128]{1,0:T(8,128)} %rate.1) | copy-start | bytes 24580
  16.1 18.3 %copy-start.6 = (s32[16,128]{1,0:T(8,128)S(1)}, s32[16,128]{1,0:T(8,128)}, u32[]{:S(2)}) copy-start(s32[16,128]{1,0:T(8,128)} %wet.1) | copy-start | bytes 24580
  16.1 2.1 %collective-permute-start.2 = (bf16[130,16,128]{2,1,0:T(8,128)(2,1)S(1)}, bf16[130,16,128]{2,1,0:T(8,128)(2,1)S(1)}, u32[]{:S(2)}, u32[]{:S(2)}) collective-permute-start(bf16[130,16,128]{2,1,0:T(8,128)(2,1)S(1)} %get-tuple-element.35), channel_id=1, source_target_pairs={{0,1},{1,0},{2,3},{3,2},{4,5},{5,4},{6,7},{7,6},{8,9},{9,8},{10,11... | collective-permute-start | bytes 1597448 | tf_op jit(solution)/shard_map/ppermute | solution.py:610
  18.4 6.0 %collective-permute-start.4 = (bf16[16,16,128]{2,1,0:T(8,128)(2,1)S(1)}, bf16[16,16,128]{2,1,0:T(8,128)(2,1)S(1)}, u32[]{:S(2)}, u32[]{:S(2)}) collective-permute-start(bf16[16,16,128]{2,1,0:T(8,128)(2,1)S(1)} %get-tuple-element.39), channel_id=1, source_target_pairs={{0,4},{2,6},{4,0},{6,2},{8,12},{10,14},{12,8},{14,10},{1,5},{3,7},... | collective-permute-start | bytes 196616 | tf_op jit(solution)/shard_map/ppermute | solution.py:612
  18.5 7.5 %collective-permute-start.6 = (bf16[16,16,128]{2,1,0:T(8,128)(2,1)S(1)}, bf16[16,16,128]{2,1,0:T(8,128)(2,1)S(1)}, u32[]{:S(2)}, u32[]{:S(2)}) collective-permute-start(bf16[16,16,128]{2,1,0:T(8,128)(2,1)S(1)} %get-tuple-element.41), channel_id=1, source_target_pairs={{0,8},{2,10},{4,12},{6,14},{8,0},{10,2},{12,4},{14,6},{1,9},{3,11}... | collective-permute-start | bytes 196616 | tf_op jit(solution)/shard_map/ppermute | solution.py:612
  20.1 14.2 %collective-permute-start.3 = (bf16[20,16,128]{2,1,0:T(8,128)(2,1)S(1)}, bf16[20,16,128]{2,1,0:T(8,128)(2,1)S(1)}, u32[]{:S(2)}, u32[]{:S(2)}) collective-permute-start(bf16[20,16,128]{2,1,0:T(8,128)(2,1)S(1)} %get-tuple-element.38), channel_id=1, source_target_pairs={{0,2},{2,0},{4,6},{6,4},{8,10},{10,8},{12,14},{14,12},{1,3},{3,1},... | collective-permute-start | bytes 245768 | tf_op jit(solution)/shard_map/ppermute | solution.py:612
  22.0 12.3 %collective-permute-start.5 = (bf16[20,16,128]{2,1,0:T(8,128)(2,1)S(1)}, bf16[20,16,128]{2,1,0:T(8,128)(2,1)S(1)}, u32[]{:S(2)}, u32[]{:S(2)}) collective-permute-start(bf16[20,16,128]{2,1,0:T(8,128)(2,1)S(1)} %get-tuple-element.40), channel_id=1, source_target_pairs={{0,6},{2,4},{4,2},{6,0},{8,14},{10,12},{12,10},{14,8},{1,7},{3,5},... | collective-permute-start | bytes 245768 | tf_op jit(solution)/shard_map/ppermute | solution.py:612
  22.0 12.3 %collective-permute-start.9 = (bf16[20,16,128]{2,1,0:T(8,128)(2,1)S(1)}, bf16[20,16,128]{2,1,0:T(8,128)(2,1)S(1)}, u32[]{:S(2)}, u32[]{:S(2)}) collective-permute-start(bf16[20,16,128]{2,1,0:T(8,128)(2,1)S(1)} %get-tuple-element.44), channel_id=1, source_target_pairs={{0,14},{2,12},{4,10},{6,8},{8,6},{10,4},{12,2},{14,0},{1,15},{3,13... | collective-permute-start | bytes 245768 | tf_op jit(solution)/shard_map/ppermute | solution.py:612
  24.4 9.9 %collective-permute-start.7 = (bf16[16,16,128]{2,1,0:T(8,128)(2,1)S(1)}, bf16[16,16,128]{2,1,0:T(8,128)(2,1)S(1)}, u32[]{:S(2)}, u32[]{:S(2)}) collective-permute-start(bf16[16,16,128]{2,1,0:T(8,128)(2,1)S(1)} %get-tuple-element.42), channel_id=1, source_target_pairs={{0,10},{2,8},{4,14},{6,12},{8,2},{10,0},{12,6},{14,4},{1,11},{3,9}... | collective-permute-start | bytes 196616 | tf_op jit(solution)/shard_map/ppermute | solution.py:612
  26.0 8.4 %collective-permute-start.8 = (bf16[16,16,128]{2,1,0:T(8,128)(2,1)S(1)}, bf16[16,16,128]{2,1,0:T(8,128)(2,1)S(1)}, u32[]{:S(2)}, u32[]{:S(2)}) collective-permute-start(bf16[16,16,128]{2,1,0:T(8,128)(2,1)S(1)} %get-tuple-element.43), channel_id=1, source_target_pairs={{0,12},{2,14},{4,8},{6,10},{8,4},{10,6},{12,0},{14,2},{1,13},{3,15... | collective-permute-start | bytes 196616 | tf_op jit(solution)/shard_map/ppermute | solution.py:612
  34.6 9.9 %collective-permute-start.14 = (bf16[16,16,128]{2,1,0:T(8,128)(2,1)S(1)}, bf16[16,16,128]{2,1,0:T(8,128)(2,1)S(1)}, u32[]{:S(2)}, u32[]{:S(2)}) collective-permute-start(bf16[16,16,128]{2,1,0:T(8,128)(2,1)S(1)} %get-tuple-element.46.rest_0_.refs_0_), channel_id=1, source_target_pairs={{0,12},{2,14},{4,8},{6,10},{8,4},{10,6},{12,0},{14,2},{1,13},{3,15... | collective-permute-start | bytes 196616 | tf_op jit(solution)/shard_map/ppermute | solution.py:612
  37.2 7.3 %collective-permute-start.13 = (bf16[16,16,128]{2,1,0:T(8,128)(2,1)S(1)}, bf16[16,16,128]{2,1,0:T(8,128)(2,1)S(1)}, u32[]{:S(2)}, u32[]{:S(2)}) collective-permute-start(bf16[16,16,128]{2,1,0:T(8,128)(2,1)S(1)} %get-tuple-element.46.rest_0_.refs_0_), channel_id=1, source_target_pairs={{0,8},{2,10},{4,12},{6,14},{8,0},{10,2},{12,4},{14,6},{1,9},{3,11}... | collective-permute-start | bytes 196616 | tf_op jit(solution)/shard_map/ppermute | solution.py:612
  37.7 6.8 %collective-permute-start.12 = (bf16[16,16,128]{2,1,0:T(8,128)(2,1)S(1)}, bf16[16,16,128]{2,1,0:T(8,128)(2,1)S(1)}, u32[]{:S(2)}, u32[]{:S(2)}) collective-permute-start(bf16[16,16,128]{2,1,0:T(8,128)(2,1)S(1)} %get-tuple-element.46.rest_0_.refs_0_), channel_id=1, source_target_pairs={{0,6},{2,4},{4,2},{6,0},{8,14},{10,12},{12,10},{14,8},{1,7},{3,5},... | collective-permute-start | bytes 196616 | tf_op jit(solution)/shard_map/ppermute | solution.py:612
  40.3 4.3 %collective-permute-start.11 = (bf16[16,16,128]{2,1,0:T(8,128)(2,1)S(1)}, bf16[16,16,128]{2,1,0:T(8,128)(2,1)S(1)}, u32[]{:S(2)}, u32[]{:S(2)}) collective-permute-start(bf16[16,16,128]{2,1,0:T(8,128)(2,1)S(1)} %get-tuple-element.46.rest_0_.refs_0_), channel_id=1, source_target_pairs={{0,4},{2,6},{4,0},{6,2},{8,12},{10,14},{12,8},{14,10},{1,5},{3,7},... | collective-permute-start | bytes 196616 | tf_op jit(solution)/shard_map/ppermute | solution.py:612
  40.3 4.3 %collective-permute-start.10 = (bf16[16,16,128]{2,1,0:T(8,128)(2,1)S(1)}, bf16[16,16,128]{2,1,0:T(8,128)(2,1)S(1)}, u32[]{:S(2)}, u32[]{:S(2)}) collective-permute-start(bf16[16,16,128]{2,1,0:T(8,128)(2,1)S(1)} %get-tuple-element.46.rest_0_.refs_0_), channel_id=1, source_target_pairs={{0,2},{2,0},{4,6},{6,4},{8,10},{10,8},{12,14},{14,12},{1,3},{3,1},... | collective-permute-start | bytes 196616 | tf_op jit(solution)/shard_map/ppermute | solution.py:612
  44.6 7.4 %collective-permute-start.16 = (bf16[96,16,128]{2,1,0:T(8,128)(2,1)S(1)}, bf16[96,16,128]{2,1,0:T(8,128)(2,1)S(1)}, u32[]{:S(2)}, u32[]{:S(2)}) collective-permute-start(bf16[96,16,128]{2,1,0:T(8,128)(2,1)S(1)} %gather_rows.4.mine), channel_id=1, source_target_pairs={{0,1},{1,0},{2,3},{3,2},{4,5},{5,4},{6,7},{7,6},{8,9},{9,8},{10,11... | collective-permute-start | bytes 1179656 | tf_op jit(solution)/shard_map/ppermute | solution.py:629
  44.7 5.9 %collective-permute-start.15 = (bf16[32,16,128]{2,1,0:T(8,128)(2,1)S(1)}, bf16[32,16,128]{2,1,0:T(8,128)(2,1)S(1)}, u32[]{:S(2)}, u32[]{:S(2)}) collective-permute-start(bf16[32,16,128]{2,1,0:T(8,128)(2,1)S(1)} %gather_rows.3.refs_4_.rest_0_), channel_id=1, source_target_pairs={{0,2},{2,0},{4,6},{6,4},{8,10},{10,8},{12,14},{14,12},{1,3},{3,1},... | collective-permute-start | bytes 393224 | tf_op jit(solution)/shard_map/ppermute | solution.py:612
  50.6 1.4 %collective-permute-start.17 = (bf16[32,16,128]{2,1,0:T(8,128)(2,1)S(1)}, bf16[32,16,128]{2,1,0:T(8,128)(2,1)S(1)}, u32[]{:S(2)}, u32[]{:S(2)}) collective-permute-start(bf16[32,16,128]{2,1,0:T(8,128)(2,1)S(1)} %gather_rows.5.odd), channel_id=1, source_target_pairs={{0,1},{1,0},{2,3},{3,2},{4,5},{5,4},{6,7},{7,6},{8,9},{9,8},{10,11... | collective-permute-start | bytes 393224 | tf_op jit(solution)/shard_map/ppermute | solution.py:632

commit v6 on v5

--- a/solution.py
+++ b/solution.py
@@ -13,6 +13,7 @@
 LANES = 128
 EDGE = 16
 GROUPS = LANES // EDGE
+FORWARD_UNROLL = 256
 UNROLL = 128
 GROUP = 4
 SETS = 2
@@ -201,9 +202,9 @@
     height = zero.shape[0]
 
     def step(g, carry):
-        base = g * UNROLL
+        base = g * FORWARD_UNROLL
         products = []
-        for u in range(0, UNROLL, 2):
+        for u in range(0, FORWARD_UNROLL, 2):
             first, second = surface[patch_ref[base + u]], surface[patch_ref[base + u + 1]]
             rows = jnp.concatenate(
                 [jnp.concatenate([first, zero], 1), jnp.concatenate([zero, second], 1)], 0
@@ -211,11 +212,11 @@
             pair = weights[pl.ds(base + u, 2)].reshape(2 * LANES, LANES)
             both = jnp.dot(rows, pair, preferred_element_type=f32)
             products += [both[:height], both[height:]]
-        for u in range(UNROLL):
+        for u in range(FORWARD_UNROLL):
             total[slot_ref[(base + u) // LANES, (base + u) % LANES]] += products[u]
         return carry
 
-    lax.fori_loop(0, blocks // UNROLL, step, 0)
+    lax.fori_loop(0, blocks // FORWARD_UNROLL, step, 0)
     half = total.shape[0] // 2
     keep_ref[...] = total[:half]
     send_ref[:half] = total[half:].astype(bf16)
@@ -506,7 +507,7 @@
     slot_ref, patch_ref, mine, odd, other, other_odd, weights, advected_hbm, air_hbm, out_hbm,
     rows, total, bottom, air, sem, air_sem,
 ):
-    fetch = pltpu.make_async_copy(advected_hbm.at[:, pl.ds(0, 8), :], bottom, sem)
+    fetch = pltpu.make_async_copy(advected_hbm.at[:, pl.ds(0, 1), :], bottom, sem)
     fetch.start()
     tracers, _, span = bottom.shape
     blocks = weights.shape[0]
@@ -541,7 +542,7 @@
         air[:, part] = exchange
         bottom[:, 0, part] += COUPLE * exchange[:tracers]
     stores = (
-        pltpu.make_async_copy(bottom, out_hbm.at[:, pl.ds(0, 8), :], sem),
+        pltpu.make_async_copy(bottom, out_hbm.at[:, pl.ds(0, 1), :], sem),
         pltpu.make_async_copy(air, air_hbm, air_sem),
     )
     for store in stores:
@@ -565,7 +566,7 @@
         scratch_shapes=[
             pltpu.VMEM((sum(part.shape[0] for part in parts), fields, lanes), bf16),
             pltpu.VMEM((span // lanes, fields, lanes), f32),
-            pltpu.VMEM((tracers, 8, span), f32),
+            pltpu.VMEM((tracers, 1, span), f32),
             pltpu.VMEM((fields, span), f32),
             pltpu.SemaphoreType.DMA,
             pltpu.SemaphoreType.DMA,

time: 56.4 us -> 55.3 us (0.980)
  Pallas kernels: 24.2 us -> 23.1 us
    pallas_call x1, Pallas kernels: 4.14 us -> 3.21 us  [forward(): pl.pallas_call(functools.partial(forward_kernel, (tracers, span, top)), o...]
where the time goes in v6:
time: 55.3 us; the launch traced here: 55.2 us
  starting transfers between devices  24.3 us (44%)
  Pallas kernels  23.1 us (42%)
  waiting for transfers between devices  5.96 us (11%)
  between operations  0.93 us (2%)
  local copies, waits for them, and re-layouts  0.88 us (2%)
    ppermute x13, starting transfers between devices, per_device(): lax.ppermute(x, 'tile', [(i, i ^ d) for i in range(tiles)])  18.1 us
    pallas_call x3, Pallas kernels, advect_some(): pl.pallas_call(functools.partial(advect_kernel, tracers, levels, first, g...  9.91 us
    ppermute x1, starting transfers between devices, per_device(): lax.ppermute(pack_b, flat, [(i, (i + 1 if i % 2 else i - 1) % devices) fo...  5.51 us
    pallas_call x1, Pallas kernels, backward(): pl.pallas_call(backward_kernel, out_shape=(jax.ShapeDtypeStruct((fields,...  4.07 us
    ppermute x13, waiting for transfers between devices, per_device(): lax.ppermute(x, 'tile', [(i, i ^ d) for i in range(tiles)])  3.76 us
    pallas_call x1, Pallas kernels, prepare(): pl.pallas_call(functools.partial(prepare_kernel, chunk), out_shape=(jax.S...  3.44 us
    pallas_call x1, Pallas kernels, forward(): pl.pallas_call(functools.partial(forward_kernel, (tracers, span, top)), o...  3.21 us
    pallas_call x1, Pallas kernels, pack(): pl.pallas_call(functools.partial(pack_kernel, tracers, levels), out_shape...  1.98 us
  transfers between devices with their start and end apart: 18, of which 4 were waited for; matrix products, arithmetic and copies ran while one was open for 1% of the time, Pallas kernels for 24%

profile of v6, /device:TPU:0, one launch (start us, length us, event | category | flops | bytes accessed | tf_op | source)
XLA Modules:
  0.0 55.2 jit_solution(13643200085524572039)
XLA Ops:
  0.6 0.0 copy-start
  0.6 0.0 copy-start.8
  0.7 0.0 copy-start.4
  0.7 0.0 copy-start.3
  0.7 2.0 %pack_edges.1 = (f32[64,128]{1,0:T(8,128)}, f32[64,128]{1,0:T(8,128)}) custom-call(f32[12,20,2048]{2,1,0:T(8,128)} %bitcast.11, f32[20,2048]{1,0:T(8,128)} %c_ref.5), custom_call_target="tpu_custom_call" | custom-call | tf_op jit(solution)/shard_map/pack_edges/pallas_call | solution.py:131
  2.7 5.5 %collective-permute-start.1 = (f32[64,128]{1,0:T(8,128)}, f32[64,128]{1,0:T(8,128)S(1)}, u32[]{:S(2)}, u32[]{:S(2)}) collective-permute-start(f32[64,128]{1,0:T(8,128)} %get-tuple-element.32), channel_id=1, source_target_pairs={{0,15},{1,2},{2,1},{3,4},{4,3},{5,6},{6,5},{7,8},{8,7},{9,10},{10,... | collective-permute-start | bytes 98312 | tf_op jit(solution)/shard_map/ppermute | solution.py:597
  8.2 0.0 collective-permute-start
  8.2 0.0 copy-done
  8.2 0.1 slice.3
  8.3 0.0 copy-done.8
  8.3 0.0 copy-done.4
  8.3 0.0 copy-done.3
  8.4 0.0 copy-start.1
  8.4 0.0 copy-start.2
  8.4 0.0 copy-start.7
  8.4 3.4 %prepare_blocks.1 = (s32[2,128]{1,0:T(2,128)S(1)}, s32[2,128]{1,0:T(2,128)S(1)}, bf16[256,128,128]{2,1,0:T(8,128)(2,1)S(1)}) custom-call(s32[32,128]{1,0:T(8,128)S(1)} %bitcast.20, s32[32,128]{1,0:T(8,128)S(1)} %bitcast.21, bf16[256,128,128]{2,1,0:T(8,128)(2,1)} %weights_hbm.1), custom_call_target="tpu_custom_call" | custom-call | tf_op jit(solution)/shard_map/prepare_blocks/pallas_call | solution.py:168
  11.8 0.0 collective-permute-done.1.x_ref
  11.9 0.0 collective-permute-done.msg_a
  11.9 0.0 copy-done.1
  11.9 0.0 copy-done.2
  11.9 0.0 copy-done.7
  11.9 3.2 %blocks_to_rows.1 = (bf16[130,16,128]{2,1,0:T(8,128)(2,1)S(1)}, f32[128,16,128]{2,1,0:T(8,128)S(1)}) custom-call(s32[2,128]{1,0:T(2,128)S(1)} %get-tuple-element.30.slot_ref, s32[256]{0:T(256)S(1)} %copy-done.7, f32[12,2048]{1,0:T(8,128)S(1)} %bitcast.18, f32[20,2048]{1,0:T(8,128)S(1)} %copy-done.1, f32[4,2048]{1,0:T(4,128)S(1)} %copy-done.2, ...), custom_call_target="tpu_custom_call" | custom-call | tf_op jit(solution)/shard_map/blocks_to_rows/pallas_call | solution.py:234
  15.1 0.0 copy-start.5
  15.1 0.0 copy-start.6
  15.1 0.6 %collective-permute-start.2 = (bf16[130,16,128]{2,1,0:T(8,128)(2,1)S(1)}, bf16[130,16,128]{2,1,0:T(8,128)(2,1)S(1)}, u32[]{:S(2)}, u32[]{:S(2)}) collective-permute-start(bf16[130,16,128]{2,1,0:T(8,128)(2,1)S(1)} %get-tuple-element.35), channel_id=1, source_target_pairs={{0,1},{1,0},{2,3},{3,2},{4,5},{5,4},{6,7},{7,6},{8,9},{9,8},{10,11... | collective-permute-start | bytes 1597448 | tf_op jit(solution)/shard_map/ppermute | solution.py:611
  15.7 1.5 %collective-permute-done.2.got = bf16[130,16,128]{2,1,0:T(8,128)(2,1)S(1)} collective-permute-done((bf16[130,16,128]{2,1,0:T(8,128)(2,1)S(1)}, bf16[130,16,128]{2,1,0:T(8,128)(2,1)S(1)}, u32[]{:S(2)}, u32[]{:S(2)}) %collective-permute-start.2) | collective-permute-done | bytes 532512 | tf_op jit(solution)/shard_map/ppermute | solution.py:611
  17.3 0.2 merge_cores.1
  17.5 0.1 collective-permute-start.4
  17.5 1.7 %collective-permute-start.6 = (bf16[16,16,128]{2,1,0:T(8,128)(2,1)S(1)}, bf16[16,16,128]{2,1,0:T(8,128)(2,1)S(1)}, u32[]{:S(2)}, u32[]{:S(2)}) collective-permute-start(bf16[16,16,128]{2,1,0:T(8,128)(2,1)S(1)} %get-tuple-element.41), channel_id=1, source_target_pairs={{0,8},{2,10},{4,12},{6,14},{8,0},{10,2},{12,4},{14,6},{1,9},{3,11}... | collective-permute-start | bytes 196616 | tf_op jit(solution)/shard_map/ppermute | solution.py:613
  19.2 1.9 %collective-permute-start.3 = (bf16[20,16,128]{2,1,0:T(8,128)(2,1)S(1)}, bf16[20,16,128]{2,1,0:T(8,128)(2,1)S(1)}, u32[]{:S(2)}, u32[]{:S(2)}) collective-permute-start(bf16[20,16,128]{2,1,0:T(8,128)(2,1)S(1)} %get-tuple-element.38), channel_id=1, source_target_pairs={{0,2},{2,0},{4,6},{6,4},{8,10},{10,8},{12,14},{14,12},{1,3},{3,1},... | collective-permute-start | bytes 245768 | tf_op jit(solution)/shard_map/ppermute | solution.py:613
  21.1 0.0 collective-permute-start.5
  21.1 2.4 %collective-permute-start.9 = (bf16[20,16,128]{2,1,0:T(8,128)(2,1)S(1)}, bf16[20,16,128]{2,1,0:T(8,128)(2,1)S(1)}, u32[]{:S(2)}, u32[]{:S(2)}) collective-permute-start(bf16[20,16,128]{2,1,0:T(8,128)(2,1)S(1)} %get-tuple-element.44), channel_id=1, source_target_pairs={{0,14},{2,12},{4,10},{6,8},{8,6},{10,4},{12,2},{14,0},{1,15},{3,13... | collective-permute-start | bytes 245768 | tf_op jit(solution)/shard_map/ppermute | solution.py:613
  23.4 0.0 collective-permute-done.4.rest_1_
  23.5 1.6 %collective-permute-start.7 = (bf16[16,16,128]{2,1,0:T(8,128)(2,1)S(1)}, bf16[16,16,128]{2,1,0:T(8,128)(2,1)S(1)}, u32[]{:S(2)}, u32[]{:S(2)}) collective-permute-start(bf16[16,16,128]{2,1,0:T(8,128)(2,1)S(1)} %get-tuple-element.42), channel_id=1, source_target_pairs={{0,10},{2,8},{4,14},{6,12},{8,2},{10,0},{12,6},{14,4},{1,11},{3,9}... | collective-permute-start | bytes 196616 | tf_op jit(solution)/shard_map/ppermute | solution.py:613
  25.0 0.0 collective-permute-done.6.rest_3_
  25.0 2.7 %collective-permute-start.8 = (bf16[16,16,128]{2,1,0:T(8,128)(2,1)S(1)}, bf16[16,16,128]{2,1,0:T(8,128)(2,1)S(1)}, u32[]{:S(2)}, u32[]{:S(2)}) collective-permute-start(bf16[16,16,128]{2,1,0:T(8,128)(2,1)S(1)} %get-tuple-element.43), channel_id=1, source_target_pairs={{0,12},{2,14},{4,8},{6,10},{8,4},{10,6},{12,0},{14,2},{1,13},{3,15... | collective-permute-start | bytes 196616 | tf_op jit(solution)/shard_map/ppermute | solution.py:613
  27.8 3.3 %advect_levels.3 = (f32[12,20,2048]{2,1,0:T(8,128)}, f32[8,128]{1,0:T(8,128)S(1)}) custom-call(f32[12,20,2048]{2,1,0:T(8,128)S(1)} %bitcast.12, f32[20,2048]{1,0:T(8,128)S(1)} %copy-done.1, f32[64,128]{1,0:T(8,128)S(1)} %collective-permute-done.msg_a, f32[64,128]{1,0:T(8,128)S(1)} %pass_on.1.msg_b, f32[16,16,128]{2,1,0:T(8,128)S(1)} %get-tuple-element.37.rest_0_.own), custom_call_target="tpu_custom_call" | custom-call | flops 32768000 | bytes 1310720 | tf_op jit(solution)/shard_map/advect_levels/pallas_call | solution.py:476
  31.1 2.3 %collective-permute-done.7.rest_4_ = bf16[16,16,128]{2,1,0:T(8,128)(2,1)S(1)} collective-permute-done((bf16[16,16,128]{2,1,0:T(8,128)(2,1)S(1)}, bf16[16,16,128]{2,1,0:T(8,128)(2,1)S(1)}, u32[]{:S(2)}, u32[]{:S(2)}) %collective-permute-start.7) | collective-permute-done | bytes 65568 | tf_op jit(solution)/shard_map/ppermute | solution.py:613
  33.4 0.0 collective-permute-done.8.rest_5_
  33.4 0.0 collective-permute-done.3.rest_0_
  33.4 0.0 collective-permute-done.5.rest_2_
  33.4 0.0 collective-permute-done.9.rest_6_
  33.4 0.0 copy-done.5
  33.4 0.2 ocean_update.1
  33.6 2.7 %collective-permute-start.14 = (bf16[16,16,128]{2,1,0:T(8,128)(2,1)S(1)}, bf16[16,16,128]{2,1,0:T(8,128)(2,1)S(1)}, u32[]{:S(2)}, u32[]{:S(2)}) collective-permute-start(bf16[16,16,128]{2,1,0:T(8,128)(2,1)S(1)} %get-tuple-element.46.rest_0_.refs_0_), channel_id=1, source_target_pairs={{0,12},{2,14},{4,8},{6,10},{8,4},{10,6},{12,0},{14,2},{1,13},{3,15... | collective-permute-start | bytes 196616 | tf_op jit(solution)/shard_map/ppermute | solution.py:613
  36.3 0.4 collective-permute-start.13
  36.8 2.6 %collective-permute-start.12 = (bf16[16,16,128]{2,1,0:T(8,128)(2,1)S(1)}, bf16[16,16,128]{2,1,0:T(8,128)(2,1)S(1)}, u32[]{:S(2)}, u32[]{:S(2)}) collective-permute-start(bf16[16,16,128]{2,1,0:T(8,128)(2,1)S(1)} %get-tuple-element.46.rest_0_.refs_0_), channel_id=1, source_target_pairs={{0,6},{2,4},{4,2},{6,0},{8,14},{10,12},{12,10},{14,8},{1,7},{3,5},... | collective-permute-start | bytes 196616 | tf_op jit(solution)/shard_map/ppermute | solution.py:613
  39.3 0.0 collective-permute-start.11
  39.3 0.9 %collective-permute-start.10 = (bf16[16,16,128]{2,1,0:T(8,128)(2,1)S(1)}, bf16[16,16,128]{2,1,0:T(8,128)(2,1)S(1)}, u32[]{:S(2)}, u32[]{:S(2)}) collective-permute-start(bf16[16,16,128]{2,1,0:T(8,128)(2,1)S(1)} %get-tuple-element.46.rest_0_.refs_0_), channel_id=1, source_target_pairs={{0,2},{2,0},{4,6},{6,4},{8,10},{10,8},{12,14},{14,12},{1,3},{3,1},... | collective-permute-start | bytes 196616 | tf_op jit(solution)/shard_map/ppermute | solution.py:613
  40.3 3.3 %advect_levels.4 = (f32[12,20,2048]{2,1,0:T(8,128)}, f32[8,128]{1,0:T(8,128)S(1)}) custom-call(f32[12,20,2048]{2,1,0:T(8,128)S(1)} %bitcast.13, f32[20,2048]{1,0:T(8,128)S(1)} %copy-done.1, f32[64,128]{1,0:T(8,128)S(1)} %collective-permute-done.msg_a, f32[64,128]{1,0:T(8,128)S(1)} %pass_on.1.msg_b, ...), custom_call_target="tpu_custom_call", output_to_operand_aliasing={{0}: (5, {})} | custom-call | flops 32768000 | bytes 1310720 | tf_op jit(solution)/shard_map/advect_levels/pallas_call | solution.py:476
  43.6 0.0 collective-permute-done.14.refs_1_
  43.6 0.0 collective-permute-done.13.refs_0_
  43.6 0.0 collective-permute-done.12.refs_3_
  43.6 0.0 collective-permute-done.11.refs_2_
  43.6 0.0 collective-permute-done.10.refs_1_
  43.7 0.1 collective-permute-start.16
  43.7 1.2 %collective-permute-start.15 = (bf16[32,16,128]{2,1,0:T(8,128)(2,1)S(1)}, bf16[32,16,128]{2,1,0:T(8,128)(2,1)S(1)}, u32[]{:S(2)}, u32[]{:S(2)}) collective-permute-start(bf16[32,16,128]{2,1,0:T(8,128)(2,1)S(1)} %gather_rows.3.refs_4_.rest_0_), channel_id=1, source_target_pairs={{0,2},{2,0},{4,6},{6,4},{8,10},{10,8},{12,14},{14,12},{1,3},{3,1},... | collective-permute-start | bytes 393224 | tf_op jit(solution)/shard_map/ppermute | solution.py:613
  44.9 3.3 %advect_levels.5 = (f32[12,20,2048]{2,1,0:T(8,128)}, f32[8,128]{1,0:T(8,128)S(1)}) custom-call(f32[12,20,2048]{2,1,0:T(8,128)S(1)} %bitcast.14, f32[20,2048]{1,0:T(8,128)S(1)} %copy-done.1, f32[64,128]{1,0:T(8,128)S(1)} %collective-permute-done.msg_a, f32[64,128]{1,0:T(8,128)S(1)} %pass_on.1.msg_b, ...), custom_call_target="tpu_custom_call", output_to_operand_aliasing={{0}: (5, {})} | custom-call | flops 32768000 | bytes 1310720 | tf_op jit(solution)/shard_map/advect_levels/pallas_call | solution.py:476
  48.2 1.4 %collective-permute-done.15.refs_0_ = bf16[32,16,128]{2,1,0:T(8,128)(2,1)S(1)} collective-permute-done((bf16[32,16,128]{2,1,0:T(8,128)(2,1)S(1)}, bf16[32,16,128]{2,1,0:T(8,128)(2,1)S(1)}, u32[]{:S(2)}, u32[]{:S(2)}) %collective-permute-start.15) | collective-permute-done | bytes 131104 | tf_op jit(solution)/shard_map/ppermute | solution.py:613
  49.7 0.1 collective-permute-start.17
  49.7 0.7 %copy.18 = f32[16,16,128]{2,1,0:T(8,128)} copy(f32[16,16,128]{2,0,1:T(8,128)S(1)} %bitcast.19) | data formatting | bytes 262144
  50.4 0.6 %collective-permute-done.17.other_odd = bf16[32,16,128]{2,1,0:T(8,128)(2,1)S(1)} collective-permute-done((bf16[32,16,128]{2,1,0:T(8,128)(2,1)S(1)}, bf16[32,16,128]{2,1,0:T(8,128)(2,1)S(1)}, u32[]{:S(2)}, u32[]{:S(2)}) %collective-permute-start.17) | collective-permute-done | bytes 131104 | tf_op jit(solution)/shard_map/ppermute | solution.py:633
  51.1 0.0 collective-permute-done.16.other
  51.1 4.1 %rows_to_columns.1 = (f32[16,2048]{1,0:T(8,128)}, f32[12,20,2048]{2,1,0:T(8,128)}) custom-call(s32[2,128]{1,0:T(2,128)S(1)} %get-tuple-element.29.slot_ref, s32[256]{0:T(256)S(1)} %copy-done.7, bf16[96,16,128]{2,1,0:T(8,128)(2,1)S(1)} %gather_rows.4.mine, bf16[32,16,128]{2,1,0:T(8,128)(2,1)S(1)} %gather_rows.5.odd, ...), custom_call_target="tpu_custom_call", output_to_operand_aliasing={{1}: (7, {})} | custom-call | tf_op jit(solution)/shard_map/rows_to_columns/pallas_call | solution.py:557
  (7 shorter events, 0.1 us)
Async XLA Ops:
  0.6 7.5 %copy-start = (f32[20,12,2048]{2,0,1:T(8,128)S(1)}, f32[20,12,2048]{2,0,1:T(8,128)}, u32[]{:S(2)}) copy-start(f32[20,12,2048]{2,0,1:T(8,128)} %param.10) | copy-start | bytes 5898244
  0.6 7.6 %copy-start.8 = (f32[16,16,128]{2,1,0:T(8,128)S(1)}, f32[16,16,128]{2,1,0:T(8,128)}, u32[]{:S(2)}) copy-start(f32[16,16,128]{2,1,0:T(8,128)} %param.17) | copy-start | bytes 393220
  0.7 7.7 %copy-start.4 = (s32[4096]{0:T(1024)S(1)}, s32[4096]{0:T(1024)}, u32[]{:S(2)}) copy-start(s32[4096]{0:T(1024)} %param.15) | copy-start | bytes 49156
  0.7 7.7 %copy-start.3 = (s32[4096,1]{0,1:T(1,128)S(1)}, s32[4096,1]{0,1:T(1,128)}, u32[]{:S(2)}) copy-start(s32[4096,1]{0,1:T(1,128)} %param.14) | copy-start | bytes 49156
  2.7 9.2 %collective-permute-start.1 = (f32[64,128]{1,0:T(8,128)}, f32[64,128]{1,0:T(8,128)S(1)}, u32[]{:S(2)}, u32[]{:S(2)}) collective-permute-start(f32[64,128]{1,0:T(8,128)} %get-tuple-element.32), channel_id=1, source_target_pairs={{0,15},{1,2},{2,1},{3,4},{4,3},{5,6},{6,5},{7,8},{8,7},{9,10},{10,... | collective-permute-start | bytes 98312 | tf_op jit(solution)/shard_map/ppermute | solution.py:597
  8.2 3.7 %collective-permute-start = (f32[64,128]{1,0:T(8,128)}, f32[64,128]{1,0:T(8,128)S(1)}, u32[]{:S(2)}, u32[]{:S(2)}) collective-permute-start(f32[64,128]{1,0:T(8,128)} %get-tuple-element.31), channel_id=1, source_target_pairs={{0,1},{1,0},{2,3},{3,2},{4,5},{5,4},{6,7},{7,6},{8,9},{9,8},{10,11... | collective-permute-start | bytes 98312 | tf_op jit(solution)/shard_map/ppermute | solution.py:600
  8.4 3.5 %copy-start.1 = (f32[20,2048]{1,0:T(8,128)S(1)}, f32[20,2048]{1,0:T(8,128)}, u32[]{:S(2)}) copy-start(f32[20,2048]{1,0:T(8,128)} %c_ref.5) | copy-start | bytes 491524
  8.4 3.5 %copy-start.2 = (f32[4,2048]{1,0:T(4,128)S(1)}, f32[4,2048]{1,0:T(4,128)}, u32[]{:S(2)}) copy-start(f32[4,2048]{1,0:T(4,128)} %air.1) | copy-start | bytes 98308
  8.4 3.5 %copy-start.7 = (s32[256]{0:T(256)S(1)}, s32[256]{0:T(256)}, u32[]{:S(2)}) copy-start(s32[256]{0:T(256)} %patch_ref.3) | copy-start | bytes 3076
  15.1 18.3 %copy-start.5 = (f32[16,128]{1,0:T(8,128)S(1)}, f32[16,128]{1,0:T(8,128)}, u32[]{:S(2)}) copy-start(f32[16,128]{1,0:T(8,128)} %rate.1) | copy-start | bytes 24580
  15.1 18.3 %copy-start.6 = (s32[16,128]{1,0:T(8,128)S(1)}, s32[16,128]{1,0:T(8,128)}, u32[]{:S(2)}) copy-start(s32[16,128]{1,0:T(8,128)} %wet.1) | copy-start | bytes 24580
  15.1 2.1 %collective-permute-start.2 = (bf16[130,16,128]{2,1,0:T(8,128)(2,1)S(1)}, bf16[130,16,128]{2,1,0:T(8,128)(2,1)S(1)}, u32[]{:S(2)}, u32[]{:S(2)}) collective-permute-start(bf16[130,16,128]{2,1,0:T(8,128)(2,1)S(1)} %get-tuple-element.35), channel_id=1, source_target_pairs={{0,1},{1,0},{2,3},{3,2},{4,5},{5,4},{6,7},{7,6},{8,9},{9,8},{10,11... | collective-permute-start | bytes 1597448 | tf_op jit(solution)/shard_map/ppermute | solution.py:611
  17.5 6.0 %collective-permute-start.4 = (bf16[16,16,128]{2,1,0:T(8,128)(2,1)S(1)}, bf16[16,16,128]{2,1,0:T(8,128)(2,1)S(1)}, u32[]{:S(2)}, u32[]{:S(2)}) collective-permute-start(bf16[16,16,128]{2,1,0:T(8,128)(2,1)S(1)} %get-tuple-element.39), channel_id=1, source_target_pairs={{0,4},{2,6},{4,0},{6,2},{8,12},{10,14},{12,8},{14,10},{1,5},{3,7},... | collective-permute-start | bytes 196616 | tf_op jit(solution)/shard_map/ppermute | solution.py:613
  17.5 7.5 %collective-permute-start.6 = (bf16[16,16,128]{2,1,0:T(8,128)(2,1)S(1)}, bf16[16,16,128]{2,1,0:T(8,128)(2,1)S(1)}, u32[]{:S(2)}, u32[]{:S(2)}) collective-permute-start(bf16[16,16,128]{2,1,0:T(8,128)(2,1)S(1)} %get-tuple-element.41), channel_id=1, source_target_pairs={{0,8},{2,10},{4,12},{6,14},{8,0},{10,2},{12,4},{14,6},{1,9},{3,11}... | collective-permute-start | bytes 196616 | tf_op jit(solution)/shard_map/ppermute | solution.py:613
  19.2 14.2 %collective-permute-start.3 = (bf16[20,16,128]{2,1,0:T(8,128)(2,1)S(1)}, bf16[20,16,128]{2,1,0:T(8,128)(2,1)S(1)}, u32[]{:S(2)}, u32[]{:S(2)}) collective-permute-start(bf16[20,16,128]{2,1,0:T(8,128)(2,1)S(1)} %get-tuple-element.38), channel_id=1, source_target_pairs={{0,2},{2,0},{4,6},{6,4},{8,10},{10,8},{12,14},{14,12},{1,3},{3,1},... | collective-permute-start | bytes 245768 | tf_op jit(solution)/shard_map/ppermute | solution.py:613
  21.1 12.3 %collective-permute-start.5 = (bf16[20,16,128]{2,1,0:T(8,128)(2,1)S(1)}, bf16[20,16,128]{2,1,0:T(8,128)(2,1)S(1)}, u32[]{:S(2)}, u32[]{:S(2)}) collective-permute-start(bf16[20,16,128]{2,1,0:T(8,128)(2,1)S(1)} %get-tuple-element.40), channel_id=1, source_target_pairs={{0,6},{2,4},{4,2},{6,0},{8,14},{10,12},{12,10},{14,8},{1,7},{3,5},... | collective-permute-start | bytes 245768 | tf_op jit(solution)/shard_map/ppermute | solution.py:613
  21.1 12.3 %collective-permute-start.9 = (bf16[20,16,128]{2,1,0:T(8,128)(2,1)S(1)}, bf16[20,16,128]{2,1,0:T(8,128)(2,1)S(1)}, u32[]{:S(2)}, u32[]{:S(2)}) collective-permute-start(bf16[20,16,128]{2,1,0:T(8,128)(2,1)S(1)} %get-tuple-element.44), channel_id=1, source_target_pairs={{0,14},{2,12},{4,10},{6,8},{8,6},{10,4},{12,2},{14,0},{1,15},{3,13... | collective-permute-start | bytes 245768 | tf_op jit(solution)/shard_map/ppermute | solution.py:613
  23.5 9.9 %collective-permute-start.7 = (bf16[16,16,128]{2,1,0:T(8,128)(2,1)S(1)}, bf16[16,16,128]{2,1,0:T(8,128)(2,1)S(1)}, u32[]{:S(2)}, u32[]{:S(2)}) collective-permute-start(bf16[16,16,128]{2,1,0:T(8,128)(2,1)S(1)} %get-tuple-element.42), channel_id=1, source_target_pairs={{0,10},{2,8},{4,14},{6,12},{8,2},{10,0},{12,6},{14,4},{1,11},{3,9}... | collective-permute-start | bytes 196616 | tf_op jit(solution)/shard_map/ppermute | solution.py:613
  25.0 8.3 %collective-permute-start.8 = (bf16[16,16,128]{2,1,0:T(8,128)(2,1)S(1)}, bf16[16,16,128]{2,1,0:T(8,128)(2,1)S(1)}, u32[]{:S(2)}, u32[]{:S(2)}) collective-permute-start(bf16[16,16,128]{2,1,0:T(8,128)(2,1)S(1)} %get-tuple-element.43), channel_id=1, source_target_pairs={{0,12},{2,14},{4,8},{6,10},{8,4},{10,6},{12,0},{14,2},{1,13},{3,15... | collective-permute-start | bytes 196616 | tf_op jit(solution)/shard_map/ppermute | solution.py:613
  33.6 9.9 %collective-permute-start.14 = (bf16[16,16,128]{2,1,0:T(8,128)(2,1)S(1)}, bf16[16,16,128]{2,1,0:T(8,128)(2,1)S(1)}, u32[]{:S(2)}, u32[]{:S(2)}) collective-permute-start(bf16[16,16,128]{2,1,0:T(8,128)(2,1)S(1)} %get-tuple-element.46.rest_0_.refs_0_), channel_id=1, source_target_pairs={{0,12},{2,14},{4,8},{6,10},{8,4},{10,6},{12,0},{14,2},{1,13},{3,15... | collective-permute-start | bytes 196616 | tf_op jit(solution)/shard_map/ppermute | solution.py:613
  36.3 7.2 %collective-permute-start.13 = (bf16[16,16,128]{2,1,0:T(8,128)(2,1)S(1)}, bf16[16,16,128]{2,1,0:T(8,128)(2,1)S(1)}, u32[]{:S(2)}, u32[]{:S(2)}) collective-permute-start(bf16[16,16,128]{2,1,0:T(8,128)(2,1)S(1)} %get-tuple-element.46.rest_0_.refs_0_), channel_id=1, source_target_pairs={{0,8},{2,10},{4,12},{6,14},{8,0},{10,2},{12,4},{14,6},{1,9},{3,11}... | collective-permute-start | bytes 196616 | tf_op jit(solution)/shard_map/ppermute | solution.py:613
  36.8 6.8 %collective-permute-start.12 = (bf16[16,16,128]{2,1,0:T(8,128)(2,1)S(1)}, bf16[16,16,128]{2,1,0:T(8,128)(2,1)S(1)}, u32[]{:S(2)}, u32[]{:S(2)}) collective-permute-start(bf16[16,16,128]{2,1,0:T(8,128)(2,1)S(1)} %get-tuple-element.46.rest_0_.refs_0_), channel_id=1, source_target_pairs={{0,6},{2,4},{4,2},{6,0},{8,14},{10,12},{12,10},{14,8},{1,7},{3,5},... | collective-permute-start | bytes 196616 | tf_op jit(solution)/shard_map/ppermute | solution.py:613
  39.3 4.3 %collective-permute-start.11 = (bf16[16,16,128]{2,1,0:T(8,128)(2,1)S(1)}, bf16[16,16,128]{2,1,0:T(8,128)(2,1)S(1)}, u32[]{:S(2)}, u32[]{:S(2)}) collective-permute-start(bf16[16,16,128]{2,1,0:T(8,128)(2,1)S(1)} %get-tuple-element.46.rest_0_.refs_0_), channel_id=1, source_target_pairs={{0,4},{2,6},{4,0},{6,2},{8,12},{10,14},{12,8},{14,10},{1,5},{3,7},... | collective-permute-start | bytes 196616 | tf_op jit(solution)/shard_map/ppermute | solution.py:613
  39.3 4.3 %collective-permute-start.10 = (bf16[16,16,128]{2,1,0:T(8,128)(2,1)S(1)}, bf16[16,16,128]{2,1,0:T(8,128)(2,1)S(1)}, u32[]{:S(2)}, u32[]{:S(2)}) collective-permute-start(bf16[16,16,128]{2,1,0:T(8,128)(2,1)S(1)} %get-tuple-element.46.rest_0_.refs_0_), channel_id=1, source_target_pairs={{0,2},{2,0},{4,6},{6,4},{8,10},{10,8},{12,14},{14,12},{1,3},{3,1},... | collective-permute-start | bytes 196616 | tf_op jit(solution)/shard_map/ppermute | solution.py:613
  43.7 7.4 %collective-permute-start.16 = (bf16[96,16,128]{2,1,0:T(8,128)(2,1)S(1)}, bf16[96,16,128]{2,1,0:T(8,128)(2,1)S(1)}, u32[]{:S(2)}, u32[]{:S(2)}) collective-permute-start(bf16[96,16,128]{2,1,0:T(8,128)(2,1)S(1)} %gather_rows.4.mine), channel_id=1, source_target_pairs={{0,1},{1,0},{2,3},{3,2},{4,5},{5,4},{6,7},{7,6},{8,9},{9,8},{10,11... | collective-permute-start | bytes 1179656 | tf_op jit(solution)/shard_map/ppermute | solution.py:630
  43.7 5.9 %collective-permute-start.15 = (bf16[32,16,128]{2,1,0:T(8,128)(2,1)S(1)}, bf16[32,16,128]{2,1,0:T(8,128)(2,1)S(1)}, u32[]{:S(2)}, u32[]{:S(2)}) collective-permute-start(bf16[32,16,128]{2,1,0:T(8,128)(2,1)S(1)} %gather_rows.3.refs_4_.rest_0_), channel_id=1, source_target_pairs={{0,2},{2,0},{4,6},{6,4},{8,10},{10,8},{12,14},{14,12},{1,3},{3,1},... | collective-permute-start | bytes 393224 | tf_op jit(solution)/shard_map/ppermute | solution.py:613
  49.7 1.4 %collective-permute-start.17 = (bf16[32,16,128]{2,1,0:T(8,128)(2,1)S(1)}, bf16[32,16,128]{2,1,0:T(8,128)(2,1)S(1)}, u32[]{:S(2)}, u32[]{:S(2)}) collective-permute-start(bf16[32,16,128]{2,1,0:T(8,128)(2,1)S(1)} %gather_rows.5.odd), channel_id=1, source_target_pairs={{0,1},{1,0},{2,3},{3,2},{4,5},{5,4},{6,7},{7,6},{8,9},{9,8},{10,11... | collective-permute-start | bytes 393224 | tf_op jit(solution)/shard_map/ppermute | solution.py:633
